TPU v7x, 128 devices: a whole 4x4x4 slice. The times are simulated.
128 devices in a mesh: tiles: 128 (over y, x, z, core).
Axes of the slice: x: 4, y: 4, z: 4, core: 2. Of those that a mesh axis runs over, the one named last changes fastest.
Arguments:
- tiles_in: float32 [1024, 250, 256], P('tiles'), may hold values from -6 to 6
- conv_weight: float32 [250, 49], replicated, may hold values from -0.875 to 0.875
- conv_bias: float32 [250], replicated, may hold values from -4 to 4
- norm_gain: float32 [250], replicated, may hold values from 0.5 to 1.5
- norm_bias: float32 [250], replicated, may hold values from -3 to 3
- weight_in: float32 [250, 1000], replicated, may hold values from -0.375 to 0.375
- bias_in: float32 [1000], replicated, may hold values from -3 to 3
- weight_out: float32 [1000, 250], replicated, may hold values from -0.1875 to 0.1875
- bias_out: float32 [250], replicated, may hold values from -3 to 3
- grad_out: float32 [1024, 250, 256], P('tiles'), may hold values from -6 to 6
- tile_counts: int32 [128], P('tiles'), may hold values from 4 to 8, as said below
- ocean_mask: int32 [1024, 256], P('tiles'), may hold values 0 or 1
- neighbours: int32 [1024, 8], P('tiles'), may hold values from -1 to 1023, as said below
- sample_ids: int32 [1024], P('tiles'), may hold values from 0 to 4, as said below
Outputs:
- output: float32 [1024, 250, 256], P('tiles')
- grad_tiles_in: float32 [1024, 250, 256], P('tiles')
- grad_conv_weight: float32 [250, 49], replicated
- grad_conv_bias: float32 [250], replicated
- grad_norm_gain: float32 [250], replicated
- grad_norm_bias: float32 [250], replicated
- grad_weight_in: float32 [250, 1000], replicated
- grad_bias_in: float32 [1000], replicated
- grad_weight_out: float32 [1000, 250], replicated
- grad_bias_out: float32 [250], replicated
Inputs may be any that keep to these rules, and one draw needn't show every extreme that they name: `tile_counts`: one device holds 8 filled slots and another (4); filled slots come first on each device. `neighbours`: each entry is -1 or a filled slot on a device whose index differs from the tile's device by at most 2; slots that are not filled have only -1. `sample_ids`: never falling along the slots; each sample holds more than 8 slots.
All inputs are finite; a program needn't handle non-finite values. No bound on the sum of `ocean_mask` on one device may be relied on, other than what follows from the above.
Results may differ from a plain program's by a relative error of at most 0.0003.
Values sent between devices are 32-bit elements; how exact they have to be, the bound alone decides.
A program may use at most 384 MiB of HBM per device.

v0:
```python
from functools import partial

import jax
import jax.numpy as jnp
from jax import lax
from jax.sharding import PartitionSpec as P

SIDE = 16
KSIZE = 7
REACH = 2
SAMPLES = 5


NORM_EPSILON = 1e-05
HIGHEST_PRECISION = lax.Precision.HIGHEST


def passed_along(block, axis, distance):
    devices = range(lax.axis_size(axis))
    route = [(i - distance, i) for i in devices if i - distance in devices]
    return lax.ppermute(block, axis, route)


def assemble(own_tiles, near_tiles):
    tile_total = own_tiles.shape[0]
    channels = own_tiles.shape[1]
    rim_width = KSIZE // 2

    def as_square(values):
        return values.reshape(tile_total, channels, SIDE, SIDE)

    sides = [as_square(near_tiles[:, direction]) for direction in range(8)]
    upper_rows = jnp.concatenate(
        [
            sides[0][:, :, SIDE - rim_width :, SIDE - rim_width :],
            sides[1][:, :, SIDE - rim_width :, :],
            sides[2][:, :, SIDE - rim_width :, :rim_width],
        ],
        axis=3,
    )
    middle_rows = jnp.concatenate(
        [
            sides[3][:, :, :, SIDE - rim_width :],
            as_square(own_tiles),
            sides[4][:, :, :, :rim_width],
        ],
        axis=3,
    )
    lower_rows = jnp.concatenate(
        [
            sides[5][:, :, :rim_width, SIDE - rim_width :],
            sides[6][:, :, :rim_width, :],
            sides[7][:, :, :rim_width, :rim_width],
        ],
        axis=3,
    )
    return jnp.concatenate([upper_rows, middle_rows, lower_rows], axis=2)


def depthwise(own_tiles, near_tiles, conv_weight, conv_bias):
    tile_total = own_tiles.shape[0]
    channels = own_tiles.shape[1]
    padded_side = SIDE + 2 * (KSIZE // 2)
    flat_tiles = assemble(own_tiles, near_tiles).reshape(
        tile_total, channels, padded_side * padded_side
    )
    flat_tiles = jnp.pad(flat_tiles, ((0, 0), (0, 0), (0, KSIZE - 1)))
    out_span = SIDE * padded_side
    running = jnp.zeros((tile_total, channels, out_span), jnp.float32)
    for row_step in range(KSIZE):
        for col_step in range(KSIZE):
            anchor = row_step * padded_side + col_step
            running = (
                running
                + conv_weight[:, row_step * KSIZE + col_step][None, :, None]
                * flat_tiles[:, :, anchor : anchor + out_span]
            )
    result = running.reshape(tile_total, channels, SIDE, padded_side)[:, :, :, :SIDE]
    return result.reshape(tile_total, channels, SIDE * SIDE) + conv_bias[None, :, None]


def dense_branch(
    oceanic, normed, tiles_in, norm_gain, norm_bias, weight_in, bias_in, weight_out, bias_out
):
    scaled = normed * norm_gain[None, :, None] + norm_bias[None, :, None]
    hidden_pre = (
        jnp.einsum("ch,tcp->thp", weight_in, scaled, precision=HIGHEST_PRECISION)
        + bias_in[None, :, None]
    )
    hidden = jax.nn.gelu(hidden_pre, approximate=False)
    update = (
        jnp.einsum("hc,thp->tcp", weight_out, hidden, precision=HIGHEST_PRECISION)
        + bias_out[None, :, None]
    )
    return oceanic[:, None, :] * (tiles_in + update)


def local(
    tiles_in,
    conv_weight,
    conv_bias,
    norm_gain,
    norm_bias,
    weight_in,
    bias_in,
    weight_out,
    bias_out,
    grad_out,
    tile_counts,
    ocean_mask,
    neighbours,
    sample_ids,
):
    slot_count = tiles_in.shape[0]
    channels = tiles_in.shape[1]
    device = lax.axis_index("tiles")
    slot_ids = lax.iota(jnp.int32, slot_count)
    filled = (slot_ids < tile_counts[0]).astype(jnp.float32)
    oceanic = ocean_mask.astype(jnp.float32) * filled[:, None]
    member = (sample_ids[:, None] == lax.iota(jnp.int32, SAMPLES)[None, :]).astype(jnp.float32)
    offsets = [shift_by for shift_by in range(-REACH, REACH + 1) if shift_by != 0]
    received = []
    for offset in offsets:
        received.append(passed_along(tiles_in, "tiles", -offset))
    gathered = jnp.concatenate(received[:REACH] + [tiles_in] + received[REACH:], axis=0)
    is_valid = neighbours >= 0
    position = (neighbours // slot_count - device + REACH) * slot_count + neighbours % slot_count
    position = jnp.where(is_valid, position, 0)
    near_tiles = gathered[position] * is_valid.astype(jnp.float32)[:, :, None, None]
    conv_out, conv_pull = jax.vjp(depthwise, tiles_in, near_tiles, conv_weight, conv_bias)
    tile_sum = jnp.sum(conv_out * oceanic[:, None, :], axis=(1, 2))
    local_sum = jnp.dot(tile_sum, member, precision=HIGHEST_PRECISION)
    local_cells = jnp.dot(jnp.sum(oceanic, axis=1), member, precision=HIGHEST_PRECISION)
    sample_sum, sample_cells = lax.psum((local_sum, local_cells), "tiles")
    entries = channels * sample_cells
    sample_mean = sample_sum / entries
    centred = conv_out - jnp.dot(member, sample_mean, precision=HIGHEST_PRECISION)[:, None, None]
    tile_square = jnp.sum(centred * centred * oceanic[:, None, :], axis=(1, 2))
    variance = (
        lax.psum(jnp.dot(tile_square, member, precision=HIGHEST_PRECISION), "tiles") / entries
    )
    inv_std = lax.rsqrt(variance + NORM_EPSILON)
    tile_inv = jnp.dot(member, inv_std, precision=HIGHEST_PRECISION)
    normed = centred * tile_inv[:, None, None]
    active = jnp.sum(sample_cells)
    output, dense_pull = jax.vjp(
        partial(dense_branch, oceanic),
        normed,
        tiles_in,
        norm_gain,
        norm_bias,
        weight_in,
        bias_in,
        weight_out,
        bias_out,
    )
    g_normed, g_residual, g_gain, g_nbias, g_weight_in, g_bias_in, g_weight_out, g_bias_out = (
        dense_pull(grad_out)
    )
    weighted = g_normed * oceanic[:, None, :]
    first_local = jnp.dot(jnp.sum(weighted, axis=(1, 2)), member, precision=HIGHEST_PRECISION)
    second_local = jnp.dot(
        jnp.sum(weighted * normed, axis=(1, 2)), member, precision=HIGHEST_PRECISION
    )
    first_sum, second_sum = lax.psum((first_local, second_local), "tiles")
    first_tile = jnp.dot(member, first_sum / entries, precision=HIGHEST_PRECISION)
    second_tile = jnp.dot(member, second_sum / entries, precision=HIGHEST_PRECISION)
    g_conv = (
        oceanic[:, None, :]
        * tile_inv[:, None, None]
        * (g_normed - first_tile[:, None, None] - normed * second_tile[:, None, None])
    )
    g_own, g_near, g_conv_weight, g_conv_bias = conv_pull(g_conv)
    pool_total = gathered.shape[0]
    onehot = (
        (position.reshape(-1)[:, None] == lax.iota(jnp.int32, pool_total)[None, :])
        & is_valid.reshape(-1)[:, None]
    ).astype(jnp.float32)
    backward_pool = jnp.einsum(
        "kq,kcp->qcp",
        onehot,
        g_near.reshape(slot_count * 8, channels, -1),
        precision=HIGHEST_PRECISION,
    )
    returned = backward_pool[REACH * slot_count : (REACH + 1) * slot_count]
    for offset in offsets:
        outgoing = backward_pool[(offset + REACH) * slot_count : (offset + REACH + 1) * slot_count]
        returned = returned + passed_along(outgoing, "tiles", offset)
    grad_tiles_in = g_residual + g_own + returned
    all_sums = lax.psum(
        (
            g_conv_weight,
            g_conv_bias,
            g_gain,
            g_nbias,
            g_weight_in,
            g_bias_in,
            g_weight_out,
            g_bias_out,
        ),
        "tiles",
    )
    scaled_grads = tuple((grad_part / active for grad_part in all_sums))
    return (output, grad_tiles_in) + scaled_grads


def solution(mesh):
    return jax.shard_map(
        local,
        mesh=mesh,
        in_specs=(
            P("tiles", None, None),
            P(),
            P(),
            P(),
            P(),
            P(),
            P(),
            P(),
            P(),
            P("tiles", None, None),
            P("tiles"),
            P("tiles", None),
            P("tiles", None),
            P("tiles"),
        ),
        out_specs=(
            P("tiles", None, None),
            P("tiles", None, None),
            P(),
            P(),
            P(),
            P(),
            P(),
            P(),
            P(),
            P(),
        ),
        check_vma=False,
    )
```

profile of v0, /device:TPU:1, one launch (start us, length us, event | category | flops | bytes accessed | tf_op | source)
XLA Modules:
  0.0 958.3 jit_solution(7435944153233527689)
XLA Ops:
  7.2 5.9 collective-permute-start
  13.1 3.0 collective-permute-start.1
  29.4 25.9 %collective-permute-done = f32[8,250,256]{2,0,1:T(8,128)} collective-permute-done((f32[8,250,256]{2,0,1:T(8,128)}, f32[8,250,256]{2,0,1:T(8,128)}, u32[]{:S(2)}, u32[]{:S(2)}) %collective-permute-start) | collective-permute-done | bytes 2048032 | tf_op jit(solution)/shard_map/ppermute | solution.py:21
  55.3 3.5 copy_dynamic-update-slice_fusion.4
  58.8 19.6 %collective-permute-done.1 = f32[8,250,256]{2,0,1:T(8,128)} collective-permute-done((f32[8,250,256]{2,0,1:T(8,128)}, f32[8,250,256]{2,0,1:T(8,128)}, u32[]{:S(2)}, u32[]{:S(2)}) %collective-permute-start.1) | collective-permute-done | bytes 2048032 | tf_op jit(solution)/shard_map/ppermute | solution.py:21
  78.4 3.6 copy_dynamic-update-slice_fusion.3
  86.6 3.6 copy_dynamic-update-slice_fusion.1
  90.2 3.5 copy_dynamic-update-slice_fusion
  93.7 13.0 %gather_fusion = f32[64,250,256]{2,1,0:T(8,128)} fusion(f32[40,250,256]{2,1,0:T(8,128)} %copy_dynamic-update-slice_fusion, s32[1024]{0:T(1024)S(1)} %pad_clamp_fusion), kind=kCustom, calls=%fused_computation | custom fusion | bytes 32768256 | tf_op jit(solution)/shard_map/gather | solution.py:129
  106.7 16.5 %copy.118 = f32[8,8,250,256]{2,3,0,1:T(8,128)} copy(f32[8,8,250,256]{3,2,1,0:T(8,128)} %bitcast.518) | data formatting | bytes 32768000 | tf_op jit(solution)/shard_map/gather | solution.py:129
  123.1 6.8 broadcast_multiply_fusion
  130.0 5.2 fusion.151
  146.3 23.4 %multiply_add_fusion = f32[8,250,352]{1,0,2:T(8,128)S(1)} fusion(f32[8,250,484]{1,0,2:T(8,128)S(1)} %bitcast.512, f32[250]{0:T(256)S(1)} %bitcast.547, f32[250]{0:T(256)S(1)} %bitcast.619, f32[250]{0:T(256)S(1)} %bitcast.623, f32[250]{0:T(256)S(1)} %bitcast.625, f32[250]{0:T(256)S(1)} %bitcast.549, f32[250]{0:T(256)S(1)} %bitcast.551, f32[250]{0:T(256)S(1)} %bitcast.553, ...), kind=kLoop, calls=%fused_computation.215 | loop fusion | flops 68288000 | bytes 130825216 | tf_op jit(solution)/shard_map/jvp()/add | solution.py:74
  172.9 67.6 %all-reduce.118 = (f32[5]{0:T(128)S(1)}, f32[5]{0:T(128)S(1)}) all-reduce(f32[5]{0:T(128)S(1)} %convolution_bitcast_fusion.8, f32[5]{0:T(128)S(1)} %copy-done.121), channel_id=1, replica_groups=mesh['tiles'=128] {'tiles'}, use_global_device_ids=true, to_apply=%region_1.2 | all-reduce | flops 10 | bytes 80 | tf_op jit(solution)/shard_map/psum | solution.py:134
  240.8 3.5 multiply_reduce_fusion.1
  246.4 63.8 %psum.93 = f32[5]{0:T(128)S(1)} all-reduce(f32[5]{0:T(128)S(1)} %convolution_bitcast_fusion.5), channel_id=1, replica_groups=mesh['tiles'=128] {'tiles'}, use_global_device_ids=true, to_apply=%region_5.6 | all-reduce | flops 5 | bytes 40 | tf_op jit(solution)/shard_map/psum | solution.py:140
  314.8 8.8 fusion.90
  323.7 40.0 %fusion.12 = (f32[1000]{0:T(1024)}, f32[8,1000,256]{2,1,0:T(8,128)}, f32[8,256,1000]{1,2,0:T(8,128)S(1)}) fusion(f32[8,256,1000]{1,2,0:T(8,128)S(1)} %get-tuple-element.238, f32[1000]{0:T(1024)S(1)} %copy-done.26, f32[1000,250]{1,0:T(8,128)S(1)} %copy-done, f32[8,250,256]{1,2,0:T(8,128)S(1)} %copy.125, f32[8,256]{1,0:T(8,128)S(1)} %get-tuple-element.110), kind=kOutput, calls=%fused_computation.21 | convolution fusion | flops 6294014976 | bytes 27640192 | tf_op jit(solution)/shard_map/transpose(jvp(hc,thp->tcp))/dot_general | solution.py:92
  363.7 19.8 %fusion.6 = f32[8,256,1000]{1,2,0:T(8,128)S(1)} fusion(f32[8,256,1000]{1,2,0:T(8,128)S(1)} %get-tuple-element.236, f32[8,256,1000]{1,2,0:T(8,128)S(1)} %get-tuple-element.238, f32[1000]{0:T(1024)S(1)} %copy-done.26, u8[256,1000]{0,1:T(8,128)(4,1)S(1)} %get-tuple-element.237), kind=kLoop, calls=%fused_computation.11 | loop fusion | flops 153600000 | bytes 24836000 | tf_op jit(solution)/shard_map/transpose(jvp())/add_any | solution.py:90
  383.6 16.8 %fusion.82 = (f32[250]{0:T(256)}, f32[8]{0:T(128)S(1)}, f32[8]{0:T(128)S(1)}, f32[250]{0:T(256)}, f32[8,256,250]{2,1,0:T(8,128)}) fusion(f32[8,250,256]{1,2,0:T(8,128)S(1)} %fusion.89, f32[8,256]{1,0:T(8,128)S(1)} %get-tuple-element.110, f32[250]{0:T(256)S(1)} %copy-done.68, f32[8,250,256]{1,2,0:T(8,128)S(1)} %copy.125, f32[8,256,1000]{1,2,0:T(8,128)S(1)} %fusion.6, ...), kind=kOutput, calls=%fused_computation.220 | convolution fusion | flops 6148607488 | bytes 15347256 | tf_op jit(solution)/shard_map/transpose(jvp(ch,tcp->thp))/dot_general | solution.py:87
  401.4 62.5 %all-reduce.117 = (f32[5]{0:T(128)S(1)}, f32[5]{0:T(128)S(1)}) all-reduce(f32[5]{0:T(128)S(1)} %convolution_bitcast_fusion.1, f32[5]{0:T(128)S(1)} %convolution_bitcast_fusion.3), channel_id=1, replica_groups=mesh['tiles'=128] {'tiles'}, use_global_device_ids=true, to_apply=%region_9.10 | all-reduce | flops 10 | bytes 80 | tf_op jit(solution)/shard_map/psum | solution.py:165
  466.7 2.9 fusion.147
  473.4 6.5 fusion.50
  479.9 7.6 fusion.32
  487.7 7.9 fusion.68
  495.6 7.8 bitcast_multiply_fusion.63
  503.4 17.9 %bitcast_multiply_fusion.81 = (f32[8,250,352]{1,0,2:T(8,128)}, f32[8,250,352]{1,0,2:T(8,128)}, f32[8,250,352]{1,0,2:T(8,128)}, f32[8,250,352]{1,0,2:T(8,128)}, f...) fusion(f32[8,250,16,22]{1,0,3,2:T(8,128)} %copy-done.3, ...), kind=kLoop, calls=%fused_computation.144 | loop fusion | flops 12672000 | bytes 53522000 | tf_op jit(solution)/shard_map/transpose(jvp())/mul | solution.py:75
  521.3 18.3 %bitcast_multiply_fusion.102 = (f32[8,250,352]{1,0,2:T(8,128)}, f32[8,250,352]{1,0,2:T(8,128)}, f32[8,250,352]{1,0,2:T(8,128)}, f32[8,250,352]{1,0,2:T(8,128)}, ...) fusion(f32[8,250,16,22]{1,0,3,2:T(8,128)} %copy-done.3, ...), kind=kLoop, calls=%fused_computation.165 | loop fusion | flops 12672000 | bytes 53522000 | tf_op jit(solution)/shard_map/transpose(jvp())/mul | solution.py:75
  539.7 80.7 %pad_add_fusion.1 = f32[8,250,490]{1,0,2:T(8,128)S(1)} fusion(f32[8,250,352]{1,0,2:T(8,128)} %get-tuple-element.180, f32[8,250,352]{1,0,2:T(8,128)} %get-tuple-element.179, f32[8,250,352]{1,0,2:T(8,128)} %get-tuple-element.178, f32[8,250,352]{1,0,2:T(8,128)} %get-tuple-element.177, f32[8,250,352]{1,0,2:T(8,128)} %get-tuple-element.176, ...), kind=kLoop, calls=%fused_computation.55 | loop fusion | flops 41160000 | bytes 125008000 | tf_op jit(solution)/shard_map/transpose(jvp())/add_any | solution.py:76
  620.3 5.2 pad_add_fusion.2
  629.5 12.9 %fusion.98 = f32[1000,250]{1,0:T(8,128)} fusion(f32[8,250,256]{1,2,0:T(8,128)S(1)} %copy-done.7, f32[8,256]{1,0:T(8,128)S(1)} %get-tuple-element.110, f32[8,1000,256]{2,1,0:T(8,128)} %get-tuple-element.106, f32[8,256,1000]{1,2,0:T(8,128)} %copy-done.5, f32[1000]{0:T(1024)S(1)} %copy-done.26), kind=kOutput, calls=%fused_computation.249 | convolution fusion | flops 6150656000 | bytes 19444192 | tf_op jit(solution)/shard_map/transpose(jvp(hc,thp->tcp))/dot_general | solution.py:92
  642.5 15.8 %fusion.87 = f32[8,250,256]{1,2,0:T(8,128)} fusion(f32[8,250,256]{1,2,0:T(8,128)S(1)} %copy-done.12, f32[250]{0:T(256)S(1)} %copy-done.115, f32[8,256]{1,0:T(8,128)S(1)} %get-tuple-element.110, f32[1000,250]{1,0:T(8,128)S(1)} %copy-done, f32[8,1000,256]{2,1,0:T(8,128)S(1)} %bitcast.520, f32[8,256,1000]{1,2,0:T(8,128)S(1)} %bitcast.517, f32[1000]{0:T(1024)S(1)} %copy-done.26), kind=kOutput, calls=%fused_computation.226 | convolution fusion | flops 6151680000 | bytes 21493192 | tf_op jit(solution)/shard_map/jvp(hc,thp->tcp)/dot_general | solution.py:92
  658.3 3.0 copy.135
  661.3 3.7 copy.127
  667.7 6.5 pad_add_fusion
  674.1 29.2 %copy.128 = f32[8,8,250,256]{3,1,0,2:T(8,128)} copy(f32[8,8,250,256]{2,0,3,1:T(8,128)} %pad_add_fusion) | data formatting | bytes 32768000 | tf_op jit(solution)/shard_map/transpose(jvp())/add_any | solution.py:32
  703.3 10.6 %fusion = f32[40,250,256]{2,0,1:T(8,128)S(1)} fusion(f32[8,8,250,256]{3,1,0,2:T(8,128)} %copy.128, s32[64]{0:T(128)S(1)} %copy-done.113, pred[64]{0:T(512)(128)(4,1)S(1)} %copy-done.116), kind=kOutput, calls=%fused_computation.2 | convolution fusion | flops 1966085120 | bytes 26624320 | tf_op jit(solution)/shard_map/kq,kcp->qcp/dot_general | solution.py:179
  713.9 4.1 fusion.152
  719.4 5.4 collective-permute-start.7
  730.4 3.2 copy.140
  734.0 10.6 %fusion.97 = f32[250,1000]{0,1:T(8,128)} fusion(f32[8,256,1000]{1,2,0:T(8,128)} %copy-done.4, f32[8,250,256]{1,2,0:T(8,128)} %copy-done.9, f32[250]{0:T(256)} %param.18, f32[250]{0:T(256)S(1)} %copy-done.69), kind=kOutput, calls=%fused_computation.248 | convolution fusion | flops 6145024000 | bytes 11242000 | tf_op jit(solution)/shard_map/transpose(jvp(ch,tcp->thp))/dot_general | solution.py:87
  746.0 107.4 %all-reduce.116 = (f32[250,49]{0,1:T(8,128)S(1)}, f32[250]{0:T(256)S(1)}, f32[250]{0:T(256)S(1)}, f32[250]{0:T(256)S(1)}, f32[1000]{0:T(1024)S(1)}, /*index=5*/f32[250]{0:T(256)S(1)}) all-reduce(f32[250,49]{0,1:T(8,128)S(1)} %pad_add_fusion.8, f32[250]{0:T(256)S(1)} %copy-done.108, ...), channel_id=1, replica_groups=mesh['tiles'=128] {'tiles'}, use_global_device_ids=true, to_apply=%region_59.60 | all-reduce | flops 14250 | bytes 114000 | tf_op jit(solution)/shard_map/psum | solution.py:190
  858.0 65.8 %all-reduce.122.cloned.1.call-done = (f32[250,1000]{0,1:T(8,128)}, f32[1000,250]{1,0:T(8,128)}) async-done(((f32[250,1000]{0,1:T(8,128)}, f32[1000,250]{1,0:T(8,128)}), (f32[250,1000]{0,1:T(8,128)}, f32[1000,250]{1,0:T(8,128)})) %all-reduce.122.cloned.1.call-update) | async-done | bytes 2000016 | tf_op jit(solution)/shard_map/psum | solution.py:190
  929.4 2.9 copy.130
  935.2 2.9 copy.132
  938.1 2.9 copy.131
  941.0 7.0 fusion.81
  948.0 3.0 copy.136
  (330 shorter events, 73.2 us)
Async XLA Ops:
  7.2 316.5 %copy-start = (f32[1000,250]{1,0:T(8,128)S(1)}, f32[1000,250]{1,0:T(8,128)}, u32[]{:S(2)}) copy-start(f32[1000,250]{1,0:T(8,128)} %param.21) | copy-start | bytes 3000004
  7.2 20.1 %copy-start.25 = (f32[250,49]{0,1:T(8,128)S(1)}, f32[250,49]{0,1:T(8,128)}, u32[]{:S(2)}) copy-start(f32[250,49]{0,1:T(8,128)} %param.15) | copy-start | bytes 147004
  7.2 916.6 %all-reduce.122.cloned.1.call-start = ((), (), s32[]{:S(2)}) async-start(), calls=%async_computation | async-start | bytes 4096000 | tf_op jit(solution)/shard_map/psum | solution.py:190
  7.2 48.1 %collective-permute-start = (f32[8,250,256]{2,0,1:T(8,128)}, f32[8,250,256]{2,0,1:T(8,128)}, u32[]{:S(2)}, u32[]{:S(2)}) collective-permute-start(f32[8,250,256]{2,0,1:T(8,128)} %param.14), channel_id=1, source_target_pairs={{0,2},{1,3},{2,4},{3,5},{4,6},{5,7},{6,8},{7,9},{8,10},{9,11},{10,... | collective-permute-start | bytes 6144008 | tf_op jit(solution)/shard_map/ppermute | solution.py:21
  13.1 65.3 %collective-permute-start.1 = (f32[8,250,256]{2,0,1:T(8,128)}, f32[8,250,256]{2,0,1:T(8,128)}, u32[]{:S(2)}, u32[]{:S(2)}) collective-permute-start(f32[8,250,256]{2,0,1:T(8,128)} %param.14), channel_id=1, source_target_pairs={{0,1},{1,2},{2,3},{3,4},{4,5},{5,6},{6,7},{7,8},{8,9},{9,10},{10,1... | collective-permute-start | bytes 6144008 | tf_op jit(solution)/shard_map/ppermute | solution.py:21
  16.2 74.0 %collective-permute-start.3 = (f32[8,250,256]{2,0,1:T(8,128)}, f32[8,250,256]{2,0,1:T(8,128)}, u32[]{:S(2)}, u32[]{:S(2)}) collective-permute-start(f32[8,250,256]{2,0,1:T(8,128)} %param.14), channel_id=1, source_target_pairs={{2,0},{3,1},{4,2},{5,3},{6,4},{7,5},{8,6},{9,7},{10,8},{11,9},{12,... | collective-permute-start | bytes 6144008 | tf_op jit(solution)/shard_map/ppermute | solution.py:21
  17.5 69.2 %collective-permute-start.2 = (f32[8,250,256]{2,0,1:T(8,128)}, f32[8,250,256]{2,0,1:T(8,128)}, u32[]{:S(2)}, u32[]{:S(2)}) collective-permute-start(f32[8,250,256]{2,0,1:T(8,128)} %param.14), channel_id=1, source_target_pairs={{1,0},{2,1},{3,2},{4,3},{5,4},{6,5},{7,6},{8,7},{9,8},{10,9},{11,1... | collective-permute-start | bytes 6144008 | tf_op jit(solution)/shard_map/ppermute | solution.py:21
  27.1 115.4 %copy-start.11 = (f32[8,250,256]{1,2,0:T(8,128)}, f32[8,250,256]{1,2,0:T(8,128)S(1)}, u32[]{:S(2)}) copy-start(f32[8,250,256]{1,2,0:T(8,128)S(1)} %copy.124) | copy-start | bytes 6144004
  29.3 116.7 %copy-start.28 = (f32[250,1]{0,1:T(1,128)}, f32[250,1]{0,1:T(1,128)S(1)}, u32[]{:S(2)}) copy-start(f32[250,1]{0,1:T(1,128)S(1)} %get-tuple-element.211) | copy-start | bytes 3004
  58.8 23.2 %copy-start.16 = (f32[8,250,256]{2,0,1:T(8,128)S(1)}, f32[8,250,256]{2,0,1:T(8,128)}, u32[]{:S(2)}) copy-start(f32[8,250,256]{2,0,1:T(8,128)} %param.14) | copy-start | bytes 6144004
  146.0 23.8 %copy-start.1 = (f32[8,250,22,22]{1,0,3,2:T(8,128)}, f32[8,250,22,22]{1,0,3,2:T(8,128)S(1)}, u32[]{:S(2)}) copy-start(f32[8,250,22,22]{1,0,3,2:T(8,128)S(1)} %copy.120) | copy-start | bytes 11616004
  146.3 25.1 %copy-start.27 = (f32[250]{0:T(256)S(1)}, f32[250]{0:T(256)}, u32[]{:S(2)}) copy-start(f32[250]{0:T(256)} %param.16) | copy-start | bytes 3004
  146.3 25.8 %copy-start.117 = (s32[8]{0:T(128)S(1)}, s32[8]{0:T(128)}, u32[]{:S(2)}) copy-start(s32[8]{0:T(128)} %param.27) | copy-start | bytes 100
  146.3 26.6 %copy-start.121 = (f32[5]{0:T(128)S(1)}, f32[5]{0:T(128)}, u32[]{:S(2)}) copy-start(f32[5]{0:T(128)} %convolution_bitcast_fusion.7) | copy-start | bytes 64
  240.6 69.7 %copy-start.119 = (f32[5]{0:T(128)}, f32[5]{0:T(128)S(1)}, u32[]{:S(2)}) copy-start(f32[5]{0:T(128)S(1)} %get-tuple-element.102) | copy-start | bytes 64
  240.7 72.0 %copy-start.72 = (f32[8]{0:T(128)}, f32[8]{0:T(128)S(1)}, u32[]{:S(2)}) copy-start(f32[8]{0:T(128)S(1)} %convolution_bitcast_fusion.6) | copy-start | bytes 100
  246.4 137.1 %copy-start.6 = (f32[8,250,256]{1,2,0:T(8,128)}, f32[8,250,256]{1,2,0:T(8,128)S(1)}, u32[]{:S(2)}) copy-start(f32[8,250,256]{1,2,0:T(8,128)S(1)} %copy.125) | copy-start | bytes 6144004
  314.8 68.7 %copy-start.9 = (f32[8,250,256]{1,2,0:T(8,128)}, f32[8,250,256]{1,2,0:T(8,128)S(1)}, u32[]{:S(2)}) copy-start(f32[8,250,256]{1,2,0:T(8,128)S(1)} %fusion.89) | copy-start | bytes 6144004
  323.6 40.1 %copy-start.5 = (f32[8,256,1000]{1,2,0:T(8,128)}, f32[8,256,1000]{1,2,0:T(8,128)S(1)}, u32[]{:S(2)}) copy-start(f32[8,256,1000]{1,2,0:T(8,128)S(1)} %get-tuple-element.238) | copy-start | bytes 24576004
  383.5 16.9 %copy-start.4 = (f32[8,256,1000]{1,2,0:T(8,128)}, f32[8,256,1000]{1,2,0:T(8,128)S(1)}, u32[]{:S(2)}) copy-start(f32[8,256,1000]{1,2,0:T(8,128)S(1)} %fusion.6) | copy-start | bytes 24576004
  383.5 16.9 %copy-start.118 = (s32[8]{0:T(128)S(1)}, s32[8]{0:T(128)}, u32[]{:S(2)}) copy-start(s32[8]{0:T(128)} %param.27) | copy-start | bytes 100
  383.6 17.2 %copy-start.120 = (f32[5]{0:T(128)S(1)}, f32[5]{0:T(128)}, u32[]{:S(2)}) copy-start(f32[5]{0:T(128)} %copy-done.119) | copy-start | bytes 64
  383.6 83.1 %copy-start.71 = (f32[8]{0:T(128)S(1)}, f32[8]{0:T(128)}, u32[]{:S(2)}) copy-start(f32[8]{0:T(128)} %copy-done.70) | copy-start | bytes 100
  383.6 83.1 %copy-start.73 = (f32[8]{0:T(128)S(1)}, f32[8]{0:T(128)}, u32[]{:S(2)}) copy-start(f32[8]{0:T(128)} %copy-done.72) | copy-start | bytes 100
  400.4 66.3 %copy-start.8 = (f32[8,256,250]{2,1,0:T(8,128)S(1)}, f32[8,256,250]{2,1,0:T(8,128)}, u32[]{:S(2)}) copy-start(f32[8,256,250]{2,1,0:T(8,128)} %get-tuple-element.239) | copy-start | bytes 6144004
  473.4 22.2 %copy-start.3 = (f32[8,250,16,22]{1,0,3,2:T(8,128)}, f32[8,250,16,22]{1,0,3,2:T(8,128)S(1)}, u32[]{:S(2)}) copy-start(f32[8,250,16,22]{1,0,3,2:T(8,128)S(1)} %pad.355) | copy-start | bytes 8448004
  539.6 80.7 %copy-start.14 = (f32[8,250,352]{1,0,2:T(8,128)S(1)}, f32[8,250,352]{1,0,2:T(8,128)}, u32[]{:S(2)}) copy-start(f32[8,250,352]{1,0,2:T(8,128)} %get-tuple-element.181) | copy-start | bytes 8448004
  539.6 80.7 %copy-start.15 = (f32[8,250,352]{1,0,2:T(8,128)S(1)}, f32[8,250,352]{1,0,2:T(8,128)}, u32[]{:S(2)}) copy-start(f32[8,250,352]{1,0,2:T(8,128)} %get-tuple-element.182) | copy-start | bytes 8448004
  627.1 15.4 %slice-start = ((s8[8192000]{0:T(1024)(128)(4,1)}), s8[4194304]{0:T(1024)(128)(4,1)S(1)}, s32[]{:S(2)}) async-start(s8[8192000]{0:T(1024)(128)(4,1)} %bitcast.516), calls=%async_computation.1 | async-start | bytes 8388608
  627.1 15.4 %slice-start.2 = ((s8[8192000]{0:T(1024)(128)(4,1)}), s8[4194304]{0:T(1024)(128)(4,1)S(1)}, s32[]{:S(2)}) async-start(s8[8192000]{0:T(1024)(128)(4,1)} %bitcast.519), calls=%async_computation.3 | async-start | bytes 8388608
  629.5 13.0 %slice-start.1 = ((s8[8192000]{0:T(1024)(128)(4,1)}), s8[3997696]{0:T(1024)(128)(4,1)S(1)}, s32[]{:S(2)}) async-start(s8[8192000]{0:T(1024)(128)(4,1)} %bitcast.516), calls=%async_computation.2 | async-start | bytes 7995392
  629.5 13.0 %slice-start.3 = ((s8[8192000]{0:T(1024)(128)(4,1)}), s8[3997696]{0:T(1024)(128)(4,1)S(1)}, s32[]{:S(2)}) async-start(s8[8192000]{0:T(1024)(128)(4,1)} %bitcast.519), calls=%async_computation.4 | async-start | bytes 7995392
  629.5 13.0 %copy-start.12 = (f32[8,250,256]{1,2,0:T(8,128)S(1)}, f32[8,250,256]{1,2,0:T(8,128)}, u32[]{:S(2)}) copy-start(f32[8,250,256]{1,2,0:T(8,128)} %copy-done.11) | copy-start | bytes 6144004
  629.5 13.0 %copy-start.115 = (f32[250]{0:T(256)S(1)}, f32[250]{0:T(256)}, u32[]{:S(2)}) copy-start(f32[250]{0:T(256)} %param.22) | copy-start | bytes 3004
  674.1 29.2 %copy-start.113 = (s32[64]{0:T(128)S(1)}, s32[64]{0:T(128)}, u32[]{:S(2)}) copy-start(s32[64]{0:T(128)} %eq.33) | copy-start | bytes 772
  674.1 29.2 %copy-start.116 = (pred[64]{0:T(512)(128)(4,1)S(1)}, pred[64]{0:T(512)(128)(4,1)}, u32[]{:S(2)}) copy-start(pred[64]{0:T(512)(128)(4,1)} %and.23) | copy-start | bytes 196
  718.0 15.6 %copy-start.69 = (f32[250]{0:T(256)S(1)}, f32[250]{0:T(256)}, u32[]{:S(2)}) copy-start(f32[250]{0:T(256)} %param.17) | copy-start | bytes 3004
  718.0 211.4 %collective-permute-start.4 = (f32[8,250,256]{2,0,1:T(8,128)}, f32[8,250,256]{2,0,1:T(8,128)}, u32[]{:S(2)}, u32[]{:S(2)}) collective-permute-start(f32[8,250,256]{2,0,1:T(8,128)} %get-tuple-element.123), channel_id=1, source_target_pairs={{2,0},{3,1},{4,2},{5,3},{6,4},{7,5},{8,6},{9,7},{10,8},{11,9},{12,... | collective-permute-start | bytes 6144008 | tf_op jit(solution)/shard_map/ppermute | solution.py:21
  719.4 212.9 %collective-permute-start.7 = (f32[8,250,256]{2,0,1:T(8,128)}, f32[8,250,256]{2,0,1:T(8,128)}, u32[]{:S(2)}, u32[]{:S(2)}) collective-permute-start(f32[8,250,256]{2,0,1:T(8,128)} %get-tuple-element.124), channel_id=1, source_target_pairs={{0,2},{1,3},{2,4},{3,5},{4,6},{5,7},{6,8},{7,9},{8,10},{9,11},{10,... | collective-permute-start | bytes 6144008 | tf_op jit(solution)/shard_map/ppermute | solution.py:21
  724.8 210.4 %collective-permute-start.6 = (f32[8,250,256]{2,0,1:T(8,128)}, f32[8,250,256]{2,0,1:T(8,128)}, u32[]{:S(2)}, u32[]{:S(2)}) collective-permute-start(f32[8,250,256]{2,0,1:T(8,128)} %get-tuple-element.125), channel_id=1, source_target_pairs={{0,1},{1,2},{2,3},{3,4},{4,5},{5,6},{6,7},{7,8},{8,9},{9,10},{10,1... | collective-permute-start | bytes 6144008 | tf_op jit(solution)/shard_map/ppermute | solution.py:21
  727.5 210.5 %collective-permute-start.5 = (f32[8,250,256]{2,0,1:T(8,128)}, f32[8,250,256]{2,0,1:T(8,128)}, u32[]{:S(2)}, u32[]{:S(2)}) collective-permute-start(f32[8,250,256]{2,0,1:T(8,128)} %get-tuple-element.126), channel_id=1, source_target_pairs={{1,0},{2,1},{3,2},{4,3},{5,4},{6,5},{7,6},{8,7},{9,8},{10,9},{11,1... | collective-permute-start | bytes 6144008 | tf_op jit(solution)/shard_map/ppermute | solution.py:21
  733.6 11.0 %copy-start.76 = (f32[250]{0:T(256)S(1)}, f32[250]{0:T(256)}, u32[]{:S(2)}) copy-start(f32[250]{0:T(256)} %get-tuple-element.60) | copy-start | bytes 3004
  733.6 11.0 %copy-start.77 = (f32[250]{0:T(256)S(1)}, f32[250]{0:T(256)}, u32[]{:S(2)}) copy-start(f32[250]{0:T(256)} %get-tuple-element.61) | copy-start | bytes 3004
  733.7 11.0 %copy-start.78 = (f32[250]{0:T(256)S(1)}, f32[250]{0:T(256)}, u32[]{:S(2)}) copy-start(f32[250]{0:T(256)} %get-tuple-element.62) | copy-start | bytes 3004
  734.0 12.0 %copy-start.105 = (f32[250]{0:T(256)S(1)}, f32[250]{0:T(256)}, u32[]{:S(2)}) copy-start(f32[250]{0:T(256)} %get-tuple-element.89) | copy-start | bytes 3004
  734.0 12.0 %copy-start.106 = (f32[250]{0:T(256)S(1)}, f32[250]{0:T(256)}, u32[]{:S(2)}) copy-start(f32[250]{0:T(256)} %get-tuple-element.92) | copy-start | bytes 3004
  734.0 12.0 %copy-start.107 = (f32[250]{0:T(256)S(1)}, f32[250]{0:T(256)}, u32[]{:S(2)}) copy-start(f32[250]{0:T(256)} %reduce_sum.624) | copy-start | bytes 3004
  734.0 12.0 %copy-start.108 = (f32[250]{0:T(256)S(1)}, f32[250]{0:T(256)}, u32[]{:S(2)}) copy-start(f32[250]{0:T(256)} %get-tuple-element.107) | copy-start | bytes 3004
  (87 other events, 563.5 us)
Sparse Core Ops, SparseCore 0:
  744.8 178.9 all-reduce.121
where the time goes:
time: 969 us; the launch traced here: 958 us
  blocking collectives  301 us (31%)
  other arithmetic  241 us (25%)
  local copies, waits for them, and re-layouts  142 us (15%)
  matrix products  118 us (12%)
  waiting for transfers between devices  114 us (12%)
  starting transfers between devices  25.2 us (3%)
  between operations  17 us (2%)
    psum x1, blocking collectives, local(): lax.psum((g_conv_weight, g_conv_bias, g_gain, g_nbias, g_weight_in, g_bia...  107 us
    add_any x2, other arithmetic, depthwise(): flat_tiles[:, :, anchor:anchor + out_span]  85.9 us
    dot_general x3, matrix products, dense_branch(): jnp.einsum('hc,thp->tcp', weight_out, hidden, precision=HIGHEST_PRECISION)  68.8 us
    psum x1, blocking collectives, local(): sample_sum, sample_cells = lax.psum((local_sum, local_cells), 'tiles')  67.6 us
    psum x1, waiting for transfers between devices, local(): lax.psum((g_conv_weight, g_conv_bias, g_gain, g_nbias, g_weight_in, g_bia...  65.8 us
    psum x1, blocking collectives, local(): lax.psum(jnp.dot(tile_square, member, precision=HIGHEST_PRECISION), 'tiles')  63.8 us
    psum x1, blocking collectives, local(): first_sum, second_sum = lax.psum((first_local, second_local), 'tiles')  62.5 us
    ppermute x8, waiting for transfers between devices, passed_along(): return lax.ppermute(block, axis, route)  48.2 us
  transfers between devices with their start and end apart: 9, of which 4 were waited for; matrix products, arithmetic and copies ran while one was open for 6% of the time, Pallas kernels for 0%

commit v1 on v0

v1 whole, which is shorter than its diff:
```python
import functools

import jax
import jax.numpy as jnp
from jax import lax
from jax.experimental import pallas as pl
from jax.experimental.pallas import tpu as pltpu
from jax.sharding import PartitionSpec as P

SIDE = 16
KSIZE = 7
RIM = 3
REACH = 2
SAMPLES = 5
CAP = 8
CELLS = SIDE * SIDE
PAD = SIDE + 2 * RIM
LANES = 128
GROUPS = 2
ROWS = CELLS * CAP
RIM_CELLS = 156
RIM_ROWS = RIM_CELLS * CAP
HIDDEN_PAD = 1024
NORM_EPSILON = 1e-05
F32 = jnp.float32
BF16 = jnp.bfloat16
MIB = 1 << 20
MESH = pl.DeviceIdType.MESH
VMEM_SPEC = pl.BlockSpec(memory_space=pltpu.VMEM)
SMEM_SPEC = pl.BlockSpec(memory_space=pltpu.SMEM)
ANY_SPEC = pl.BlockSpec(memory_space=pl.ANY)


def params(mib=56, **more):
    return pltpu.CompilerParams(vmem_limit_bytes=mib * MIB, **more)


def rim_index(r, c):
    if r < RIM:
        return r * SIDE + c
    if r >= SIDE - RIM:
        return 48 + (r - (SIDE - RIM)) * SIDE + c
    if c < RIM:
        return 96 + (r - RIM) * RIM + c
    return 126 + (r - RIM) * RIM + c - (SIDE - RIM)


def region_runs():
    spans = {-1: (0, SIDE - RIM, RIM), 0: (RIM, 0, SIDE), 1: (RIM + SIDE, 0, RIM)}
    order = [(-1, -1), (-1, 0), (-1, 1), (0, -1), (0, 1), (1, -1), (1, 0), (1, 1)]
    runs = []
    for dr, dc in order:
        dst_r, src_r, rows = spans[dr]
        dst_c, src_c, cols = spans[dc]
        found = []

        def add(cells):
            start = 0
            while start < len(cells):
                stop = start + 1
                while (
                    stop < len(cells)
                    and stop - start < 8
                    and cells[stop][0] - cells[stop - 1][0] == cells[1][0] - cells[0][0]
                    and cells[stop][1] - cells[stop - 1][1] == cells[1][1] - cells[0][1]
                ):
                    stop += 1
                step = (cells[1][0] - cells[0][0], cells[1][1] - cells[0][1])
                found.append((cells[start][0], step[0], cells[start][1], step[1], stop - start))
                start = stop

        if dr == 0:
            for j in range(cols):
                cells = [
                    ((dst_r + i) * PAD + dst_c + j, rim_index(src_r + i, src_c + j))
                    for i in range(rows)
                ]
                add(cells[:RIM])
                add(cells[RIM : SIDE - RIM])
                add(cells[SIDE - RIM :])
        else:
            for i in range(rows):
                add(
                    [
                        ((dst_r + i) * PAD + dst_c + j, rim_index(src_r + i, src_c + j))
                        for j in range(cols)
                    ]
                )
        runs.append(found)
    return runs


RUNS = region_runs()


def to_rows_kernel(x_ref, o_ref):
    t = pl.program_id(0)
    for g in range(GROUPS):
        v = x_ref[0, g * LANES : (g + 1) * LANES, :]
        if g == 1:
            channel = lax.broadcasted_iota(jnp.int32, v.shape, 0)
            v = jnp.where(channel < 250 - LANES, v, 0.0)
        o_ref[g, pl.ds(t, CELLS, stride=CAP), :] = v.T


def to_rows_rim_kernel(x_ref, o_ref, rim_ref):
    to_rows_kernel(x_ref, o_ref)

    @pl.when(pl.program_id(0) == CAP - 1)
    def _():
        for g in range(GROUPS):
            for first, rim, cells in [(0, 0, 48), (13 * SIDE, 48, 48)]:
                rim_ref[g, pl.ds(rim * CAP, cells * CAP), :] = o_ref[
                    g, pl.ds(first * CAP, cells * CAP), :
                ]
            for r in range(RIM, SIDE - RIM):
                for c in (0, SIDE - RIM):
                    rim_ref[g, pl.ds(rim_index(r, c) * CAP, RIM * CAP), :] = o_ref[
                        g, pl.ds((r * SIDE + c) * CAP, RIM * CAP), :
                    ]


def to_rows(x, with_rim):
    block = pl.BlockSpec((GROUPS, ROWS, LANES), lambda t: (0, 0, 0))
    rows = jax.ShapeDtypeStruct((GROUPS, ROWS, LANES), F32)
    rim_block = pl.BlockSpec((GROUPS, RIM_ROWS, LANES), lambda t: (0, 0, 0))
    rim = jax.ShapeDtypeStruct((GROUPS, RIM_ROWS, LANES), F32)
    return pl.pallas_call(
        to_rows_rim_kernel if with_rim else to_rows_kernel,
        grid=(CAP,),
        in_specs=[pl.BlockSpec((1, 2 * LANES, CELLS), lambda t: (t, 0, 0))],
        out_specs=(block, rim_block) if with_rim else block,
        out_shape=(rows, rim) if with_rim else rows,
        compiler_params=params(),
        cost_estimate=pl.CostEstimate(flops=0, bytes_accessed=5 * MIB, transcendentals=0),
        name="to_rows",
    )(x)


def from_rows_kernel(x_ref, o_ref):
    t = pl.program_id(0)
    for g in range(GROUPS):
        o_ref[0, g * LANES : (g + 1) * LANES, :] = x_ref[g, pl.ds(t, CELLS, stride=CAP), :].T


def from_rows(x):
    return pl.pallas_call(
        from_rows_kernel,
        grid=(CAP,),
        in_specs=[pl.BlockSpec((GROUPS, ROWS, LANES), lambda t: (0, 0, 0))],
        out_specs=pl.BlockSpec((1, 2 * LANES, CELLS), lambda t: (t, 0, 0)),
        out_shape=jax.ShapeDtypeStruct((CAP, 250, CELLS), F32),
        compiler_params=params(),
        cost_estimate=pl.CostEstimate(flops=0, bytes_accessed=5 * MIB, transcendentals=0),
        name="from_rows",
    )(x)


def lane_mask(g):
    lane = lax.broadcasted_iota(jnp.int32, (CAP, LANES), 1)
    return (lane < 250 - g * LANES).astype(F32)


def conv_kernel(
    near_ref, own_ref, rim_ref, r0, r1, r2, r3, w_ref, b_ref, mask_ref, member_ref,
    padded_ref, conv_ref, stat_ref, pool, sems,
):
    sources = [r0, r1, rim_ref, r2, r3]
    copies = [
        pltpu.make_async_copy(
            src, pool.at[:, pl.ds(i * RIM_ROWS, RIM_ROWS), :], sems.at[i]
        )
        for i, src in enumerate(sources)
    ]
    for copy in copies:
        copy.start()
    for g in range(GROUPS):
        pool[g, pl.ds(5 * RIM_ROWS, RIM_ROWS), :] = jnp.zeros((RIM_ROWS, LANES), F32)
        for r in range(SIDE):
            padded_ref[g, pl.ds(((r + RIM) * PAD + RIM) * CAP, SIDE * CAP), :] = own_ref[
                g, pl.ds(r * SIDE * CAP, SIDE * CAP), :
            ]
    for copy in copies:
        copy.wait()

    def fill(t, carry):
        for k in range(8):
            q = near_ref[t, k]
            for dst, dst_step, src, src_step, length in RUNS[k]:
                for g in range(GROUPS):
                    padded_ref[
                        g, pl.ds(dst * CAP + t, length, stride=dst_step * CAP), :
                    ] = pool[g, pl.ds(q + src * CAP, length, stride=src_step * CAP), :]
        return carry

    lax.fori_loop(0, CAP, fill, 0)

    sums = jnp.zeros((CAP, LANES), F32)
    cells = jnp.zeros((CAP, LANES), F32)
    for g in range(GROUPS):

        def row(r, carry):
            total, count = carry
            acc = jnp.broadcast_to(b_ref[g][None], (SIDE, CAP, LANES))
            for a in range(KSIZE):
                x = padded_ref[g, pl.ds((r + a) * PAD * CAP, PAD * CAP), :].reshape(
                    PAD, CAP, LANES
                )
                for b in range(KSIZE):
                    acc = acc + w_ref[g, a * KSIZE + b][None] * x[b : b + SIDE]
            conv_ref[g, pl.ds(r * SIDE * CAP, SIDE * CAP), :] = acc.reshape(SIDE * CAP, LANES)
            m = mask_ref[pl.ds(r * SIDE, SIDE)]
            return total + jnp.sum(acc * m, axis=0), count + jnp.sum(m, axis=0)

        total, count = lax.fori_loop(
            0, SIDE, row, (jnp.zeros((CAP, LANES), F32), jnp.zeros((CAP, LANES), F32))
        )
        sums = sums + total
        cells = count
    entries = 250.0 * cells
    total = jnp.broadcast_to(jnp.sum(sums, axis=1, keepdims=True), (CAP, LANES))
    mean = total / jnp.maximum(entries, 1.0)

    squares = jnp.zeros((CAP, LANES), F32)
    for g in range(GROUPS):

        def square(r, acc):
            x = conv_ref[g, pl.ds(r * SIDE * CAP, SIDE * CAP), :].reshape(SIDE, CAP, LANES)
            diff = x - mean[None]
            return acc + jnp.sum(diff * diff * mask_ref[pl.ds(r * SIDE, SIDE)], axis=0)

        part = lax.fori_loop(0, SIDE, square, jnp.zeros((CAP, LANES), F32))
        squares = squares + part * lane_mask(g)
    spread = jnp.broadcast_to(jnp.sum(squares, axis=1, keepdims=True), (CAP, LANES))

    member = member_ref[...]
    n_tile = member * entries
    n = jnp.sum(n_tile, axis=0, keepdims=True)
    centre = jnp.sum(n_tile * mean, axis=0, keepdims=True) / jnp.maximum(n, 1.0)
    off = mean - centre
    m2 = jnp.sum(member * spread + n_tile * off * off, axis=0, keepdims=True)
    row_id = lax.broadcasted_iota(jnp.int32, (CAP, LANES), 0)
    stat_ref[...] = jnp.where(
        row_id == 0, n, jnp.where(row_id == 1, centre, jnp.where(row_id == 2, m2, 0.0))
    )


def conv_forward(near, own, rim, received, w, b, mask, member):
    return pl.pallas_call(
        conv_kernel,
        in_specs=[SMEM_SPEC, VMEM_SPEC] + [ANY_SPEC] * 5 + [VMEM_SPEC] * 4,
        out_specs=(VMEM_SPEC,) * 3,
        out_shape=(
            jax.ShapeDtypeStruct((GROUPS, PAD * PAD * CAP, LANES), F32),
            jax.ShapeDtypeStruct((GROUPS, ROWS, LANES), F32),
            jax.ShapeDtypeStruct((CAP, LANES), F32),
        ),
        scratch_shapes=[
            pltpu.VMEM((GROUPS, 6 * RIM_ROWS, LANES), F32),
            pltpu.SemaphoreType.DMA((5,)),
        ],
        compiler_params=params(),
        name="conv_forward",
    )(near, own, rim, *received, w, b, mask, member)


def exchange(x, send, recv, slots, first, mine, count, peer_of):
    copies = []
    for j in range(1, count):
        copies.append(
            pltpu.make_async_remote_copy(
                src_ref=x,
                dst_ref=slots.at[mine],
                send_sem=send.at[first + j],
                recv_sem=recv.at[first + j],
                device_id=(peer_of(j),),
                device_id_type=MESH,
            )
        )
    for copy in copies:
        copy.start()
    slots[mine] = x[...]
    for copy in copies:
        copy.wait()


INNER = 8
OUTER = 16


def merge_stats(parts):
    n = jnp.sum(parts[:, 0:1], axis=0)
    mean = jnp.sum(parts[:, 0:1] * parts[:, 1:2], axis=0) / jnp.maximum(n, 1.0)
    off = parts[:, 1:2] - mean[None]
    m2 = jnp.sum(parts[:, 2:3] + parts[:, 0:1] * off * off, axis=0)
    row_id = lax.broadcasted_iota(jnp.int32, (CAP, LANES), 0)
    return jnp.where(row_id == 0, n, jnp.where(row_id == 1, mean, jnp.where(row_id == 2, m2, 0.0)))


def merge_sums(parts):
    return jnp.sum(parts, axis=0)


def reduce_kernel(merge, x_ref, o_ref, inner, outer, partial, send, recv):
    me = lax.axis_index("tiles")
    group, place = me // INNER, me % INNER

    def inner_peer(j):
        return group * INNER + (place + j) % INNER

    def outer_peer(j):
        return ((group + j) % OUTER) * INNER + place

    barrier = pltpu.get_barrier_semaphore()
    for j in range(1, INNER):
        pl.semaphore_signal(barrier, inc=1, device_id=(inner_peer(j),), device_id_type=MESH)
    for j in range(1, OUTER):
        pl.semaphore_signal(barrier, inc=1, device_id=(outer_peer(j),), device_id_type=MESH)
    pl.semaphore_wait(barrier, INNER + OUTER - 2)
    exchange(x_ref, send, recv, inner, 0, place, INNER, inner_peer)
    partial[...] = merge(inner[...])
    exchange(partial, send, recv, outer, INNER, group, OUTER, outer_peer)
    o_ref[...] = merge(outer[...])


def reduce_small(x, merge, collective_id, name):
    return pl.pallas_call(
        functools.partial(reduce_kernel, merge),
        in_specs=[VMEM_SPEC],
        out_specs=VMEM_SPEC,
        out_shape=jax.ShapeDtypeStruct((CAP, LANES), F32),
        scratch_shapes=[
            pltpu.VMEM((INNER, CAP, LANES), F32),
            pltpu.VMEM((OUTER, CAP, LANES), F32),
            pltpu.VMEM((CAP, LANES), F32),
            pltpu.SemaphoreType.DMA((INNER + OUTER,)),
            pltpu.SemaphoreType.DMA((INNER + OUTER,)),
        ],
        compiler_params=pltpu.CompilerParams(collective_id=collective_id, has_side_effects=True),
        name=name,
    )(x)


def split(x):
    high = x.astype(BF16)
    return high, (x - high.astype(F32)).astype(BF16)


def dot3(a, b, lhs_dim, rhs_dim):
    dims = (((lhs_dim,), (rhs_dim,)), ((), ()))
    dot = functools.partial(lax.dot_general, dimension_numbers=dims, preferred_element_type=F32)
    return dot(a[0], b[0]) + dot(a[1], b[0]) + dot(a[0], b[1])


ERF_P = 0.3275911 * 0.7071067811865476
ERF_A = [0.5 * c for c in (1.061405429, -1.453152027, 1.421413741, -0.284496736, 0.254829592)]


def gelu_parts(x):
    size = jnp.abs(x)
    t = pl.reciprocal(1.0 + ERF_P * size)
    e = jnp.exp(-0.5 * (x * x))
    poly = ERF_A[0]
    for c in ERF_A[1:]:
        poly = poly * t + c
    tail = poly * t * e
    cdf = jnp.where(x < 0.0, tail, 1.0 - tail)
    return x * cdf, cdf + x * (e * 0.3989422804014327)


BLOCK_ROWS = 512
BLOCKS = ROWS // BLOCK_ROWS


def tile_values(stat_row, member):
    return jnp.broadcast_to(
        jnp.sum(member * stat_row, axis=1, keepdims=True), (CAP, LANES)
    )


def norm_values(stat, member):
    n = stat[0:1]
    variance = stat[2:3] / n
    inv = lax.rsqrt(variance + NORM_EPSILON)
    sample = lax.broadcasted_iota(jnp.int32, (1, LANES), 1) < SAMPLES
    inv = jnp.where(sample, inv, 0.0)
    return tile_values(stat[1:2], member), tile_values(inv, member)


def by_tile(x):
    return x.reshape(-1, CAP, LANES)


def dense_kernel(
    stat_ref, member_ref, conv_ref, tiles_ref, grad_ref, mask_ref,
    gain_ref, nbias_ref, win_ref, bin_ref, wout_ref, bout_ref,
    out_ref, gscaled_ref, dwin_ref, dwout_ref, vec_ref, hvec_ref, sums_ref,
    win_hi, win_lo, wout_hi, wout_lo,
):
    step = pl.program_id(0)

    @pl.when(step == 0)
    def _():
        win_hi[...], win_lo[...] = split(win_ref[...])
        wout_hi[...], wout_lo[...] = split(wout_ref[...])
        dwin_ref[...] = jnp.zeros_like(dwin_ref)
        dwout_ref[...] = jnp.zeros_like(dwout_ref)
        vec_ref[...] = jnp.zeros_like(vec_ref)
        hvec_ref[...] = jnp.zeros_like(hvec_ref)
        sums_ref[...] = jnp.zeros_like(sums_ref)

    win = (win_hi[...], win_lo[...])
    wout = (wout_hi[...], wout_lo[...])
    mean, inv = norm_values(stat_ref[...], member_ref[...])
    mask = mask_ref[...]
    normed = [(by_tile(conv_ref[g]) - mean[None]) * inv[None] for g in range(GROUPS)]
    flat = lambda parts: jnp.concatenate([p.reshape(-1, LANES) for p in parts], axis=1)
    scaled = split(
        flat([normed[g] * gain_ref[g][None, None] + nbias_ref[g][None, None] for g in range(GROUPS)])
    )
    pre = dot3(scaled, win, 1, 0) + bin_ref[...]
    hidden, slope = gelu_parts(pre)
    hidden = split(hidden)
    update = dot3(hidden, wout, 1, 0) + bout_ref[...]
    g_update = [by_tile(grad_ref[g]) * mask for g in range(GROUPS)]
    for g in range(GROUPS):
        out = mask * (by_tile(tiles_ref[g]) + by_tile(update[:, g * LANES : (g + 1) * LANES]))
        out_ref[g] = out.reshape(-1, LANES)
    g_flat = flat(g_update)
    g_split = split(g_flat)
    g_pre = dot3(g_split, wout, 1, 1) * slope
    hvec_ref[...] += jnp.sum(g_pre, axis=0, keepdims=True)
    g_pre = split(g_pre)
    dwout_ref[...] += dot3(g_split, hidden, 0, 0)
    dwin_ref[...] += dot3(scaled, g_pre, 0, 0)
    g_scaled = dot3(g_pre, win, 1, 1)
    first = jnp.zeros((CAP, LANES), F32)
    second = jnp.zeros((CAP, LANES), F32)
    rows = []
    for g in range(GROUPS):
        gs = by_tile(g_scaled[:, g * LANES : (g + 1) * LANES])
        gscaled_ref[g] = gs.reshape(-1, LANES)
        gain_sum = jnp.sum(gs * normed[g], axis=0)
        bias_sum = jnp.sum(gs, axis=0)
        first = first + bias_sum * gain_ref[g][None]
        second = second + gain_sum * gain_ref[g][None]
        rows.append((jnp.sum(g_update[g], axis=0), gain_sum, bias_sum))
    for g in range(GROUPS):
        for i in range(3):
            vec_ref[g, i] += rows[g][i]
    sums_ref[0] += first
    sums_ref[1] += second


def dense(stat, member, conv, tiles, grad, mask, gain, nbias, win, bin_, wout, bout):
    block = pl.BlockSpec((GROUPS, BLOCK_ROWS, LANES), lambda i: (0, i, 0))
    mask_block = pl.BlockSpec((BLOCK_ROWS // CAP, CAP, LANES), lambda i: (i, 0, 0))
    whole = lambda *shape: pl.BlockSpec(shape, lambda i: (0,) * len(shape))
    shape = lambda *dims: jax.ShapeDtypeStruct(dims, F32)
    return pl.pallas_call(
        dense_kernel,
        grid=(BLOCKS,),
        in_specs=[
            whole(CAP, LANES), whole(CAP, LANES), block, block, block, mask_block,
            whole(GROUPS, LANES), whole(GROUPS, LANES),
            whole(256, HIDDEN_PAD), whole(1, HIDDEN_PAD),
            whole(HIDDEN_PAD, 256), whole(1, 256),
        ],
        out_specs=(
            block, block, whole(256, HIDDEN_PAD), whole(256, HIDDEN_PAD),
            whole(GROUPS, 3, CAP, LANES), whole(1, HIDDEN_PAD), whole(2, CAP, LANES),
        ),
        out_shape=(
            shape(GROUPS, ROWS, LANES), shape(GROUPS, ROWS, LANES),
            shape(256, HIDDEN_PAD), shape(256, HIDDEN_PAD),
            shape(GROUPS, 3, CAP, LANES), shape(1, HIDDEN_PAD), shape(2, CAP, LANES),
        ),
        scratch_shapes=[
            pltpu.VMEM((256, HIDDEN_PAD), BF16), pltpu.VMEM((256, HIDDEN_PAD), BF16),
            pltpu.VMEM((HIDDEN_PAD, 256), BF16), pltpu.VMEM((HIDDEN_PAD, 256), BF16),
        ],
        compiler_params=params(),
        name="dense",
    )(stat, member, conv, tiles, grad, mask, gain, nbias, win, bin_, wout, bout)


def back_kernel(
    near_ref, stat_ref, sum_ref, member_ref, conv_ref, gscaled_ref, padded_ref, mask_ref,
    gain_ref, w_ref,
    own_out, p0, p1, p2, p3, dw_ref, db_ref, gconv, gpad, pool, sems,
):
    member = member_ref[...]
    stat = stat_ref[...]
    mean, inv = norm_values(stat, member)
    sums = sum_ref[...]
    sample = lax.broadcasted_iota(jnp.int32, (1, LANES), 1) < SAMPLES
    share = jnp.where(sample, 1.0 / stat[0:1], 0.0)
    first = tile_values(sums[0:1] * share, member)
    second = tile_values(sums[1:2] * share, member)
    for g in range(GROUPS):
        gain = gain_ref[g][None, None]

        def gradient(r, acc):
            rows = pl.ds(r * SIDE * CAP, SIDE * CAP)
            normed = (by_tile(conv_ref[g, rows, :]) - mean[None]) * inv[None]
            g_normed = by_tile(gscaled_ref[g, rows, :]) * gain
            value = (mask_ref[pl.ds(r * SIDE, SIDE)] * inv[None]) * (
                g_normed - first[None] - normed * second[None]
            )
            gconv[g, rows, :] = value.reshape(-1, LANES)
            return acc + jnp.sum(value, axis=0)

        db_ref[g] = lax.fori_loop(0, SIDE, gradient, jnp.zeros((CAP, LANES), F32)) * lane_mask(g)

        def input_row(r, carry):
            low = jnp.maximum(r - (SIDE - 1), 0)
            high = jnp.minimum(r, KSIZE - 1)

            def tap(a, acc):
                x = by_tile(gconv[g, pl.ds((r - a) * SIDE * CAP, SIDE * CAP), :])
                for b in range(KSIZE):
                    part = w_ref[g, a * KSIZE + b][None] * x
                    acc = acc[:b] + tuple(
                        acc[b + i] + part[i] for i in range(SIDE)
                    ) + acc[b + SIDE :]
                return acc

            acc = lax.fori_loop(
                low, high + 1, tap, tuple(jnp.zeros((CAP, LANES), F32) for _ in range(PAD))
            )
            for i in range(PAD):
                gpad[g, pl.ds((r * PAD + i) * CAP, CAP), :] = acc[i]
            return carry

        lax.fori_loop(0, PAD, input_row, 0)

        def zero(i, carry):
            pool[g, pl.ds(i * RIM_ROWS, RIM_ROWS), :] = jnp.zeros((RIM_ROWS, LANES), F32)
            return carry

        lax.fori_loop(0, 6, zero, 0)

    def scatter(t, carry):
        for k in range(8):
            q = near_ref[t, k]
            for src, src_step, dst, dst_step, length in RUNS[k]:
                for g in range(GROUPS):
                    place = pl.ds(q + dst * CAP, length, stride=dst_step * CAP)
                    pool[g, place, :] = (
                        pool[g, place, :]
                        + gpad[g, pl.ds(src * CAP + t, length, stride=src_step * CAP), :]
                    )
        return carry

    lax.fori_loop(0, CAP, scatter, 0)
    targets = [p0, p1, None, p2, p3]
    copies = [
        pltpu.make_async_copy(
            pool.at[:, pl.ds(i * RIM_ROWS, RIM_ROWS), :], target, sems.at[i]
        )
        for i, target in enumerate(targets)
        if target is not None
    ]
    for copy in copies:
        copy.start()
    for g in range(GROUPS):
        for r in range(SIDE):
            own_out[g, pl.ds(r * SIDE * CAP, SIDE * CAP), :] = gpad[
                g, pl.ds(((r + RIM) * PAD + RIM) * CAP, SIDE * CAP), :
            ]
    add_rims(own_out, [lambda g, rows: pool[g, pl.ds(2 * RIM_ROWS + rows.start, rows.size), :]])

    for g in range(GROUPS):

        def weight_row(a, carry):
            def one(r, acc):
                x = by_tile(padded_ref[g, pl.ds((r + a) * PAD * CAP, PAD * CAP), :])
                y = by_tile(gconv[g, pl.ds(r * SIDE * CAP, SIDE * CAP), :])
                return tuple(
                    acc[b] + jnp.sum(x[b : b + SIDE] * y, axis=0) for b in range(KSIZE)
                )

            acc = lax.fori_loop(
                0, SIDE, one, tuple(jnp.zeros((CAP, LANES), F32) for _ in range(KSIZE))
            )
            for b in range(KSIZE):
                dw_ref[g, a * KSIZE + b] = acc[b]
            return carry

        lax.fori_loop(0, KSIZE, weight_row, 0)
    for copy in copies:
        copy.wait()


def add_rims(own, sources):
    for g in range(GROUPS):
        spans = [(0, 0, 48), (13 * SIDE, 48, 48)]
        for r in range(RIM, SIDE - RIM):
            spans += [(r * SIDE + c, rim_index(r, c), RIM) for c in (0, SIDE - RIM)]
        for first, rim, cells in spans:
            rows = pl.ds(first * CAP, cells * CAP)
            value = own[g, rows, :]
            for source in sources:
                value = value + source(g, pl.ds(rim * CAP, cells * CAP))
            own[g, rows, :] = value


def conv_backward(near, stat, sums, member, conv, gscaled, padded, mask, gain, w):
    shape = lambda *dims: jax.ShapeDtypeStruct(dims, F32)
    rim = shape(GROUPS, RIM_ROWS, LANES)
    return pl.pallas_call(
        back_kernel,
        in_specs=[SMEM_SPEC] + [VMEM_SPEC] * 9,
        out_specs=(VMEM_SPEC,) + (ANY_SPEC,) * 4 + (VMEM_SPEC,) * 2,
        out_shape=(
            shape(GROUPS, ROWS, LANES), rim, rim, rim, rim,
            shape(GROUPS, KSIZE * KSIZE, CAP, LANES), shape(GROUPS, CAP, LANES),
        ),
        scratch_shapes=[
            pltpu.VMEM((GROUPS, ROWS, LANES), F32),
            pltpu.VMEM((GROUPS, PAD * PAD * CAP, LANES), F32),
            pltpu.VMEM((GROUPS, 6 * RIM_ROWS, LANES), F32),
            pltpu.SemaphoreType.DMA((5,)),
        ],
        compiler_params=params(),
        name="conv_backward",
    )(near, stat, sums, member, conv, gscaled, padded, mask, gain, w)


def final_kernel(own_ref, grad_ref, mask_ref, r0, r1, r2, r3, o_ref, total):
    t = pl.program_id(0)

    @pl.when(t == 0)
    def _():
        for g in range(GROUPS):

            def add(r, carry):
                rows = pl.ds(r * SIDE * CAP, SIDE * CAP)
                value = by_tile(grad_ref[g, rows, :]) * mask_ref[pl.ds(r * SIDE, SIDE)]
                total[g, rows, :] = own_ref[g, rows, :] + value.reshape(-1, LANES)
                return carry

            lax.fori_loop(0, SIDE, add, 0)
        add_rims(total, [lambda g, rows, ref=ref: ref[g, rows, :] for ref in (r0, r1, r2, r3)])

    for g in range(GROUPS):
        o_ref[0, g * LANES : (g + 1) * LANES, :] = total[g, pl.ds(t, CELLS, stride=CAP), :].T


def final(own, grad, mask, returned):
    return pl.pallas_call(
        final_kernel,
        grid=(CAP,),
        in_specs=[VMEM_SPEC] * 7,
        out_specs=pl.BlockSpec((1, 2 * LANES, CELLS), lambda t: (t, 0, 0)),
        out_shape=jax.ShapeDtypeStruct((CAP, 250, CELLS), F32),
        scratch_shapes=[pltpu.VMEM((GROUPS, ROWS, LANES), F32)],
        compiler_params=params(),
        name="final",
    )(own, grad, mask, *returned)


def passed_along(block, axis, distance):
    devices = range(lax.axis_size(axis))
    route = [(i - distance, i) for i in devices if i - distance in devices]
    return lax.ppermute(block, axis, route)


def lane_groups(x):
    x = jnp.pad(x, [(0, 0)] * (x.ndim - 1) + [(0, 6)])
    x = x.reshape(x.shape[:-1] + (GROUPS, LANES))
    return jnp.moveaxis(x, -2, 0)


def from_groups(x):
    x = jnp.moveaxis(x, 0, -2)
    return x.reshape(x.shape[:-2] + (GROUPS * LANES,))[..., :250]


def prepare(device, tile_counts, ocean_mask, neighbours, sample_ids):
    slot = lax.iota(jnp.int32, CAP)
    filled = (slot < tile_counts[0]).astype(F32)
    oceanic = ocean_mask.astype(F32) * filled[:, None]
    mask = jnp.broadcast_to(oceanic.T[:, :, None], (CELLS, CAP, LANES))
    lane = lax.iota(jnp.int32, LANES)
    member = (sample_ids[:, None] == lane[None, :]).astype(F32)
    source = neighbours // CAP - device + REACH
    place = source * RIM_ROWS + neighbours % CAP
    near = jnp.where(neighbours >= 0, place, 5 * RIM_ROWS)
    return mask, member, near


OFFSETS = [-2, -1, 1, 2]


def local(
    tiles_in, conv_weight, conv_bias, norm_gain, norm_bias, weight_in, bias_in,
    weight_out, bias_out, grad_out, tile_counts, ocean_mask, neighbours, sample_ids,
):
    device = lax.axis_index("tiles")
    mask, member, near = prepare(device, tile_counts, ocean_mask, neighbours, sample_ids)
    w = jnp.broadcast_to(
        lane_groups(conv_weight.T)[:, :, None, :], (GROUPS, KSIZE * KSIZE, CAP, LANES)
    )
    b = jnp.broadcast_to(lane_groups(conv_bias)[:, None, :], (GROUPS, CAP, LANES))
    gain, nbias = lane_groups(norm_gain), lane_groups(norm_bias)
    win = jnp.pad(weight_in, ((0, 6), (0, 24)))
    wout = jnp.pad(weight_out, ((0, 24), (0, 6)))
    bin_ = jnp.pad(bias_in, (0, 24))[None]
    bout = jnp.pad(bias_out, (0, 6))[None]

    tiles, rim = to_rows(tiles_in, True)
    received = [passed_along(rim, "tiles", -offset) for offset in OFFSETS]
    grad = to_rows(grad_out, False)
    padded, conv, stat = conv_forward(near, tiles, rim, received, w, b, mask, member)
    stat = reduce_small(stat, merge_stats, 1, "reduce_stats")
    out, gscaled, dwin, dwout, vec, hvec, sums = dense(
        stat, member, conv, tiles, grad, mask, gain, nbias, win, bin_, wout, bout
    )
    tile_sums = jnp.sum(sums, axis=2)
    sample_sums = jnp.pad(jnp.dot(tile_sums, member, precision="highest"), ((0, 6), (0, 0)))
    sample_sums = reduce_small(sample_sums, merge_sums, 2, "reduce_sums")
    dwin, dwout, vec, hvec = lax.psum((dwin, dwout, jnp.sum(vec, axis=2), hvec), "tiles")
    own, p0, p1, p2, p3, dw, db = conv_backward(
        near, stat, sample_sums, member, conv, gscaled, padded, mask, gain, w
    )
    returned = [
        passed_along(block, "tiles", offset) for block, offset in zip((p0, p1, p2, p3), OFFSETS)
    ]
    output = from_rows(out)
    dw, db = lax.psum((jnp.sum(dw, axis=2), jnp.sum(db, axis=1)), "tiles")
    grad_tiles = final(own, grad, mask, returned)
    active = jnp.sum(jnp.where(lax.iota(jnp.int32, LANES) < SAMPLES, stat[0], 0.0)) / 250.0
    share = 1.0 / active
    vec = from_groups(vec) * share
    return (
        output,
        grad_tiles,
        from_groups(dw).T * share,
        from_groups(db) * share,
        vec[1],
        vec[2],
        dwin[:250, :1000] * share,
        hvec[0, :1000] * share,
        dwout[:250, :1000].T * share,
        vec[0],
    )


def solution(mesh):
    tiles = P("tiles")
    whole = P()
    return jax.shard_map(
        local,
        mesh=mesh,
        in_specs=(tiles,) + (whole,) * 8 + (tiles,) * 5,
        out_specs=(tiles, tiles) + (whole,) * 8,
        check_vma=False,
    )
```

time: 969 us -> 399 us (0.41)
  other arithmetic: 241 us -> 8.52 us
  blocking collectives: 301 us -> 100 us
  Pallas kernels: 0 us -> 144 us
  matrix products: 118 us -> 0.19 us
  local copies, waits for them, and re-layouts: 142 us -> 26.9 us
  waiting for transfers between devices: 114 us -> 77.1 us
    psum x4 -> x1, blocking collectives: 301 us -> 100 us  [local(): dw, db = lax.psum((jnp.sum(dw, axis=2), jnp.sum(db, axis=1)), 'tiles')]
    pallas_call x0 -> x9, Pallas kernels: none -> 144 us  [the longest x2 35.9 us: reduce_small(): pl.pallas_call(functools.partial(reduce_kernel, merge), in_specs=[VMEM_SP...]
    dot_general x16 -> x1, matrix products: 118 us -> 0.19 us  [local(): jnp.dot(tile_sums, member, precision='highest')]
    add_any x5 -> x0, other arithmetic: 113 us -> none  [the longest x2 85.9 us: depthwise(): flat_tiles[:, :, anchor:anchor + out_span]]
    mul x6, other arithmetic: 51.3 us -> 3.28 us  [the longest x1 1.38 us: local(): dwin[:250, :1000] * share]
    add x2 -> x0, other arithmetic: 30.4 us -> none  [the longest x1 23.4 us: depthwise(): running + conv_weight[:, row_step * KSIZE + col_step][None, :, None] * fl...]
    gather x2 -> x0, local copies, waits for them, and re-layouts: 29.4 us -> none  [local(): gathered[position] * is_valid.astype(jnp.float32)[:, :, None, None]]
    reduce_sum x9 -> x5, other arithmetic: 33.2 us -> 3.9 us  [the longest x2 1.81 us: local(): dw, db = lax.psum((jnp.sum(dw, axis=2), jnp.sum(db, axis=1)), 'tiles')]
  transfers between devices with their start and end apart: 9 -> 9, of which waited for: 4 -> 4; matrix products, arithmetic and copies ran while one was open for 6% -> 5% of each run, Pallas kernels for 0% -> 3%
where the time goes in v1:
time: 399 us; the launch traced here: 398 us
  Pallas kernels  144 us (36%)
  blocking collectives  100 us (25%)
  waiting for transfers between devices  77.1 us (19%)
  local copies, waits for them, and re-layouts  26.9 us (7%)
  starting transfers between devices  25.4 us (6%)
  between operations  15.7 us (4%)
  other arithmetic  8.52 us (2%)
    psum x1, blocking collectives, local(): dw, db = lax.psum((jnp.sum(dw, axis=2), jnp.sum(db, axis=1)), 'tiles')  100 us
    psum x1, waiting for transfers between devices, local(): lax.psum((dwin, dwout, jnp.sum(vec, axis=2), hvec), 'tiles')  55.6 us
    pallas_call x2, Pallas kernels, reduce_small(): pl.pallas_call(functools.partial(reduce_kernel, merge), in_specs=[VMEM_SP...  35.9 us
    pallas_call x1, Pallas kernels, dense(): pl.pallas_call(dense_kernel, grid=(BLOCKS,), in_specs=[whole(CAP, LANES),...  35.9 us
    pallas_call x1, Pallas kernels, conv_backward(): pl.pallas_call(back_kernel, in_specs=[SMEM_SPEC] + [VMEM_SPEC] * 9, out_s...  27.1 us
    ppermute x8, starting transfers between devices, passed_along(): return lax.ppermute(block, axis, route)  25.4 us
    ppermute x8, waiting for transfers between devices, passed_along(): return lax.ppermute(block, axis, route)  21.4 us
    unnamed x41, local copies, waits for them, and re-layouts  19 us
  transfers between devices with their start and end apart: 9, of which 4 were waited for; matrix products, arithmetic and copies ran while one was open for 5% of the time, Pallas kernels for 3%

profile of v1, /device:TPU:1, one launch (start us, length us, event | category | flops | bytes accessed | tf_op | source)
XLA Modules:
  0.0 397.7 jit_solution(13396970322063576926)
XLA Ops:
  7.2 3.6 copy.42.x_ref
  10.8 6.4 %to_rows.2 = (f32[2,2048,128]{2,1,0:T(8,128)}, f32[2,1248,128]{2,1,0:T(8,128)}) custom-call(f32[8,250,256]{2,1,0:T(8,128)} %copy.42.x_ref), custom_call_target="tpu_custom_call" | custom-call | bytes 5242880 | tf_op jit(solution)/shard_map/to_rows/pallas_call | solution.py:128
  17.2 1.3 collective-permute-start.3
  18.5 3.3 collective-permute-start.2
  21.9 4.2 %collective-permute-start.1 = (f32[2,1248,128]{2,1,0:T(8,128)}, f32[2,1248,128]{2,1,0:T(8,128)}, u32[]{:S(2)}, u32[]{:S(2)}) collective-permute-start(f32[2,1248,128]{2,1,0:T(8,128)} %get-tuple-element.30.rim_ref), channel_id=1, source_target_pairs={{0,1},{1,2},{2,3},{3,4},{4,5},{5,6},{6,7},{7,8},{8,9},{9,10},{10,1... | collective-permute-start | bytes 3833864 | tf_op jit(solution)/shard_map/ppermute | solution.py:666
  26.1 4.7 %collective-permute-start = (f32[2,1248,128]{2,1,0:T(8,128)}, f32[2,1248,128]{2,1,0:T(8,128)}, u32[]{:S(2)}, u32[]{:S(2)}) collective-permute-start(f32[2,1248,128]{2,1,0:T(8,128)} %get-tuple-element.30.rim_ref), channel_id=1, source_target_pairs={{0,2},{1,3},{2,4},{3,5},{4,6},{5,7},{6,8},{7,9},{8,10},{9,11},{10,... | collective-permute-start | bytes 3833864 | tf_op jit(solution)/shard_map/ppermute | solution.py:666
  32.0 0.6 pad.38
  32.9 1.6 copy.46
  34.6 1.1 pad.37.win_ref
  35.6 1.0 pad.39.wout_ref
  36.7 1.9 copy.45.x_ref
  38.6 6.1 %to_rows.3.grad_ref = f32[2,2048,128]{2,1,0:T(8,128)} custom-call(f32[8,250,256]{2,1,0:T(8,128)} %copy.45.x_ref), custom_call_target="tpu_custom_call" | custom-call | bytes 5242880 | tf_op jit(solution)/shard_map/to_rows/pallas_call | solution.py:128
  44.7 0.6 pad_bitcast_fusion
  45.3 0.7 fusion.8.member_ref
  46.0 0.6 fusion.6.near_ref
  46.6 3.0 collective-permute-done.3.r3
  49.6 14.4 %collective-permute-done.2.r2 = f32[2,1248,128]{2,1,0:T(8,128)} collective-permute-done((f32[2,1248,128]{2,1,0:T(8,128)}, f32[2,1248,128]{2,1,0:T(8,128)}, u32[]{:S(2)}, u32[]{:S(2)}) %collective-permute-start.2) | collective-permute-done | bytes 1277984 | tf_op jit(solution)/shard_map/ppermute | solution.py:666
  64.0 4.0 %collective-permute-done.r0 = f32[2,1248,128]{2,1,0:T(8,128)} collective-permute-done((f32[2,1248,128]{2,1,0:T(8,128)}, f32[2,1248,128]{2,1,0:T(8,128)}, u32[]{:S(2)}, u32[]{:S(2)}) %collective-permute-start) | collective-permute-done | bytes 1277984 | tf_op jit(solution)/shard_map/ppermute | solution.py:666
  68.0 0.6 broadcast_in_dim.39.b_ref
  68.6 0.8 broadcast_in_dim.37.w_ref
  69.3 1.3 broadcast_in_dim.40.mask_ref
  70.6 18.8 %conv_forward.1 = (f32[2,3872,128]{2,1,0:T(8,128)}, f32[2,2048,128]{2,1,0:T(8,128)}, f32[8,128]{1,0:T(8,128)}) custom-call(s32[8,8]{1,0:T(8,128)} %fusion.6.near_ref, f32[2,2048,128]{2,1,0:T(8,128)} %get-tuple-element.29.own_ref.tiles_ref, f32[2,1248,128]{2,1,0:T(8,128)} %get-tuple-element.30.rim_ref, f32[2,1248,128]{2,1,0:T(8,128)} %collective-permute-done.r0, ...), custom_call_target="tpu_custom_call" | custom-call | tf_op jit(solution)/shard_map/conv_forward/pallas_call | solution.py:249
  89.4 21.7 %reduce_stats.1.stat_ref = f32[8,128]{1,0:T(8,128)} custom-call(f32[8,128]{1,0:T(8,128)} %get-tuple-element.31.x_ref), custom_call_target="tpu_custom_call" | custom-call | tf_op jit(solution)/shard_map/reduce_stats/pallas_call | solution.py:327
  111.1 1.3 fusion.14
  112.4 35.9 %dense.1 = (f32[2,2048,128]{2,1,0:T(8,128)}, f32[2,2048,128]{2,1,0:T(8,128)}, f32[256,1024]{1,0:T(8,128)}, f32[256,1024]{1,0:T(8,128)}, f32[2,3,8,128]{3,2,1,0:T...) custom-call(f32[8,128]{1,0:T(8,128)} %reduce_stats.1.stat_ref, f32[8,128]{1,0:T(8,128)} %fusion.8.member_ref, ...), custom_call_target="tpu_custom_call" | custom-call | tf_op jit(solution)/shard_map/dense/pallas_call | solution.py:460
  148.3 0.8 reduce_sum.45
  149.3 0.6 pad.41.x_ref
  149.9 14.2 %reduce_sums.1.sum_ref = f32[8,128]{1,0:T(8,128)} custom-call(f32[8,128]{1,0:T(8,128)} %pad.41.x_ref), custom_call_target="tpu_custom_call" | custom-call | tf_op jit(solution)/shard_map/reduce_sums/pallas_call | solution.py:327
  164.1 27.1 %conv_backward.1 = (f32[2,2048,128]{2,1,0:T(8,128)}, f32[2,1248,128]{2,1,0:T(8,128)}, f32[2,1248,128]{2,1,0:T(8,128)}, f32[2,1248,128]{2,1,0:T(8,128)}, f32[2,12...) custom-call(s32[8,8]{1,0:T(8,128)} %fusion.6.near_ref, f32[8,128]{1,0:T(8,128)} %reduce_stats.1.stat_ref, ...), custom_call_target="tpu_custom_call" | custom-call | tf_op jit(solution)/shard_map/conv_backward/pallas_call | solution.py:611
  191.3 0.7 reduce_sum.48
  192.0 1.1 reduce_sum.46
  193.2 1.3 collective-permute-start.4
  194.5 3.2 collective-permute-start.5
  197.7 4.2 %collective-permute-start.6 = (f32[2,1248,128]{2,1,0:T(8,128)}, f32[2,1248,128]{2,1,0:T(8,128)}, u32[]{:S(2)}, u32[]{:S(2)}) collective-permute-start(f32[2,1248,128]{2,1,0:T(8,128)} %get-tuple-element.40), channel_id=1, source_target_pairs={{0,1},{1,2},{2,3},{3,4},{4,5},{5,6},{6,7},{7,8},{8,9},{9,10},{10,1... | collective-permute-start | bytes 3833864 | tf_op jit(solution)/shard_map/ppermute | solution.py:666
  201.9 3.3 collective-permute-start.7
  205.9 100.3 %all-reduce.9 = (f32[49,256]{1,0:T(8,128)S(1)}, f32[256]{0:T(256)S(1)}, f32[3,256]{1,0:T(4,128)S(1)}, f32[1,1024]{1,0:T(1,128)S(1)}) all-reduce(f32[49,256]{1,0:T(8,128)S(1)} %bitcast.36, f32[256]{0:T(256)S(1)} %bitcast.42, f32[3,256]{1,0:T(4,128)S(1)} %bitcast.41, f32[1,1024]{1,0:T(1,128)S(1)} %copy-done.8), channel_id=1, replica_groups=mesh['tiles'=128] {'tiles'}, use_global_device_ids=true, to_apply=%region_2.3 | all-reduce | flops 14592 | bytes 116736 | tf_op jit(solution)/shard_map/psum | solution.py:731
  306.8 5.1 %from_rows.1 = f32[8,250,256]{2,1,0:T(8,128)} custom-call(f32[2,2048,128]{2,1,0:T(8,128)} %get-tuple-element.33.x_ref), custom_call_target="tpu_custom_call" | custom-call | bytes 5242880 | tf_op jit(solution)/shard_map/from_rows/pallas_call | solution.py:147
  311.9 4.1 %copy.48 = f32[8,250,256]{2,0,1:T(8,128)} copy(f32[8,250,256]{2,1,0:T(8,128)} %from_rows.1) | data formatting | bytes 4096000
  316.0 0.6 fusion.15
  316.5 0.6 slice_multiply_fusion.3
  317.1 0.6 fusion.1
  317.8 55.6 %all-reduce.13.cloned.1.call-done = (f32[256,1024]{1,0:T(8,128)}, f32[256,1024]{1,0:T(8,128)}) async-done(((f32[256,1024]{1,0:T(8,128)}, f32[256,1024]{1,0:T(8,128)}), (f32[256,1024]{1,0:T(8,128)}, f32[256,1024]{1,0:T(8,128)})) %all-reduce.13.cloned.1.call-update) | async-done | bytes 2097168 | tf_op jit(solution)/shard_map/psum | solution.py:723
  373.4 1.4 slice_multiply_fusion.1
  374.8 1.3 copy.50
  376.2 1.3 copy.51
  377.5 1.0 copy-done.1
  378.5 8.2 %final.1 = f32[8,250,256]{2,1,0:T(8,128)} custom-call(f32[2,2048,128]{2,1,0:T(8,128)} %get-tuple-element.37.own_ref, f32[2,2048,128]{2,1,0:T(8,128)} %to_rows.3.grad_ref, f32[256,8,128]{2,1,0:T(8,128)} %broadcast_in_dim.40.mask_ref, f32[2,1248,128]{2,1,0:T(8,128)} %copy-done.1, f32[2,1248,128]{2,1,0:T(8,128)} %collective-permute-done.5.r1, ...), custom_call_target="tpu_custom_call" | custom-call | tf_op jit(solution)/shard_map/final/pallas_call | solution.py:651
  386.8 4.1 %copy.49 = f32[8,250,256]{2,0,1:T(8,128)} copy(f32[8,250,256]{2,1,0:T(8,128)} %final.1) | data formatting | bytes 4096000
  (54 shorter events, 1.9 us)
Async XLA Ops:
  7.2 366.2 %all-reduce.13.cloned.1.call-start = ((), (), s32[]{:S(2)}) async-start(), calls=%async_computation | async-start | bytes 4194304 | tf_op jit(solution)/shard_map/psum | solution.py:723
  10.8 20.6 %copy-start.11 = (f32[250]{0:T(256)S(1)}, f32[250]{0:T(256)}, u32[]{:S(2)}) copy-start(f32[250]{0:T(256)} %param.22) | copy-start | bytes 3004
  10.8 21.2 %copy-start.9 = (f32[1000]{0:T(1024)S(1)}, f32[1000]{0:T(1024)}, u32[]{:S(2)}) copy-start(f32[1000]{0:T(1024)} %param.20) | copy-start | bytes 12004
  10.8 21.8 %copy-start.5 = (f32[250,49]{0,1:T(8,128)S(1)}, f32[250,49]{0,1:T(8,128)}, u32[]{:S(2)}) copy-start(f32[250,49]{0,1:T(8,128)} %param.15) | copy-start | bytes 147004
  10.8 21.9 %copy-start.7 = (s32[8,256]{1,0:T(8,128)S(1)}, s32[8,256]{1,0:T(8,128)}, u32[]{:S(2)}) copy-start(s32[8,256]{1,0:T(8,128)} %param.25) | copy-start | bytes 24580
  17.2 32.3 %collective-permute-start.3 = (f32[2,1248,128]{2,1,0:T(8,128)}, f32[2,1248,128]{2,1,0:T(8,128)S(1)}, u32[]{:S(2)}, u32[]{:S(2)}) collective-permute-start(f32[2,1248,128]{2,1,0:T(8,128)} %get-tuple-element.30.rim_ref), channel_id=1, source_target_pairs={{2,0},{3,1},{4,2},{5,3},{6,4},{7,5},{8,6},{9,7},{10,8},{11,9},{12,... | collective-permute-start | bytes 3833864 | tf_op jit(solution)/shard_map/ppermute | solution.py:666
  18.5 45.4 %collective-permute-start.2 = (f32[2,1248,128]{2,1,0:T(8,128)}, f32[2,1248,128]{2,1,0:T(8,128)}, u32[]{:S(2)}, u32[]{:S(2)}) collective-permute-start(f32[2,1248,128]{2,1,0:T(8,128)} %get-tuple-element.30.rim_ref), channel_id=1, source_target_pairs={{1,0},{2,1},{3,2},{4,3},{5,4},{6,5},{7,6},{8,7},{9,8},{10,9},{11,1... | collective-permute-start | bytes 3833864 | tf_op jit(solution)/shard_map/ppermute | solution.py:666
  21.9 42.1 %collective-permute-start.1 = (f32[2,1248,128]{2,1,0:T(8,128)}, f32[2,1248,128]{2,1,0:T(8,128)}, u32[]{:S(2)}, u32[]{:S(2)}) collective-permute-start(f32[2,1248,128]{2,1,0:T(8,128)} %get-tuple-element.30.rim_ref), channel_id=1, source_target_pairs={{0,1},{1,2},{2,3},{3,4},{4,5},{5,6},{6,7},{7,8},{8,9},{9,10},{10,1... | collective-permute-start | bytes 3833864 | tf_op jit(solution)/shard_map/ppermute | solution.py:666
  26.1 41.9 %collective-permute-start = (f32[2,1248,128]{2,1,0:T(8,128)}, f32[2,1248,128]{2,1,0:T(8,128)}, u32[]{:S(2)}, u32[]{:S(2)}) collective-permute-start(f32[2,1248,128]{2,1,0:T(8,128)} %get-tuple-element.30.rim_ref), channel_id=1, source_target_pairs={{0,2},{1,3},{2,4},{3,5},{4,6},{5,7},{6,8},{7,9},{8,10},{9,11},{10,... | collective-permute-start | bytes 3833864 | tf_op jit(solution)/shard_map/ppermute | solution.py:666
  32.9 2.7 copy-start.4
  34.6 2.1 copy-start
  38.6 6.1 %copy-start.12 = (f32[250]{0:T(256)S(1)}, f32[250]{0:T(256)}, u32[]{:S(2)}) copy-start(f32[250]{0:T(256)} %param.16) | copy-start | bytes 3004
  38.6 6.1 %copy-start.13 = (f32[250]{0:T(256)S(1)}, f32[250]{0:T(256)}, u32[]{:S(2)}) copy-start(f32[250]{0:T(256)} %param.18) | copy-start | bytes 3004
  38.6 6.1 %copy-start.14 = (f32[250]{0:T(256)S(1)}, f32[250]{0:T(256)}, u32[]{:S(2)}) copy-start(f32[250]{0:T(256)} %param.17) | copy-start | bytes 3004
  38.6 6.7 %copy-start.15 = (s32[8]{0:T(128)S(1)}, s32[8]{0:T(128)}, u32[]{:S(2)}) copy-start(s32[8]{0:T(128)} %param.27) | copy-start | bytes 100
  38.6 7.3 %copy-start.10 = (s32[8,8]{1,0:T(8,128)S(1)}, s32[8,8]{1,0:T(8,128)}, u32[]{:S(2)}) copy-start(s32[8,8]{1,0:T(8,128)} %param.26) | copy-start | bytes 772
  49.6 21.1 %copy-start.2 = (f32[2,1248,128]{2,1,0:T(8,128)}, f32[2,1248,128]{2,1,0:T(8,128)S(1)}, u32[]{:S(2)}) copy-start(f32[2,1248,128]{2,1,0:T(8,128)S(1)} %collective-permute-done.3.r3) | copy-start | bytes 3833860
  164.1 27.9 %copy-start.6 = (f32[2,3,8,128]{3,2,1,0:T(8,128)S(1)}, f32[2,3,8,128]{3,2,1,0:T(8,128)}, u32[]{:S(2)}) copy-start(f32[2,3,8,128]{3,2,1,0:T(8,128)} %get-tuple-element.44) | copy-start | bytes 73732
  191.3 14.6 %copy-start.8 = (f32[1,1024]{1,0:T(1,128)S(1)}, f32[1,1024]{1,0:T(1,128)}, u32[]{:S(2)}) copy-start(f32[1,1024]{1,0:T(1,128)} %get-tuple-element.46) | copy-start | bytes 12292
  193.2 184.3 %collective-permute-start.4 = (f32[2,1248,128]{2,1,0:T(8,128)}, f32[2,1248,128]{2,1,0:T(8,128)S(1)}, u32[]{:S(2)}, u32[]{:S(2)}) collective-permute-start(f32[2,1248,128]{2,1,0:T(8,128)} %get-tuple-element.38), channel_id=1, source_target_pairs={{2,0},{3,1},{4,2},{5,3},{6,4},{7,5},{8,6},{9,7},{10,8},{11,9},{12,... | collective-permute-start | bytes 3833864 | tf_op jit(solution)/shard_map/ppermute | solution.py:666
  194.5 183.0 %collective-permute-start.5 = (f32[2,1248,128]{2,1,0:T(8,128)}, f32[2,1248,128]{2,1,0:T(8,128)}, u32[]{:S(2)}, u32[]{:S(2)}) collective-permute-start(f32[2,1248,128]{2,1,0:T(8,128)} %get-tuple-element.39), channel_id=1, source_target_pairs={{1,0},{2,1},{3,2},{4,3},{5,4},{6,5},{7,6},{8,7},{9,8},{10,9},{11,1... | collective-permute-start | bytes 3833864 | tf_op jit(solution)/shard_map/ppermute | solution.py:666
  197.7 179.8 %collective-permute-start.6 = (f32[2,1248,128]{2,1,0:T(8,128)}, f32[2,1248,128]{2,1,0:T(8,128)}, u32[]{:S(2)}, u32[]{:S(2)}) collective-permute-start(f32[2,1248,128]{2,1,0:T(8,128)} %get-tuple-element.40), channel_id=1, source_target_pairs={{0,1},{1,2},{2,3},{3,4},{4,5},{5,6},{6,7},{7,8},{8,9},{9,10},{10,1... | collective-permute-start | bytes 3833864 | tf_op jit(solution)/shard_map/ppermute | solution.py:666
  201.9 175.6 %collective-permute-start.7 = (f32[2,1248,128]{2,1,0:T(8,128)}, f32[2,1248,128]{2,1,0:T(8,128)}, u32[]{:S(2)}, u32[]{:S(2)}) collective-permute-start(f32[2,1248,128]{2,1,0:T(8,128)} %get-tuple-element.41), channel_id=1, source_target_pairs={{0,2},{1,3},{2,4},{3,5},{4,6},{5,7},{6,8},{7,9},{8,10},{9,11},{10,... | collective-permute-start | bytes 3833864 | tf_op jit(solution)/shard_map/ppermute | solution.py:666
  373.4 2.7 copy-start.3
  377.5 1.0 copy-start.1
Sparse Core Ops, SparseCore 0:
  206.0 167.3 all-reduce.12

commit v2 on v1

v2 whole, which is shorter than its diff:
```python
import functools

import jax
import jax.numpy as jnp
from jax import lax
from jax.experimental import pallas as pl
from jax.experimental.pallas import tpu as pltpu
from jax.sharding import PartitionSpec as P

SIDE = 16
KSIZE = 7
RIM = 3
REACH = 2
SAMPLES = 5
CAP = 8
CELLS = SIDE * SIDE
PAD = SIDE + 2 * RIM
LANES = 128
GROUPS = 2
ROWS = CELLS * CAP
RIM_CELLS = 156
RIM_ROWS = RIM_CELLS * CAP
HIDDEN_PAD = 1024
NORM_EPSILON = 1e-05
F32 = jnp.float32
BF16 = jnp.bfloat16
MIB = 1 << 20
MESH = pl.DeviceIdType.MESH
VMEM_SPEC = pl.BlockSpec(memory_space=pltpu.VMEM)
SMEM_SPEC = pl.BlockSpec(memory_space=pltpu.SMEM)
ANY_SPEC = pl.BlockSpec(memory_space=pl.ANY)


def params(mib=56, **more):
    return pltpu.CompilerParams(vmem_limit_bytes=mib * MIB, **more)


HALF_RIM = RIM_ROWS // 2


def rim_spans(half):
    base = half * 78
    outer = 0 if half == 0 else SIDE - RIM
    inner = RIM if half == 0 else SIDE // 2
    spans = [(outer * SIDE, base, 48)]
    for i in range(5):
        spans.append(((inner + i) * SIDE, base + 48 + i * RIM, RIM))
        spans.append(((inner + i) * SIDE + SIDE - RIM, base + 63 + i * RIM, RIM))
    return spans


RIM_OF = {
    first + i: rim + i
    for half in range(2)
    for first, rim, cells in rim_spans(half)
    for i in range(cells)
}


def rim_index(r, c):
    return RIM_OF[r * SIDE + c]


def region_runs():
    spans = {-1: (0, SIDE - RIM, RIM), 0: (RIM, 0, SIDE), 1: (RIM + SIDE, 0, RIM)}
    order = [(-1, -1), (-1, 0), (-1, 1), (0, -1), (0, 1), (1, -1), (1, 0), (1, 1)]
    runs = []
    for dr, dc in order:
        dst_r, src_r, rows = spans[dr]
        dst_c, src_c, cols = spans[dc]
        found = []

        def add(cells):
            start = 0
            while start < len(cells):
                stop = start + 1
                while (
                    stop < len(cells)
                    and stop - start < 8
                    and cells[stop][0] - cells[stop - 1][0] == cells[1][0] - cells[0][0]
                    and cells[stop][1] - cells[stop - 1][1] == cells[1][1] - cells[0][1]
                ):
                    stop += 1
                step = (cells[1][0] - cells[0][0], cells[1][1] - cells[0][1])
                found.append((cells[start][0], step[0], cells[start][1], step[1], stop - start))
                start = stop

        if dr == 0:
            for j in range(cols):
                cells = [
                    ((dst_r + i) * PAD + dst_c + j, rim_index(src_r + i, src_c + j))
                    for i in range(rows)
                ]
                for low, high in ((0, RIM), (RIM, 8), (8, SIDE - RIM), (SIDE - RIM, SIDE)):
                    add(cells[low:high])
        else:
            for i in range(rows):
                add(
                    [
                        ((dst_r + i) * PAD + dst_c + j, rim_index(src_r + i, src_c + j))
                        for j in range(cols)
                    ]
                )
        runs.append(found)
    return runs


RUNS = region_runs()


ROLES = 6
PIECES = [(g, half) for half in range(2) for g in range(GROUPS)]


def piece(ref, role, p):
    g, half = PIECES[p]
    return ref.at[g, pl.ds(role * RIM_ROWS + half * HALF_RIM, HALF_RIM), :]


def halo_peers():
    me = lax.axis_index("tiles")
    total = lax.axis_size("tiles")
    sign = 2 * (me % 2) - 1
    ahead = (me + 2 * sign + total) % total
    behind = (me - 2 * sign + total) % total
    return ahead, behind, me - sign


def remote(src, dst, send, recv, peer):
    return pltpu.make_async_remote_copy(
        src_ref=src, dst_ref=dst, send_sem=send, recv_sem=recv,
        device_id=(peer,), device_id_type=MESH,
    )


def greet(peers):
    barrier = pltpu.get_barrier_semaphore()
    for peer in peers:
        pl.semaphore_signal(barrier, inc=1, device_id=(peer,), device_id_type=MESH)
    return lambda: pl.semaphore_wait(barrier, len(peers))


def load_native(x_ref, buf, sems, first=0):
    copies = []
    for g, half in PIECES:
        rows = 1024 if g == 0 else 976
        copies.append(
            pltpu.make_async_copy(
                x_ref.at[pl.ds(g * 1024, rows), pl.ds(half * LANES, LANES)],
                buf.at[half, pl.ds(g * 1024, rows), :],
                sems.at[first + len(copies)],
            )
        )
    return copies


def to_rows(buf, out, g, half):
    for t in range(CAP):
        block = buf[half, pl.ds(g * 1024 + t, LANES, stride=CAP), :]
        out[g, pl.ds(half * 1024 + t, LANES, stride=CAP), :] = block.T


def store_native(buf, out_ref, sems, first=0):
    copies = []
    for g, half in PIECES:
        rows = 1024 if g == 0 else 976
        copies.append(
            pltpu.make_async_copy(
                buf.at[half, pl.ds(g * 1024, rows), :],
                out_ref.at[pl.ds(g * 1024, rows), pl.ds(half * LANES, LANES)],
                sems.at[first + len(copies)],
            )
        )
    return copies


def from_rows(rows, buf, g, half):
    for t in range(CAP):
        block = rows[g, pl.ds(half * 1024 + t, LANES, stride=CAP), :]
        buf[half, pl.ds(g * 1024 + t, LANES, stride=CAP), :] = block.T


def lane_mask(g):
    lane = lax.broadcasted_iota(jnp.int32, (CAP, LANES), 1)
    return (lane < 250 - g * LANES).astype(F32)


def shape(*dims):
    return jax.ShapeDtypeStruct(dims, F32)


def buffer(*dims):
    return pltpu.VMEM(dims, F32)


def semaphores(count):
    return pltpu.SemaphoreType.DMA((count,))


INNER = 8
OUTER = 16


def inner_peers():
    me = lax.axis_index("tiles")
    group, place = me // INNER, me % INNER
    return [group * INNER + (place + j) % INNER for j in range(1, INNER)]


def outer_peers():
    me = lax.axis_index("tiles")
    group, place = me // INNER, me % INNER
    return [((group + j) % OUTER) * INNER + place for j in range(1, OUTER)]


def exchange(x, send, recv, slots, first, mine, peers):
    copies = [
        remote(x, slots.at[mine], send.at[first + j], recv.at[first + j], peer)
        for j, peer in enumerate(peers)
    ]
    for copy in copies:
        copy.start()
    slots[mine] = x[...]
    for copy in copies:
        copy.wait()


def reduce_vector(merge, partial, inner, outer, send, recv):
    me = lax.axis_index("tiles")
    exchange(partial, send, recv, inner, 0, me % INNER, inner_peers())
    partial[...] = merge(inner[...])
    exchange(partial, send, recv, outer, INNER, me // INNER, outer_peers())
    return merge(outer[...])


def merge_stats(parts):
    n = jnp.sum(parts[:, 0:1], axis=0)
    mean = jnp.sum(parts[:, 0:1] * parts[:, 1:2], axis=0) / jnp.maximum(n, 1.0)
    off = parts[:, 1:2] - mean[None]
    m2 = jnp.sum(parts[:, 2:3] + parts[:, 0:1] * off * off, axis=0)
    return stack_rows(n, mean, m2)


def stack_rows(*rows):
    row_id = lax.broadcasted_iota(jnp.int32, (CAP, LANES), 0)
    value = jnp.zeros((CAP, LANES), F32)
    for i, row in enumerate(rows):
        value = jnp.where(row_id == i, row, value)
    return value


def merge_sums(parts):
    return jnp.sum(parts, axis=0)


def by_tile(x):
    return x.reshape(-1, CAP, LANES)


def own_conv(g, padded, conv, w, lanes_ref):
    bias = jnp.broadcast_to(lanes_ref[g, 0:1, :], (CAP, LANES))[None]

    def row(r, carry):
        acc = jnp.broadcast_to(bias, (SIDE, CAP, LANES))
        for a in range(KSIZE):
            x = by_tile(padded[g, pl.ds((r + a) * PAD * CAP, PAD * CAP), :])
            for b in range(KSIZE):
                acc = acc + w[g, a * KSIZE + b][None] * x[b : b + SIDE]
        conv[g, pl.ds(r * SIDE * CAP, SIDE * CAP), :] = acc.reshape(-1, LANES)
        return carry

    lax.fori_loop(0, SIDE, row, 0)


def gather(near_ref, pool, padded):
    def fill(t, carry):
        for k in range(8):
            q = near_ref[t, k]
            for dst, dst_step, src, src_step, length in RUNS[k]:
                for g in range(GROUPS):
                    padded[g, pl.ds(dst * CAP + t, length, stride=dst_step * CAP), :] = pool[
                        g, pl.ds(q + src * CAP, length, stride=src_step * CAP), :
                    ]
        return carry

    lax.fori_loop(0, CAP, fill, 0)


def halo_conv(padded, conv, w):
    blank = jnp.zeros((RIM, CAP, LANES), F32)
    for g in range(GROUPS):
        for r in [0, 1, 2, 13, 14, 15]:
            rows = pl.ds(r * SIDE * CAP, SIDE * CAP)
            acc = by_tile(conv[g, rows, :])
            for a in range(KSIZE):
                if RIM <= r + a < RIM + SIDE:
                    continue
                x = by_tile(padded[g, pl.ds(((r + a) * PAD + RIM) * CAP, SIDE * CAP), :])
                x = jnp.concatenate([blank, x, blank], axis=0)
                for b in range(KSIZE):
                    acc = acc + w[g, a * KSIZE + b][None] * x[b : b + SIDE]
            conv[g, rows, :] = acc.reshape(-1, LANES)

        def columns(r, carry):
            left = [jnp.zeros((CAP, LANES), F32) for _ in range(RIM)]
            right = [jnp.zeros((CAP, LANES), F32) for _ in range(RIM)]
            for a in range(KSIZE):
                first = (r + a) * PAD * CAP
                xl = by_tile(padded[g, pl.ds(first, RIM * CAP), :])
                xr = by_tile(padded[g, pl.ds(first + (RIM + SIDE) * CAP, RIM * CAP), :])
                for c in range(RIM):
                    for b in range(RIM - c):
                        left[c] = left[c] + w[g, a * KSIZE + b] * xl[c + b]
                    for b in range(KSIZE - 1 - c, KSIZE):
                        right[c] = right[c] + w[g, a * KSIZE + b] * xr[c + b - KSIZE + 1]
            for c in range(RIM):
                cell = pl.ds((r * SIDE + c) * CAP, CAP)
                conv[g, cell, :] = conv[g, cell, :] + left[c]
                cell = pl.ds((r * SIDE + SIDE - RIM + c) * CAP, CAP)
                conv[g, cell, :] = conv[g, cell, :] + right[c]
            return carry

        lax.fori_loop(0, SIDE, columns, 0)


def local_stats(conv, mask, member):
    zero = jnp.zeros((CAP, LANES), F32)
    sums, cells = zero, zero
    for g in range(GROUPS):

        def add(r, carry):
            rows = pl.ds(r * SIDE * CAP, SIDE * CAP)
            m = by_tile(mask[rows, :])
            x = by_tile(conv[g, rows, :])
            return carry[0] + jnp.sum(x * m, axis=0), carry[1] + jnp.sum(m, axis=0)

        total, cells = lax.fori_loop(0, SIDE, add, (zero, zero))
        sums = sums + total
    entries = 250.0 * cells
    total = jnp.broadcast_to(jnp.sum(sums, axis=1, keepdims=True), (CAP, LANES))
    mean = total / jnp.maximum(entries, 1.0)
    squares = zero
    for g in range(GROUPS):

        def square(r, acc):
            rows = pl.ds(r * SIDE * CAP, SIDE * CAP)
            diff = by_tile(conv[g, rows, :]) - mean[None]
            return acc + jnp.sum(diff * diff * by_tile(mask[rows, :]), axis=0)

        squares = squares + lax.fori_loop(0, SIDE, square, zero) * lane_mask(g)
    spread = jnp.broadcast_to(jnp.sum(squares, axis=1, keepdims=True), (CAP, LANES))
    n_tile = member * entries
    n = jnp.sum(n_tile, axis=0, keepdims=True)
    centre = jnp.sum(n_tile * mean, axis=0, keepdims=True) / jnp.maximum(n, 1.0)
    off = mean - centre
    m2 = jnp.sum(member * spread + n_tile * off * off, axis=0, keepdims=True)
    return stack_rows(n, centre, m2)


def forward_kernel(
    near_ref, x_ref, g_ref, ocean_ref, member_ref, wt_ref, lanes_ref,
    tiles_out, grad_out, mask_out, conv_out, padded_out, stat_ref,
    xbuf, gbuf, tiles, grad, mask, pool, padded, conv, w, inner, outer, partial,
    load_sem, store_sem, send, recv, small_send, small_recv,
):
    ahead, behind, partner = halo_peers()
    ready = greet([ahead, behind, partner] + inner_peers() + outer_peers())
    loads = load_native(x_ref, xbuf, load_sem) + load_native(g_ref, gbuf, load_sem, 4)
    for copy in loads:
        copy.start()
    for half in range(2):
        xbuf[half, pl.ds(2000, 48), :] = jnp.zeros((48, LANES), F32)
        gbuf[half, pl.ds(2000, 48), :] = jnp.zeros((48, LANES), F32)
    for g in range(GROUPS):
        pool[g, pl.ds(5 * RIM_ROWS, RIM_ROWS), :] = jnp.zeros((RIM_ROWS, LANES), F32)

        def clear(i, carry):
            padded[g, pl.ds(i * PAD * CAP, PAD * CAP), :] = jnp.zeros((PAD * CAP, LANES), F32)
            return carry

        lax.fori_loop(0, PAD, clear, 0)
    taps = wt_ref[...]
    taps = jnp.concatenate([taps, jnp.zeros((KSIZE * KSIZE, 6), F32)], axis=1)
    for g in range(GROUPS):
        for k in range(KSIZE * KSIZE):
            w[g, k] = jnp.broadcast_to(
                taps[k : k + 1, g * LANES : (g + 1) * LANES], (CAP, LANES)
            )
    ready()

    sends = [[], [], []]
    for p, (g, half) in enumerate(PIECES):
        loads[p].wait()
        to_rows(xbuf, tiles, g, half)
        for first, rim, cells in rim_spans(half):
            pool[g, pl.ds(4 * RIM_ROWS + rim * CAP, cells * CAP), :] = tiles[
                g, pl.ds(first * CAP, cells * CAP), :
            ]
        for kind, (role, peer) in enumerate([(1, ahead), (0, behind), (3, partner)]):
            i = kind * 4 + p
            copy = remote(
                piece(pool, 4, p), piece(pool, role, p), send.at[i], recv.at[i], peer
            )
            copy.start()
            sends[kind].append(copy)
    stores = [pltpu.make_async_copy(tiles, tiles_out, store_sem.at[0])]
    stores[0].start()
    for g in range(GROUPS):

        def centre(r, carry):
            padded[g, pl.ds(((r + RIM) * PAD + RIM) * CAP, SIDE * CAP), :] = tiles[
                g, pl.ds(r * SIDE * CAP, SIDE * CAP), :
            ]
            return carry

        lax.fori_loop(0, SIDE, centre, 0)
    for p, (g, half) in enumerate(PIECES):
        loads[4 + p].wait()
        to_rows(gbuf, grad, g, half)
    for half in range(2):
        for t in range(CAP):
            row = ocean_ref[t : t + 1, half * LANES : (half + 1) * LANES]
            mask[pl.ds(half * 1024 + t, LANES, stride=CAP), :] = jnp.broadcast_to(
                row, (LANES, LANES)
            ).T
    for source, target in [(grad, grad_out), (mask, mask_out)]:
        stores.append(pltpu.make_async_copy(source, target, store_sem.at[len(stores)]))
        stores[-1].start()

    passed = []

    def pass_on(p):
        sends[0][p].wait_recv()
        copy = remote(
            piece(pool, 1, p), piece(pool, 2, p), send.at[12 + p], recv.at[12 + p], partner
        )
        copy.start()
        passed.append(copy)

    own_conv(0, padded, conv, w, lanes_ref)
    pass_on(0)
    own_conv(1, padded, conv, w, lanes_ref)
    for p in range(1, 4):
        pass_on(p)
    for copy in sends[1] + sends[2] + passed:
        copy.wait_recv()
    gather(near_ref, pool, padded)
    halo_conv(padded, conv, w)
    for source, target in [(conv, conv_out), (padded, padded_out)]:
        stores.append(pltpu.make_async_copy(source, target, store_sem.at[len(stores)]))
        stores[-1].start()
    partial[...] = local_stats(conv, mask, member_ref[...])
    stat_ref[...] = reduce_vector(merge_stats, partial, inner, outer, small_send, small_recv)
    for copy in sends[0] + sends[1] + sends[2] + passed:
        copy.wait_send()
    for copy in stores:
        copy.wait()


def forward(near, x, g, ocean, member, wt, lanes):
    rows = (GROUPS, ROWS, LANES)
    wide = (GROUPS, PAD * PAD * CAP, LANES)
    return pl.pallas_call(
        forward_kernel,
        in_specs=[SMEM_SPEC, ANY_SPEC, ANY_SPEC] + [VMEM_SPEC] * 4,
        out_specs=(ANY_SPEC,) * 5 + (VMEM_SPEC,),
        out_shape=(
            shape(*rows), shape(*rows), shape(ROWS, LANES), shape(*rows), shape(*wide),
            shape(CAP, LANES),
        ),
        scratch_shapes=[buffer(*rows)] * 4 + [
            buffer(ROWS, LANES), buffer(GROUPS, ROLES * RIM_ROWS, LANES), buffer(*wide),
            buffer(*rows), buffer(GROUPS, KSIZE * KSIZE, CAP, LANES),
            buffer(INNER, CAP, LANES), buffer(OUTER, CAP, LANES), buffer(CAP, LANES),
            semaphores(8), semaphores(5), semaphores(16), semaphores(16),
            semaphores(INNER + OUTER), semaphores(INNER + OUTER),
        ],
        compiler_params=params(collective_id=1, has_side_effects=True),
        name="forward",
    )(near, x, g, ocean, member, wt, lanes)


def sums_kernel(sums_ref, member_ref, o_ref, inner, outer, partial, send, recv):
    ready = greet(inner_peers() + outer_peers())
    rows = [
        jnp.sum(member_ref[...] * jnp.sum(sums_ref[i], axis=1, keepdims=True), axis=0, keepdims=True)
        for i in range(2)
    ]
    partial[...] = stack_rows(*rows)
    ready()
    o_ref[...] = reduce_vector(merge_sums, partial, inner, outer, send, recv)


def reduce_sums(sums, member):
    return pl.pallas_call(
        sums_kernel,
        in_specs=[VMEM_SPEC] * 2,
        out_specs=VMEM_SPEC,
        out_shape=shape(CAP, LANES),
        scratch_shapes=[
            buffer(INNER, CAP, LANES), buffer(OUTER, CAP, LANES), buffer(CAP, LANES),
            semaphores(INNER + OUTER), semaphores(INNER + OUTER),
        ],
        compiler_params=pltpu.CompilerParams(collective_id=2, has_side_effects=True),
        name="reduce_sums",
    )(sums, member)


def split(x):
    high = x.astype(BF16)
    return high, (x - high.astype(F32)).astype(BF16)


def dot3(a, b, lhs_dim, rhs_dim):
    dims = (((lhs_dim,), (rhs_dim,)), ((), ()))
    dot = functools.partial(lax.dot_general, dimension_numbers=dims, preferred_element_type=F32)
    return dot(a[0], b[0]) + dot(a[1], b[0]) + dot(a[0], b[1])


ERF_P = 0.3275911 * 0.7071067811865476
ERF_A = [0.5 * c for c in (1.061405429, -1.453152027, 1.421413741, -0.284496736, 0.254829592)]


def gelu_parts(x):
    size = jnp.abs(x)
    t = pl.reciprocal(1.0 + ERF_P * size)
    e = jnp.exp(-0.5 * (x * x))
    poly = ERF_A[0]
    for c in ERF_A[1:]:
        poly = poly * t + c
    tail = poly * t * e
    cdf = jnp.where(x < 0.0, tail, 1.0 - tail)
    return x * cdf, cdf + x * (e * 0.3989422804014327)


BLOCK_ROWS = 512
BLOCKS = ROWS // BLOCK_ROWS


def tile_values(stat_row, member):
    return jnp.broadcast_to(
        jnp.sum(member * stat_row, axis=1, keepdims=True), (CAP, LANES)
    )


def norm_values(stat, member):
    n = stat[0:1]
    variance = stat[2:3] / n
    inv = lax.rsqrt(variance + NORM_EPSILON)
    sample = lax.broadcasted_iota(jnp.int32, (1, LANES), 1) < SAMPLES
    inv = jnp.where(sample, inv, 0.0)
    return tile_values(stat[1:2], member), tile_values(inv, member)


def edge_zero(x, rows, columns):
    row = lax.broadcasted_iota(jnp.int32, x.shape, 0)
    column = lax.broadcasted_iota(jnp.int32, x.shape, 1)
    return jnp.where((row < rows) & (column < columns), x, 0.0)


def dense_kernel(
    stat_ref, member_ref, conv_ref, tiles_ref, grad_ref, mask_ref,
    lanes_ref, win_ref, bin_ref, wout_ref,
    out_ref, gscaled_ref, dw_ref, vec_ref, hvec_ref, sums_ref,
    win_hi, win_lo, wout_hi, wout_lo,
):
    step = pl.program_id(0)

    @pl.when(step == 0)
    def _():
        win_hi[...], win_lo[...] = split(edge_zero(win_ref[...], 1000, 250))
        wout_hi[...], wout_lo[...] = split(edge_zero(wout_ref[...], 1000, 250))
        dw_ref[...] = jnp.zeros_like(dw_ref)
        vec_ref[...] = jnp.zeros_like(vec_ref)
        hvec_ref[...] = jnp.zeros_like(hvec_ref)
        sums_ref[...] = jnp.zeros_like(sums_ref)

    win = (win_hi[...], win_lo[...])
    wout = (wout_hi[...], wout_lo[...])
    mean, inv = norm_values(stat_ref[...], member_ref[...])
    mask = by_tile(mask_ref[...])
    line = lambda g, i: lanes_ref[g, i : i + 1, :]
    normed = [(by_tile(conv_ref[g]) - mean[None]) * inv[None] for g in range(GROUPS)]
    flat = lambda parts: jnp.concatenate([p.reshape(-1, LANES) for p in parts], axis=1)
    scaled = split(
        flat([normed[g] * line(g, 1)[None] + line(g, 2)[None] for g in range(GROUPS)])
    )
    pre = dot3(scaled, win, 1, 1) + bin_ref[...]
    hidden, slope = gelu_parts(pre)
    hidden = split(hidden)
    update = dot3(hidden, wout, 1, 0)
    g_update = [by_tile(grad_ref[g]) * mask for g in range(GROUPS)]
    for g in range(GROUPS):
        part = by_tile(update[:, g * LANES : (g + 1) * LANES] + line(g, 3))
        out_ref[g] = (mask * (by_tile(tiles_ref[g]) + part)).reshape(-1, LANES)
    g_split = split(flat(g_update))
    g_pre = dot3(g_split, wout, 1, 1) * slope
    hvec_ref[...] += jnp.sum(g_pre, axis=0, keepdims=True)
    g_pre = split(g_pre)
    dw_ref[0:256, :] += dot3(scaled, g_pre, 0, 0)
    dw_ref[256:512, :] += dot3(g_split, hidden, 0, 0)
    g_scaled = dot3(g_pre, win, 1, 0)
    first = jnp.zeros((CAP, LANES), F32)
    second = jnp.zeros((CAP, LANES), F32)
    for g in range(GROUPS):
        gs = by_tile(g_scaled[:, g * LANES : (g + 1) * LANES])
        gscaled_ref[g] = gs.reshape(-1, LANES)
        gain_sum = jnp.sum(gs * normed[g], axis=0)
        bias_sum = jnp.sum(gs, axis=0)
        first = first + bias_sum * line(g, 1)
        second = second + gain_sum * line(g, 1)
        vec_ref[g, 0] += jnp.sum(g_update[g], axis=0)
        vec_ref[g, 1] += gain_sum
        vec_ref[g, 2] += bias_sum
    sums_ref[0] += first
    sums_ref[1] += second


def dense(stat, member, conv, tiles, grad, mask, lanes, win, bin_, wout):
    block = pl.BlockSpec((GROUPS, BLOCK_ROWS, LANES), lambda i: (0, i, 0))
    mask_block = pl.BlockSpec((BLOCK_ROWS, LANES), lambda i: (i, 0))
    whole = lambda *dims: pl.BlockSpec(dims, lambda i: (0,) * len(dims))
    return pl.pallas_call(
        dense_kernel,
        grid=(BLOCKS,),
        in_specs=[
            whole(CAP, LANES), whole(CAP, LANES), block, block, block, mask_block,
            whole(GROUPS, CAP, LANES), whole(HIDDEN_PAD, 256), whole(1, HIDDEN_PAD),
            whole(HIDDEN_PAD, 256),
        ],
        out_specs=(
            block, block, whole(512, HIDDEN_PAD),
            whole(GROUPS, 3, CAP, LANES), whole(1, HIDDEN_PAD), whole(2, CAP, LANES),
        ),
        out_shape=(
            shape(GROUPS, ROWS, LANES), shape(GROUPS, ROWS, LANES), shape(512, HIDDEN_PAD),
            shape(GROUPS, 3, CAP, LANES), shape(1, HIDDEN_PAD), shape(2, CAP, LANES),
        ),
        scratch_shapes=[pltpu.VMEM((HIDDEN_PAD, 256), BF16)] * 4,
        compiler_params=params(),
        name="dense",
    )(stat, member, conv, tiles, grad, mask, lanes, win, bin_, wout)


def back_kernel(
    near_ref, stat_ref, sum_ref, member_ref, conv_ref, gscaled_ref, mask_ref, lanes_ref, wt_ref,
    own_out, pool_out, gconv, db_ref, gpad, pool, w, sems,
):
    taps = wt_ref[...]
    taps = jnp.concatenate([taps, jnp.zeros((KSIZE * KSIZE, 6), F32)], axis=1)
    for g in range(GROUPS):
        for k in range(KSIZE * KSIZE):
            w[g, k] = jnp.broadcast_to(
                taps[k : k + 1, g * LANES : (g + 1) * LANES], (CAP, LANES)
            )
    member = member_ref[...]
    stat = stat_ref[...]
    mean, inv = norm_values(stat, member)
    sums = sum_ref[...]
    sample = lax.broadcasted_iota(jnp.int32, (1, LANES), 1) < SAMPLES
    share = jnp.where(sample, 1.0 / stat[0:1], 0.0)
    first = tile_values(sums[0:1] * share, member)
    second = tile_values(sums[1:2] * share, member)
    for g in range(GROUPS):
        gain = lanes_ref[g, 1:2, :][None]

        def gradient(r, acc):
            rows = pl.ds(r * SIDE * CAP, SIDE * CAP)
            normed = (by_tile(conv_ref[g, rows, :]) - mean[None]) * inv[None]
            g_normed = by_tile(gscaled_ref[g, rows, :]) * gain
            value = (by_tile(mask_ref[rows, :]) * inv[None]) * (
                g_normed - first[None] - normed * second[None]
            )
            gconv[g, rows, :] = value.reshape(-1, LANES)
            return acc + jnp.sum(value, axis=0)

        db_ref[g] = lax.fori_loop(0, SIDE, gradient, jnp.zeros((CAP, LANES), F32)) * lane_mask(g)

        def input_row(r, carry):
            low = jnp.maximum(r - (SIDE - 1), 0)
            high = jnp.minimum(r, KSIZE - 1)

            def tap(a, acc):
                x = by_tile(gconv[g, pl.ds((r - a) * SIDE * CAP, SIDE * CAP), :])
                for b in range(KSIZE):
                    part = w[g, a * KSIZE + b][None] * x
                    acc = (
                        acc[:b] + tuple(acc[b + i] + part[i] for i in range(SIDE)) + acc[b + SIDE :]
                    )
                return acc

            acc = lax.fori_loop(
                low, high + 1, tap, tuple(jnp.zeros((CAP, LANES), F32) for _ in range(PAD))
            )
            for i in range(PAD):
                gpad[g, pl.ds((r * PAD + i) * CAP, CAP), :] = acc[i]
            return carry

        lax.fori_loop(0, PAD, input_row, 0)

        def zero(i, carry):
            pool[g, pl.ds(i * RIM_ROWS, RIM_ROWS), :] = jnp.zeros((RIM_ROWS, LANES), F32)
            return carry

        lax.fori_loop(0, ROLES, zero, 0)

    def scatter(t, carry):
        for k in range(8):
            q = near_ref[t, k]
            for src, src_step, dst, dst_step, length in RUNS[k]:
                for g in range(GROUPS):
                    place = pl.ds(q + dst * CAP, length, stride=dst_step * CAP)
                    pool[g, place, :] = (
                        pool[g, place, :]
                        + gpad[g, pl.ds(src * CAP + t, length, stride=src_step * CAP), :]
                    )
        return carry

    lax.fori_loop(0, CAP, scatter, 0)
    copy = pltpu.make_async_copy(
        pool.at[:, pl.ds(0, (ROLES - 1) * RIM_ROWS), :], pool_out, sems.at[0]
    )
    copy.start()
    for g in range(GROUPS):
        for r in range(SIDE):
            own_out[g, pl.ds(r * SIDE * CAP, SIDE * CAP), :] = gpad[
                g, pl.ds(((r + RIM) * PAD + RIM) * CAP, SIDE * CAP), :
            ]
    copy.wait()


def conv_backward(near, stat, sums, member, conv, gscaled, mask, lanes, wt):
    rows = (GROUPS, ROWS, LANES)
    return pl.pallas_call(
        back_kernel,
        in_specs=[SMEM_SPEC] + [VMEM_SPEC] * 8,
        out_specs=(VMEM_SPEC, ANY_SPEC, VMEM_SPEC, VMEM_SPEC),
        out_shape=(
            shape(*rows), shape(GROUPS, (ROLES - 1) * RIM_ROWS, LANES), shape(*rows),
            shape(GROUPS, CAP, LANES),
        ),
        scratch_shapes=[
            buffer(GROUPS, PAD * PAD * CAP, LANES), buffer(GROUPS, ROLES * RIM_ROWS, LANES),
            buffer(GROUPS, KSIZE * KSIZE, CAP, LANES), semaphores(1),
        ],
        compiler_params=params(),
        name="conv_backward",
    )(near, stat, sums, member, conv, gscaled, mask, lanes, wt)


SMALL = 16
HALF = 256


def tail_kernel(
    pool_ref, gconv_ref, padded_ref, rows_ref, big_ref, vec_ref, hvec_ref, db_ref,
    rim_out, big_out, small_ref, native_out,
    pool, gconv, padded, rows, native, pay, got, half, other, slots, zslots, big, small, tile,
    sslots, zcslots, load_sem, store_sem, send, recv,
):
    me = lax.axis_index("tiles")
    core, z, xy = me % 2, (me // 2) % 4, me // INNER
    ahead, behind, partner = halo_peers()
    z_peers = [xy * INNER + ((z + j) % 4) * 2 + core for j in range(1, 4)]
    xy_peers = outer_peers()
    zc_peers = inner_peers()
    ready = greet([ahead, behind, partner] + zc_peers + xy_peers)
    mine = pl.multiple_of(core * HALF, HALF)
    theirs = pl.multiple_of((1 - core) * HALF, HALF)

    loads = [
        pltpu.make_async_copy(source, target, load_sem.at[i])
        for i, (source, target) in enumerate(
            [
                (rows_ref, rows),
                (pool_ref.at[:, pl.ds(RIM_ROWS, RIM_ROWS), :], pool.at[0]),
                (gconv_ref, gconv),
                (padded_ref, padded),
                (big_ref.at[pl.ds(mine, HALF), :], half),
                (pool_ref.at[:, pl.ds(4 * RIM_ROWS, RIM_ROWS), :], pool.at[1]),
            ]
        )
    ]
    for copy in loads:
        copy.start()
    loads[0].wait()
    stores = store_native(native, native_out, store_sem)
    for p, (g, part) in enumerate(PIECES):
        from_rows(rows, native, g, part)
        stores[p].start()
    ready()

    used = [0]

    def start(source, target, peer):
        i = used[0]
        used[0] += 1
        copy = remote(source, target, send.at[i], recv.at[i], peer)
        copy.start()
        return copy

    def part_of(ref, p):
        g, part = PIECES[p]
        return ref.at[g, pl.ds(part * HALF_RIM, HALF_RIM), :]

    payload = [start(piece(pool_ref, 2, p), part_of(pay, p), partner) for p in range(4)]
    direct = [start(piece(pool_ref, 0, p), part_of(got.at[0], p), ahead) for p in range(4)]
    halves = start(big_ref.at[pl.ds(theirs, HALF), :], other, partner)
    near = [start(piece(pool_ref, 3, p), part_of(got.at[2], p), partner) for p in range(4)]
    loads[1].wait()
    merged = []
    for p, (g, part) in enumerate(PIECES):
        payload[p].wait_recv()
        span = pl.ds(part * HALF_RIM, HALF_RIM)
        pool[0, g, span, :] = pool[0, g, span, :] + pay[g, span, :]
        merged.append(start(part_of(pool.at[0], p), part_of(got.at[1], p), behind))

    def weight_rows(g, low, high):
        def weight_row(a, carry):
            def one(r, acc):
                x = by_tile(padded[g, pl.ds((r + a) * PAD * CAP, PAD * CAP), :])
                y = by_tile(gconv[g, pl.ds(r * SIDE * CAP, SIDE * CAP), :])
                return tuple(
                    acc[b] + jnp.sum(x[b : b + SIDE] * y, axis=0) for b in range(KSIZE)
                )

            acc = lax.fori_loop(
                0, SIDE, one, tuple(jnp.zeros((CAP, LANES), F32) for _ in range(KSIZE))
            )
            for b in range(KSIZE):
                small[g, pl.ds(a * KSIZE + b, 1), :] = jnp.sum(acc[b], axis=0, keepdims=True)
            return carry

        lax.fori_loop(low, high, weight_row, 0)

    loads[2].wait()
    loads[3].wait()
    weight_rows(0, 0, 2)
    loads[4].wait()
    halves.wait_recv()
    half[...] = half[...] + other[...]
    scattered = [
        start(
            half.at[pl.ds(pl.multiple_of((peer // INNER) * 16, 16), 16), :], slots.at[xy], peer
        )
        for peer in xy_peers
    ]
    slots[xy] = half[pl.ds(pl.multiple_of(xy * 16, 16), 16), :]
    weight_rows(0, 2, KSIZE)
    weight_rows(1, 0, 4)
    for copy in scattered:
        copy.wait_recv()
    big_rows = pl.ds(pl.multiple_of(core * HALF + xy * 16, 16), 16)
    z_lanes = lambda i: pl.ds(pl.multiple_of(i * 256, 256), 256)
    for copy in scattered:
        copy.wait_send()
    half[0:16, :] = jnp.sum(slots[...], axis=0)
    z_scattered = [
        start(
            half.at[pl.ds(0, 16), z_lanes((peer // 2) % 4)], zslots.at[z], peer
        )
        for peer in z_peers
    ]
    zslots[z] = half[0:16, z_lanes(z)]
    weight_rows(1, 4, KSIZE)
    for g in range(GROUPS):
        lines = [jnp.sum(db_ref[g], axis=0, keepdims=True)]
        lines += [jnp.sum(vec_ref[g, i], axis=0, keepdims=True) for i in range(3)]
        lines += [hvec_ref[0:1, pl.ds((g * 4 + i) * LANES, LANES)] for i in range(4)]
        for i, line in enumerate(lines):
            small[g, pl.ds(49 + i, 1), :] = line
        small[g, pl.ds(57, 7), :] = jnp.zeros((7, LANES), F32)
    small_tile = lambda q: small.at[q // 8, pl.ds(pl.multiple_of((q % 8) * CAP, CAP), CAP), :]
    small_scattered = [
        start(small_tile(peer // INNER), sslots.at[xy], peer) for peer in xy_peers
    ]
    sslots[xy] = small[xy // 8, pl.ds(pl.multiple_of((xy % 8) * CAP, CAP), CAP), :]
    for copy in z_scattered:
        copy.wait_recv()
    big[big_rows, z_lanes(z)] = jnp.sum(zslots[...], axis=0)
    own = big.at[big_rows, z_lanes(z)]
    z_gathered = [start(own, own, peer) for peer in z_peers]
    for copy in small_scattered:
        copy.wait_recv()
    tile[...] = jnp.sum(sslots[...], axis=0)
    zc_gathered = [start(tile, zcslots.at[me % INNER], peer) for peer in zc_peers]
    zcslots[me % INNER] = tile[...]
    for copy in z_gathered:
        copy.wait_recv()
    own = big.at[big_rows, :]
    xy_gathered = [start(own, own, peer) for peer in xy_peers]
    for copy in zc_gathered:
        copy.wait_recv()
    small_ref[xy] = jnp.sum(zcslots[...], axis=0)
    small_gathered = [start(small_ref.at[xy], small_ref.at[xy], peer) for peer in xy_peers]
    for copy in xy_gathered:
        copy.wait_recv()
    own = big.at[pl.ds(mine, HALF), :]
    crossed = start(own, own, partner)
    loads[5].wait()
    for copy in near + direct:
        copy.wait_recv()
    for p, (g, part) in enumerate(PIECES):
        merged[p].wait_recv()
        span = pl.ds(part * HALF_RIM, HALF_RIM)
        pool[1, g, span, :] = (pool[1, g, span, :] + got[2, g, span, :]) + (
            got[0, g, span, :] + got[1, g, span, :]
        )
    finish = [pltpu.make_async_copy(pool.at[1], rim_out, store_sem.at[4])]
    finish[0].start()
    crossed.wait_recv()
    finish.append(pltpu.make_async_copy(big, big_out, store_sem.at[5]))
    finish[1].start()
    for copy in small_gathered:
        copy.wait_recv()
    every = payload + direct + [halves] + near + merged + z_scattered + small_scattered
    every += z_gathered + zc_gathered + xy_gathered + small_gathered + [crossed]
    for copy in every:
        copy.wait_send()
    for copy in stores + finish:
        copy.wait()


def tail(pool, gconv, padded, rows, big, vec, hvec, db):
    rim = (GROUPS, RIM_ROWS, LANES)
    count = 17 + 15 + 3 + 15 + 3 + 7 + 15 + 15 + 1
    return pl.pallas_call(
        tail_kernel,
        in_specs=[ANY_SPEC] * 5 + [VMEM_SPEC] * 3,
        out_specs=(ANY_SPEC, ANY_SPEC, VMEM_SPEC, ANY_SPEC),
        out_shape=(
            shape(*rim), shape(512, HIDDEN_PAD), shape(SMALL, CAP, LANES), shape(2000, 256),
        ),
        scratch_shapes=[
            buffer(2, *rim), buffer(GROUPS, ROWS, LANES),
            buffer(GROUPS, PAD * PAD * CAP, LANES), buffer(GROUPS, ROWS, LANES),
            buffer(GROUPS, ROWS, LANES), buffer(*rim), buffer(3, *rim),
            buffer(HALF, HIDDEN_PAD), buffer(HALF, HIDDEN_PAD), buffer(OUTER, 16, HIDDEN_PAD),
            buffer(4, 16, 256), buffer(512, HIDDEN_PAD), buffer(GROUPS, 64, LANES),
            buffer(CAP, LANES), buffer(OUTER, CAP, LANES), buffer(INNER, CAP, LANES),
            semaphores(6), semaphores(6), semaphores(count), semaphores(count),
        ],
        compiler_params=params(collective_id=3, has_side_effects=True),
        name="tail",
    )(pool, gconv, padded, rows, big, vec, hvec, db)


def final_kernel(
    own_ref, grad_ref, mask_ref, rim_ref, big_ref, small_ref, stat_ref, native_ref,
    out_ref, tiles_ref, dwin_ref, dwout_ref, dconv_ref, lines_ref, hline_ref,
    total, buf, through, sems,
):
    whole = pltpu.make_async_copy(native_ref, through, sems.at[4])
    whole.start()
    stores = store_native(buf, tiles_ref, sems)
    for p, (g, half) in enumerate(PIECES):

        def add(r, carry):
            rows = pl.ds(r * SIDE * CAP, SIDE * CAP)
            total[g, rows, :] = own_ref[g, rows, :] + grad_ref[g, rows, :] * mask_ref[rows, :]
            return carry

        lax.fori_loop(half * 8, half * 8 + 8, add, 0)
        for first, rim, cells in rim_spans(half):
            rows = pl.ds(first * CAP, cells * CAP)
            total[g, rows, :] = total[g, rows, :] + rim_ref[g, pl.ds(rim * CAP, cells * CAP), :]
        from_rows(total, buf, g, half)
        stores[p].start()
    whole.wait()
    whole = pltpu.make_async_copy(through, out_ref, sems.at[5])
    whole.start()
    sample = lax.broadcasted_iota(jnp.int32, (1, LANES), 1) < SAMPLES
    cells = jnp.sum(jnp.where(sample, stat_ref[0:1, :], 0.0), axis=1, keepdims=True)
    share = 250.0 / cells
    dwin_ref[...] = big_ref[0:256, :].T[:1000, :250] * share
    dwout_ref[...] = big_ref[256:512, :].T[:1000, :250] * share
    flat = []
    for g in range(GROUPS):
        flat.append(
            jnp.concatenate([small_ref[g * 8 + i] for i in range(8)], axis=0) * share
        )
    flat = jnp.concatenate(flat, axis=1)
    dconv_ref[...] = flat[0:49, :250]
    lines_ref[...] = flat[48:56, :250]
    for g in range(GROUPS):
        for i in range(4):
            j = 53 + i
            hline_ref[0:1, pl.ds((g * 4 + i) * LANES, LANES)] = (
                flat[j : j + 1, g * LANES : (g + 1) * LANES]
            )
    whole.wait()
    for copy in stores:
        copy.wait()


def final(own, grad, mask, rim, big, small, stat, native):
    return pl.pallas_call(
        final_kernel,
        in_specs=[VMEM_SPEC] * 7 + [ANY_SPEC],
        out_specs=(ANY_SPEC,) * 2 + (VMEM_SPEC,) * 5,
        out_shape=(
            shape(2000, 256), shape(2000, 256), shape(1000, 250), shape(1000, 250),
            shape(49, 250), shape(8, 250), shape(1, HIDDEN_PAD),
        ),
        scratch_shapes=[
            buffer(GROUPS, ROWS, LANES), buffer(GROUPS, ROWS, LANES), buffer(2000, 256), semaphores(6)
        ],
        compiler_params=params(),
        name="final",
    )(own, grad, mask, rim, big, small, stat, native)


def native(x):
    return jnp.transpose(x, (1, 0, 2)).reshape(2000, CELLS)


def from_native(x):
    return jnp.transpose(x.reshape(250, CAP, CELLS), (1, 0, 2))


def prepare(device, tile_counts, ocean_mask, neighbours, sample_ids):
    slot = lax.iota(jnp.int32, CAP)
    filled = (slot < tile_counts[0]).astype(F32)
    ocean = ocean_mask.astype(F32) * filled[:, None]
    lane = lax.iota(jnp.int32, LANES)
    member = (sample_ids[:, None] == lane[None, :]).astype(F32)
    offset = (neighbours // CAP - device) * (2 * (device % 2) - 1)
    role = jnp.full_like(offset, 4)
    for i, value in enumerate((2, -2, 1, -1)):
        role = jnp.where(offset == value, i, role)
    place = role * RIM_ROWS + neighbours % CAP
    near = jnp.where(neighbours >= 0, place, 5 * RIM_ROWS)
    return ocean, member, near


def local(
    tiles_in, conv_weight, conv_bias, norm_gain, norm_bias, weight_in, bias_in,
    weight_out, bias_out, grad_out, tile_counts, ocean_mask, neighbours, sample_ids,
):
    device = lax.axis_index("tiles")
    ocean, member, near = prepare(device, tile_counts, ocean_mask, neighbours, sample_ids)
    lanes = jnp.stack([conv_bias, norm_gain, norm_bias, bias_out])
    lanes = jnp.pad(lanes, ((0, 4), (0, 6))).reshape(CAP, GROUPS, LANES).transpose(1, 0, 2)
    bin_ = jnp.pad(bias_in, (0, 24))[None]
    wt = conv_weight.T
    tiles, grad, mask, conv, padded, stat = forward(
        near, native(tiles_in), native(grad_out), ocean, member, wt, lanes
    )
    out, gscaled, big, vec, hvec, sums = dense(
        stat, member, conv, tiles, grad, mask, lanes, weight_in.T, bin_, weight_out
    )
    sample_sums = reduce_sums(sums, member)
    own, pool, gconv, db = conv_backward(
        near, stat, sample_sums, member, conv, gscaled, mask, lanes, wt
    )
    rim, big, small, out = tail(pool, gconv, padded, out, big, vec, hvec, db)
    output, grad_tiles, dwin, dwout, dconv, lines, hline = final(
        own, grad, mask, rim, big, small, stat, out
    )
    return (
        from_native(output),
        from_native(grad_tiles),
        dconv.T,
        lines[1],
        lines[3],
        lines[4],
        dwin.T,
        hline[0, :1000],
        dwout,
        lines[2],
    )


def solution(mesh):
    tiles = P("tiles")
    whole = P()
    return jax.shard_map(
        local,
        mesh=mesh,
        in_specs=(tiles,) + (whole,) * 8 + (tiles,) * 5,
        out_specs=(tiles, tiles) + (whole,) * 8,
        check_vma=False,
    )
```

time: 399 us -> 220 us (0.55)
  blocking collectives: 100 us -> 0 us
  waiting for transfers between devices: 77.1 us -> 0 us
  Pallas kernels: 144 us -> 210 us
  starting transfers between devices: 25.4 us -> 0 us
  local copies, waits for them, and re-layouts: 26.9 us -> 2.02 us
  between operations: 15.7 us -> 1.37 us
    psum x1 -> x0, blocking collectives: 100 us -> none  [local(): dw, db = lax.psum((jnp.sum(dw, axis=2), jnp.sum(db, axis=1)), 'tiles')]
    pallas_call x8 -> x5, Pallas kernels: 108 us -> 174 us  [the longest x1 77.2 us: tail(): pl.pallas_call(tail_kernel, in_specs=[ANY_SPEC] * 5 + [VMEM_SPEC] * 3, ou...]
    psum x1 -> x0, waiting for transfers between devices: 55.6 us -> none  [local(): lax.psum((dwin, dwout, jnp.sum(vec, axis=2), hvec), 'tiles')]
    ppermute x8 -> x0, starting transfers between devices: 25.4 us -> none  [passed_along(): return lax.ppermute(block, axis, route)]
    ppermute x8 -> x0, waiting for transfers between devices: 21.4 us -> none  [passed_along(): return lax.ppermute(block, axis, route)]
    unnamed x41 -> x2, local copies, waits for them, and re-layouts: 19 us -> 0.01 us
  transfers between devices with their start and end apart: 9 -> 0, of which waited for: 4 -> 0; matrix products, arithmetic and copies ran while one was open for 5% -> 0% of each run, Pallas kernels for 3% -> 0%
where the time goes in v2:
time: 220 us; the launch traced here: 219 us
  Pallas kernels  210 us (95%)
  other arithmetic  5.32 us (2%)
    pallas_call x1, Pallas kernels, tail(): pl.pallas_call(tail_kernel, in_specs=[ANY_SPEC] * 5 + [VMEM_SPEC] * 3, ou...  77.2 us
    pallas_call x1, Pallas kernels, forward(): pl.pallas_call(forward_kernel, in_specs=[SMEM_SPEC, ANY_SPEC, ANY_SPEC] +...  55.9 us
    pallas_call x1, Pallas kernels, dense(): pl.pallas_call(dense_kernel, grid=(BLOCKS,), in_specs=[whole(CAP, LANES),...  36.9 us
    pallas_call x1, Pallas kernels, conv_backward(): pl.pallas_call(back_kernel, in_specs=[SMEM_SPEC] + [VMEM_SPEC] * 8, out_s...  19.3 us
    pallas_call x1, Pallas kernels, reduce_sums(): pl.pallas_call(sums_kernel, in_specs=[VMEM_SPEC] * 2, out_specs=VMEM_SPEC...  12.9 us
    pallas_call x1, Pallas kernels, final(): pl.pallas_call(final_kernel, in_specs=[VMEM_SPEC] * 7 + [ANY_SPEC], out_s...  8.16 us

profile of v2, /device:TPU:1, one launch (start us, length us, event | category | flops | bytes accessed | tf_op | source)
XLA Modules:
  0.0 219.2 jit_solution(11982281506783260781)
XLA Ops:
  0.7 1.3 fusion.4.near_ref
  2.6 1.4 convert_multiply_fusion.ocean_ref
  4.0 1.3 fusion.6.member_ref
  5.3 1.3 fusion.lanes_ref
  6.6 0.0 copy-start
  6.6 55.9 %forward.1 = (f32[2,2048,128]{2,1,0:T(8,128)}, f32[2,2048,128]{2,1,0:T(8,128)}, f32[2048,128]{1,0:T(8,128)}, f32[2,2048,128]{2,1,0:T(8,128)}, f32[2,3872,128]{2,1,0:T(8,128)}, /*index=5*/f32[8,128]{1,0:T(8,128)}) custom-call(s32[8,8]{1,0:T(8,128)} %fusion.4.near_ref, f32[2000,256]{1,0:T(8,128)} %bitcast.33, f32[2000,256]{1,0:T(8,128)} %bitcast.34, ...), custom_call_target="tpu_custom_call" | custom-call | tf_op jit(solution)/shard_map/forward/pallas_call | solution.py:463
  62.5 0.0 copy-done
  62.5 0.6 pad.9
  63.1 36.9 %dense.1 = (f32[2,2048,128]{2,1,0:T(8,128)}, f32[2,2048,128]{2,1,0:T(8,128)}, f32[512,1024]{1,0:T(8,128)}, f32[2,3,8,128]{3,2,1,0:T(8,128)}, f32[1,1024]{1,0:T(1,128)}, /*index=5*/f32[2,8,128]{2,1,0:T(8,128)}) custom-call(f32[8,128]{1,0:T(8,128)} %get-tuple-element.37.stat_ref, f32[8,128]{1,0:T(8,128)} %fusion.6.member_ref, ...), custom_call_target="tpu_custom_call" | custom-call | tf_op jit(solution)/shard_map/dense/pallas_call | solution.py:623
  100.1 12.9 %reduce_sums.1.sum_ref = f32[8,128]{1,0:T(8,128)} custom-call(f32[2,8,128]{2,1,0:T(8,128)} %get-tuple-element.42.sums_ref, f32[8,128]{1,0:T(8,128)} %fusion.6.member_ref), custom_call_target="tpu_custom_call" | custom-call | tf_op jit(solution)/shard_map/reduce_sums/pallas_call | solution.py:495
  113.0 19.3 %conv_backward.1 = (f32[2,2048,128]{2,1,0:T(8,128)}, f32[2,6240,128]{2,1,0:T(8,128)}, f32[2,2048,128]{2,1,0:T(8,128)}, f32[2,8,128]{2,1,0:T(8,128)}) custom-call(s32[8,8]{1,0:T(8,128)} %fusion.4.near_ref, f32[8,128]{1,0:T(8,128)} %get-tuple-element.37.stat_ref, f32[8,128]{1,0:T(8,128)} %reduce_sums.1.sum_ref, f32[8,128]{1,0:T(8,128)} %fusion.6.member_ref, ...), custom_call_target="tpu_custom_call" | custom-call | tf_op jit(solution)/shard_map/conv_backward/pallas_call | solution.py:734
  132.3 77.2 %tail.1 = (f32[2,1248,128]{2,1,0:T(8,128)}, f32[512,1024]{1,0:T(8,128)}, f32[16,8,128]{2,1,0:T(8,128)}, f32[2000,256]{1,0:T(8,128)}) custom-call(f32[2,6240,128]{2,1,0:T(8,128)} %get-tuple-element.45.pool_ref, f32[2,2048,128]{2,1,0:T(8,128)} %get-tuple-element.46.gconv_ref, f32[2,3872,128]{2,1,0:T(8,128)} %get-tuple-element.47.padded_ref, ...), custom_call_target="tpu_custom_call" | custom-call | tf_op jit(solution)/shard_map/tail/pallas_call | solution.py:927
  209.6 8.2 %final.1 = (f32[2000,256]{1,0:T(8,128)}, f32[2000,256]{1,0:T(8,128)}, f32[1000,250]{1,0:T(8,128)}, f32[1000,250]{1,0:T(8,128)}, f32[49,250]{1,0:T(8,128)}, /*index=5*/f32[8,250]{1,0:T(8,128)}, f32[1,1024]{1,0:T(1,128)}) custom-call(f32[2,2048,128]{2,1,0:T(8,128)} %get-tuple-element.44.own_ref, f32[2,2048,128]{2,1,0:T(8,128)} %get-tuple-element.40.grad_ref, ...), custom_call_target="tpu_custom_call" | custom-call | tf_op jit(solution)/shard_map/final/pallas_call | solution.py:997
  217.8 1.4 fusion.7
  (1 shorter events, 0.0 us)
Async XLA Ops:
  6.6 55.9 %copy-start = (f32[1000]{0:T(1024)S(1)}, f32[1000]{0:T(1024)}, u32[]{:S(2)}) copy-start(f32[1000]{0:T(1024)} %param.20) | copy-start | bytes 12004

commit v3 on v0

v3 whole, which is shorter than its diff:
```python
import functools

import jax
import jax.numpy as jnp
from jax import lax
from jax.experimental import pallas as pl
from jax.experimental.pallas import tpu as pltpu
from jax.sharding import PartitionSpec as P

SIDE = 16
KSIZE = 7
RIM = 3
REACH = 2
SAMPLES = 5
CAP = 8
CELLS = SIDE * SIDE
PAD = SIDE + 2 * RIM
LANES = 128
GROUPS = 2
ROWS = CELLS * CAP
RIM_CELLS = 156
RIM_ROWS = RIM_CELLS * CAP
HIDDEN_PAD = 1024
NORM_EPSILON = 1e-05
F32 = jnp.float32
BF16 = jnp.bfloat16
MIB = 1 << 20
MESH = pl.DeviceIdType.MESH
VMEM_SPEC = pl.BlockSpec(memory_space=pltpu.VMEM)
SMEM_SPEC = pl.BlockSpec(memory_space=pltpu.SMEM)
ANY_SPEC = pl.BlockSpec(memory_space=pl.ANY)


def params(mib=60, **more):
    return pltpu.CompilerParams(vmem_limit_bytes=mib * MIB, **more)


HALF_RIM = RIM_ROWS // 2


def rim_spans(half):
    base = half * 78
    outer = 0 if half == 0 else SIDE - RIM
    inner = RIM if half == 0 else SIDE // 2
    spans = [(outer * SIDE, base, 48)]
    for i in range(5):
        spans.append(((inner + i) * SIDE, base + 48 + i * RIM, RIM))
        spans.append(((inner + i) * SIDE + SIDE - RIM, base + 63 + i * RIM, RIM))
    return spans


RIM_OF = {
    first + i: rim + i
    for half in range(2)
    for first, rim, cells in rim_spans(half)
    for i in range(cells)
}


def rim_index(r, c):
    return RIM_OF[r * SIDE + c]


def region_runs():
    spans = {-1: (0, SIDE - RIM, RIM), 0: (RIM, 0, SIDE), 1: (RIM + SIDE, 0, RIM)}
    order = [(-1, -1), (-1, 0), (-1, 1), (0, -1), (0, 1), (1, -1), (1, 0), (1, 1)]
    runs = []
    for dr, dc in order:
        dst_r, src_r, rows = spans[dr]
        dst_c, src_c, cols = spans[dc]
        found = []

        def add(cells):
            start = 0
            while start < len(cells):
                stop = start + 1
                while (
                    stop < len(cells)
                    and stop - start < 8
                    and cells[stop][0] - cells[stop - 1][0] == cells[1][0] - cells[0][0]
                    and cells[stop][1] - cells[stop - 1][1] == cells[1][1] - cells[0][1]
                ):
                    stop += 1
                step = (cells[1][0] - cells[0][0], cells[1][1] - cells[0][1])
                found.append((cells[start][0], step[0], cells[start][1], step[1], stop - start))
                start = stop

        if dr == 0:
            for j in range(cols):
                cells = [
                    ((dst_r + i) * PAD + dst_c + j, rim_index(src_r + i, src_c + j))
                    for i in range(rows)
                ]
                for low, high in ((0, RIM), (RIM, 8), (8, SIDE - RIM), (SIDE - RIM, SIDE)):
                    add(cells[low:high])
        else:
            for i in range(rows):
                add(
                    [
                        ((dst_r + i) * PAD + dst_c + j, rim_index(src_r + i, src_c + j))
                        for j in range(cols)
                    ]
                )
        runs.append(found)
    return runs


RUNS = region_runs()


ROLES = 6
PIECES = [(g, half) for g in range(GROUPS) for half in range(2)]


def piece(ref, role, p):
    g, half = PIECES[p]
    return ref[g].at[pl.ds(role * RIM_ROWS + half * HALF_RIM, HALF_RIM), :]


def halo_peers():
    me = lax.axis_index("tiles")
    total = lax.axis_size("tiles")
    sign = 2 * (me % 2) - 1
    ahead = (me + 2 * sign + total) % total
    behind = (me - 2 * sign + total) % total
    return ahead, behind, me - sign


def remote(src, dst, send, recv, peer):
    return pltpu.make_async_remote_copy(
        src_ref=src, dst_ref=dst, send_sem=send, recv_sem=recv,
        device_id=(peer,), device_id_type=MESH,
    )


def greet(peers):
    barrier = pltpu.get_barrier_semaphore()
    for peer in peers:
        pl.semaphore_signal(barrier, inc=1, device_id=(peer,), device_id_type=MESH)
    return lambda: pl.semaphore_wait(barrier, len(peers))


def load_native(x_ref, buf, sems, first=0):
    copies = []
    for g, half in PIECES:
        rows = 1024 if g == 0 else 976
        copies.append(
            pltpu.make_async_copy(
                x_ref.at[pl.ds(g * 1024, rows), pl.ds(half * LANES, LANES)],
                buf.at[half, pl.ds(g * 1024, rows), :],
                sems.at[first + len(copies)],
            )
        )
    return copies


def to_rows(buf, out, g, half):
    for t in range(CAP):
        block = buf[half, pl.ds(g * 1024 + t, LANES, stride=CAP), :]
        out[g, pl.ds(half * 1024 + t, LANES, stride=CAP), :] = block.T


def store_native(buf, out_ref, sems, first=0):
    copies = []
    for g, half in PIECES:
        rows = 1024 if g == 0 else 976
        copies.append(
            pltpu.make_async_copy(
                buf.at[half, pl.ds(g * 1024, rows), :],
                out_ref.at[pl.ds(g * 1024, rows), pl.ds(half * LANES, LANES)],
                sems.at[first + len(copies)],
            )
        )
    return copies


def from_rows(rows, buf, g, half):
    for t in range(CAP):
        block = rows[g, pl.ds(half * 1024 + t, LANES, stride=CAP), :]
        buf[half, pl.ds(g * 1024 + t, LANES, stride=CAP), :] = block.T


def lane_mask(g):
    lane = lax.broadcasted_iota(jnp.int32, (CAP, LANES), 1)
    return (lane < 250 - g * LANES).astype(F32)


def shape(*dims):
    return jax.ShapeDtypeStruct(dims, F32)


def buffer(*dims):
    return pltpu.VMEM(dims, F32)


def semaphores(count):
    return pltpu.SemaphoreType.DMA((count,))


INNER = 8
OUTER = 16


def inner_peers():
    me = lax.axis_index("tiles")
    group, place = me // INNER, me % INNER
    return [group * INNER + (place + j) % INNER for j in range(1, INNER)]


def outer_peers():
    me = lax.axis_index("tiles")
    group, place = me // INNER, me % INNER
    return [((group + j) % OUTER) * INNER + place for j in range(1, OUTER)]


def exchange_start(x, send, recv, slots, first, mine, peers):
    copies = [
        remote(x, slots.at[mine], send.at[first + j], recv.at[first + j], peer)
        for j, peer in enumerate(peers)
    ]
    for copy in copies:
        copy.start()
    slots[mine] = x[...]
    return copies


def merge_stats(parts):
    n = jnp.sum(parts[:, 0:1], axis=0)
    mean = jnp.sum(parts[:, 0:1] * parts[:, 1:2], axis=0) / jnp.maximum(n, 1.0)
    off = parts[:, 1:2] - mean[None]
    m2 = jnp.sum(parts[:, 2:3] + parts[:, 0:1] * off * off, axis=0)
    return stack_rows(n, mean, m2)


def stack_rows(*rows):
    row_id = lax.broadcasted_iota(jnp.int32, (CAP, LANES), 0)
    value = jnp.zeros((CAP, LANES), F32)
    for i, row in enumerate(rows):
        value = jnp.where(row_id == i, row, value)
    return value


def merge_sums(parts):
    return jnp.sum(parts, axis=0)


def by_tile(x):
    return x.reshape(-1, CAP, LANES)


def own_conv(g, padded, conv, w, lanes_ref):
    bias = jnp.broadcast_to(lanes_ref[g, 0:1, :], (CAP, LANES))[None]

    def row(r, carry):
        acc = jnp.broadcast_to(bias, (SIDE, CAP, LANES))
        for a in range(KSIZE):
            x = by_tile(padded[g, pl.ds((r + a) * PAD * CAP, PAD * CAP), :])
            for b in range(KSIZE):
                acc = acc + w[g, a * KSIZE + b][None] * x[b : b + SIDE]
        conv[g, pl.ds(r * SIDE * CAP, SIDE * CAP), :] = acc.reshape(-1, LANES)
        return carry

    lax.fori_loop(0, SIDE, row, 0)


def place_of(n, me):
    offset = (n // CAP - me) * (2 * (me % 2) - 1)
    role = jnp.where(offset == 2, 0, jnp.where(offset == -2, 1, 4))
    role = jnp.where(offset == 1, 2, jnp.where(offset == -1, 3, role))
    valid = n >= 0
    return jnp.where(valid, role, 5), jnp.where(valid, n % CAP, 0)


def gather(g, near_ref, me, pool, padded):
    def fill(t, carry):
        for k in range(8):
            role, slot = place_of(near_ref[t, k], me)
            q = role * RIM_ROWS + slot
            for dst, dst_step, src, src_step, length in RUNS[k]:
                padded[g, pl.ds(dst * CAP + t, length, stride=dst_step * CAP), :] = pool[g][
                    pl.ds(q + src * CAP, length, stride=src_step * CAP), :
                ]
        return carry

    lax.fori_loop(0, CAP, fill, 0)


def halo_conv(g, padded, conv, w):
    blank = jnp.zeros((RIM, CAP, LANES), F32)
    for r in [0, 1, 2, 13, 14, 15]:
        rows = pl.ds(r * SIDE * CAP, SIDE * CAP)
        acc = by_tile(conv[g, rows, :])
        for a in range(KSIZE):
            if RIM <= r + a < RIM + SIDE:
                continue
            x = by_tile(padded[g, pl.ds(((r + a) * PAD + RIM) * CAP, SIDE * CAP), :])
            x = jnp.concatenate([blank, x, blank], axis=0)
            for b in range(KSIZE):
                acc = acc + w[g, a * KSIZE + b][None] * x[b : b + SIDE]
        conv[g, rows, :] = acc.reshape(-1, LANES)

    def columns(r, carry):
        left = [jnp.zeros((CAP, LANES), F32) for _ in range(RIM)]
        right = [jnp.zeros((CAP, LANES), F32) for _ in range(RIM)]
        for a in range(KSIZE):
            first = (r + a) * PAD * CAP
            xl = by_tile(padded[g, pl.ds(first, RIM * CAP), :])
            xr = by_tile(padded[g, pl.ds(first + (RIM + SIDE) * CAP, RIM * CAP), :])
            for c in range(RIM):
                for b in range(RIM - c):
                    left[c] = left[c] + w[g, a * KSIZE + b] * xl[c + b]
                for b in range(KSIZE - 1 - c, KSIZE):
                    right[c] = right[c] + w[g, a * KSIZE + b] * xr[c + b - KSIZE + 1]
        for c in range(RIM):
            cell = pl.ds((r * SIDE + c) * CAP, CAP)
            conv[g, cell, :] = conv[g, cell, :] + left[c]
            cell = pl.ds((r * SIDE + SIDE - RIM + c) * CAP, CAP)
            conv[g, cell, :] = conv[g, cell, :] + right[c]
        return carry

    lax.fori_loop(0, SIDE, columns, 0)


def masked_sum(g, conv, mask):
    zero = jnp.zeros((CAP, LANES), F32)

    def add(r, carry):
        rows = pl.ds(r * SIDE * CAP, SIDE * CAP)
        m = by_tile(mask[rows, :])
        x = by_tile(conv[g, rows, :])
        return carry[0] + jnp.sum(x * m, axis=0), carry[1] + jnp.sum(m, axis=0)

    return lax.fori_loop(0, SIDE, add, (zero, zero))


def local_stats(sums, cells, conv, mask, member):
    entries = 250.0 * cells
    total = jnp.broadcast_to(jnp.sum(sums, axis=1, keepdims=True), (CAP, LANES))
    mean = total / jnp.maximum(entries, 1.0)
    zero = jnp.zeros((CAP, LANES), F32)
    squares = zero
    for g in range(GROUPS):

        def square(r, acc):
            rows = pl.ds(r * SIDE * CAP, SIDE * CAP)
            diff = by_tile(conv[g, rows, :]) - mean[None]
            return acc + jnp.sum(diff * diff * by_tile(mask[rows, :]), axis=0)

        squares = squares + lax.fori_loop(0, SIDE, square, zero) * lane_mask(g)
    spread = jnp.broadcast_to(jnp.sum(squares, axis=1, keepdims=True), (CAP, LANES))
    n_tile = member * entries
    n = jnp.sum(n_tile, axis=0, keepdims=True)
    centre = jnp.sum(n_tile * mean, axis=0, keepdims=True) / jnp.maximum(n, 1.0)
    off = mean - centre
    m2 = jnp.sum(member * spread + n_tile * off * off, axis=0, keepdims=True)
    return stack_rows(n, centre, m2)


def split(x):
    high = x.astype(BF16)
    return high, (x - high.astype(F32)).astype(BF16)


def dot3(a, b, lhs_dim, rhs_dim):
    dims = (((lhs_dim,), (rhs_dim,)), ((), ()))
    left = jnp.concatenate([a[0], a[1], a[0]], axis=lhs_dim)
    right = jnp.concatenate([b[0], b[0], b[1]], axis=rhs_dim)
    return lax.dot_general(left, right, dimension_numbers=dims, preferred_element_type=F32)


ERF_P = 0.3275911 * 0.7071067811865476
ERF_A = [0.5 * c for c in (1.061405429, -1.453152027, 1.421413741, -0.284496736, 0.254829592)]


def gelu_parts(x):
    size = jnp.abs(x)
    t = pl.reciprocal(1.0 + ERF_P * size)
    e = jnp.exp(-0.5 * (x * x))
    poly = ERF_A[0]
    for c in ERF_A[1:]:
        poly = poly * t + c
    tail = poly * t * e
    cdf = jnp.where(x < 0.0, tail, 1.0 - tail)
    return x * cdf, cdf + x * (e * 0.3989422804014327)


BLOCK_ROWS = 512
BLOCKS = ROWS // BLOCK_ROWS
HIDDEN_PART = 512


def tile_values(stat_row, member):
    return jnp.broadcast_to(
        jnp.sum(member * stat_row, axis=1, keepdims=True), (CAP, LANES)
    )


def norm_values(stat, member):
    n = stat[0:1]
    variance = stat[2:3] / n
    inv = lax.rsqrt(variance + NORM_EPSILON)
    sample = lax.broadcasted_iota(jnp.int32, (1, LANES), 1) < SAMPLES
    inv = jnp.where(sample, inv, 0.0)
    return tile_values(stat[1:2], member), tile_values(inv, member)


def edge_zero(x, rows, columns):
    row = lax.broadcasted_iota(jnp.int32, x.shape, 0)
    column = lax.broadcasted_iota(jnp.int32, x.shape, 1)
    return jnp.where((row < rows) & (column < columns), x, 0.0)


def dense(
    stat, member, conv, tiles, grad, mask, lanes, bias_in, weights, out, gscaled, dw, vec, hvec
):
    win_hi, win_lo, wout_hi, wout_lo = weights
    mean, inv = norm_values(stat, member)
    line = lambda g, i: lanes[g, i : i + 1, :]
    flat = lambda parts: jnp.concatenate([p.reshape(-1, LANES) for p in parts], axis=1)
    zero = jnp.zeros((CAP, LANES), F32)

    def block(i, carry):
        first, second = carry
        rows = pl.ds(pl.multiple_of(i * BLOCK_ROWS, BLOCK_ROWS), BLOCK_ROWS)
        m = by_tile(mask[rows, :])
        normed = [(by_tile(conv[g, rows, :]) - mean[None]) * inv[None] for g in range(GROUPS)]
        scaled = split(
            flat([normed[g] * line(g, 1)[None] + line(g, 2)[None] for g in range(GROUPS)])
        )
        g_update = [by_tile(grad[g, rows, :]) * m for g in range(GROUPS)]
        g_split = split(flat(g_update))
        update = 0.0
        g_scaled = 0.0
        for h in range(0, HIDDEN_PAD, HIDDEN_PART):
            part = slice(h, h + HIDDEN_PART)
            win = (win_hi[part, :], win_lo[part, :])
            wout = (wout_hi[part, :], wout_lo[part, :])
            pre = dot3(scaled, win, 1, 1) + bias_in[:, part]
            g_hidden = dot3(g_split, wout, 1, 1)
            hidden, slope = gelu_parts(pre)
            hidden = split(hidden)
            g_pre = g_hidden * slope
            hvec[:, part] += jnp.sum(g_pre, axis=0, keepdims=True)
            g_pre = split(g_pre)
            update = update + dot3(hidden, wout, 1, 0)
            g_scaled = g_scaled + dot3(g_pre, win, 1, 0)
            dw[0:256, part] += dot3(scaled, g_pre, 0, 0)
            dw[256:512, part] += dot3(g_split, hidden, 0, 0)
        for g in range(GROUPS):
            span = slice(g * LANES, (g + 1) * LANES)
            value = m * (by_tile(tiles[g, rows, :]) + by_tile(update[:, span] + line(g, 3)))
            out[g, rows, :] = value.reshape(-1, LANES)
            gs = by_tile(g_scaled[:, span])
            gscaled[g, rows, :] = gs.reshape(-1, LANES)
            gain_sum = jnp.sum(gs * normed[g], axis=0)
            bias_sum = jnp.sum(gs, axis=0)
            first = first + bias_sum * line(g, 1)
            second = second + gain_sum * line(g, 1)
            vec[g, 0] += jnp.sum(g_update[g], axis=0)
            vec[g, 1] += gain_sum
            vec[g, 2] += bias_sum
        return first, second

    return lax.fori_loop(0, BLOCKS, block, (zero, zero))


def conv_gradient(stat, sums, member, conv, gscaled, mask, lanes, db):
    mean, inv = norm_values(stat, member)
    sample = lax.broadcasted_iota(jnp.int32, (1, LANES), 1) < SAMPLES
    share = jnp.where(sample, 1.0 / stat[0:1], 0.0)
    first = tile_values(sums[0:1] * share, member)
    second = tile_values(sums[1:2] * share, member)
    for g in range(GROUPS):
        gain = lanes[g, 1:2, :][None]

        def gradient(r, acc):
            rows = pl.ds(r * SIDE * CAP, SIDE * CAP)
            normed = (by_tile(conv[g, rows, :]) - mean[None]) * inv[None]
            g_normed = by_tile(gscaled[g, rows, :]) * gain
            value = (by_tile(mask[rows, :]) * inv[None]) * (
                g_normed - first[None] - normed * second[None]
            )
            gscaled[g, rows, :] = value.reshape(-1, LANES)
            return acc + jnp.sum(value, axis=0)

        db[g] = lax.fori_loop(0, SIDE, gradient, jnp.zeros((CAP, LANES), F32)) * lane_mask(g)


def input_gradient(g, gconv, w, gpad):
    def input_row(r, carry):
        low = jnp.maximum(r - (SIDE - 1), 0)
        high = jnp.minimum(r, KSIZE - 1)

        def tap(a, acc):
            x = by_tile(gconv[g, pl.ds((r - a) * SIDE * CAP, SIDE * CAP), :])
            for b in range(KSIZE):
                part = w[g, a * KSIZE + b][None] * x
                acc = acc[:b] + tuple(acc[b + i] + part[i] for i in range(SIDE)) + acc[b + SIDE :]
            return acc

        acc = lax.fori_loop(
            low, high + 1, tap, tuple(jnp.zeros((CAP, LANES), F32) for _ in range(PAD))
        )
        for i in range(PAD):
            gpad[pl.ds((r * PAD + i) * CAP, CAP), :] = acc[i]
        return carry

    lax.fori_loop(0, PAD, input_row, 0)


def own_gradient(g, gpad, grad, mask):
    def add(r, carry):
        rows = pl.ds(r * SIDE * CAP, SIDE * CAP)
        centre = gpad[pl.ds(((r + RIM) * PAD + RIM) * CAP, SIDE * CAP), :]
        grad[g, rows, :] = grad[g, rows, :] * mask[rows, :] + centre
        return carry

    lax.fori_loop(0, SIDE, add, 0)


def scatter_chunks():
    spans = {-1: (0, SIDE - RIM), 0: (RIM, 0), 1: (RIM + SIDE, 0)}
    order = [(-1, -1), (-1, 0), (-1, 1), (0, -1), (0, 1), (1, -1), (1, 0), (1, 1)]
    chunks = []
    for dr, dc in order:
        dst_r, src_r = spans[dr]
        dst_c, src_c = spans[dc]
        cols = RIM if dc else SIDE
        if dr == 0:
            groups = [range(0, 3), range(3, 8), range(8, 13), range(13, 16)]
        elif dc == 0:
            groups = [[0], [1], [2]]
        else:
            groups = [range(3)]
        chunks.append(
            [
                [
                    ((dst_r + i) * PAD + dst_c, rim_index(src_r + i, src_c), cols)
                    for i in group
                ]
                for group in groups
            ]
        )
    return chunks


CHUNKS = scatter_chunks()
CHUNK = 16
BACK_ROLES = 5


def onehots(near_ref, me, spread):
    size = (BACK_ROLES, CHUNK, CAP, LANES)
    role = lax.broadcasted_iota(jnp.int32, size, 0)
    cell = lax.broadcasted_iota(jnp.int32, size, 1)
    slot = lax.broadcasted_iota(jnp.int32, size, 2)
    lane = lax.broadcasted_iota(jnp.int32, size, 3)
    code = jnp.where(lane // CAP == cell, role * CAP + slot, -1)
    code = code.reshape(BACK_ROLES * LANES, LANES)
    lane = lax.broadcasted_iota(jnp.int32, (1, LANES), 1) % CAP
    for k in range(8):
        wanted = jnp.full((1, LANES), -2, jnp.int32)
        for t in range(CAP):
            n = near_ref[t, k]
            role, slot = place_of(n, me)
            wanted = jnp.where(lane == t, jnp.where(n >= 0, role * CAP + slot, -2), wanted)
        spread[k] = jnp.where(code == wanted, 1.0, 0.0).astype(BF16)


def scatter(g, gpad, spread, pool):
    for k in range(8):
        hot = spread[k]
        hot = jnp.concatenate([hot, hot], axis=1)
        for chunk in CHUNKS[k]:
            parts = [gpad[pl.ds(dst * CAP, cells * CAP), :] for dst, _, cells in chunk]
            used = sum(cells for _, _, cells in chunk)
            if used < CHUNK:
                parts.append(jnp.zeros(((CHUNK - used) * CAP, LANES), F32))
            value = parts[0] if len(parts) == 1 else jnp.concatenate(parts, axis=0)
            value = jnp.concatenate(split(value), axis=0)
            moved = jnp.dot(hot, value, preferred_element_type=F32)
            for role in range(BACK_ROLES):
                first = role * LANES
                for _, rim, cells in chunk:
                    rows = pl.ds(role * RIM_ROWS + rim * CAP, cells * CAP)
                    pool[g][rows, :] = pool[g][rows, :] + moved[first : first + cells * CAP]
                    first += cells * CAP


def weight_gradient(g, padded, gconv, small):
    def weight_row(a, carry):
        def one(r, acc):
            x = by_tile(padded[g, pl.ds((r + a) * PAD * CAP, PAD * CAP), :])
            y = by_tile(gconv[g, pl.ds(r * SIDE * CAP, SIDE * CAP), :])
            return tuple(acc[b] + jnp.sum(x[b : b + SIDE] * y, axis=0) for b in range(KSIZE))

        acc = lax.fori_loop(
            0, SIDE, one, tuple(jnp.zeros((CAP, LANES), F32) for _ in range(KSIZE))
        )
        for b in range(KSIZE):
            small[g, pl.ds(a * KSIZE + b, 1), :] = jnp.sum(acc[b], axis=0, keepdims=True)
        return carry

    lax.fori_loop(0, KSIZE, weight_row, 0)


HALF = 256
SLAB = 16


def block_kernel(
    near_ref, count_ref, sample_ref, x_ref, g_ref, ocean_ref, wt_ref, cb_ref, gain_ref, nbias_ref,
    bout_ref, bin_ref, win_ref, wout_ref,
    native_out, total_out, big_out, small_ref, stat_ref,
    xbuf, gbuf, tiles, grad, mask, pool0, pool1, padded, conv, w, lanes, member, bias_in,
    win_hi, win_lo, wout_hi, wout_lo, dw, vec, hvec, db, gpad, spread, pay, got,
    other, slots, zslots, slab, big, small, tile, sslots, zcslots, inner, outer, partial,
    load_sem, store_sem, send, recv,
):
    pool = (pool0, pool1)
    me = lax.axis_index("tiles")
    core, z, xy = me % 2, (me // 2) % 4, me // INNER
    ahead, behind, partner = halo_peers()
    z_peers = [xy * INNER + ((z + j) % 4) * 2 + core for j in range(1, 4)]
    xy_peers = outer_peers()
    zc_peers = inner_peers()
    ready = greet([ahead, behind, partner] + zc_peers + xy_peers)

    used = [0]
    started = []

    def start(source, target, peer):
        i = used[0]
        used[0] += 1
        copy = remote(source, target, send.at[i], recv.at[i], peer)
        copy.start()
        started.append(copy)
        return copy

    def arrived(copies):
        for copy in copies:
            copy.wait_recv()

    def sent():
        for copy in started:
            copy.wait_send()
        started.clear()

    loads = load_native(x_ref, xbuf, load_sem) + load_native(g_ref, gbuf, load_sem, 4)
    for copy in loads:
        copy.start()
    for half in range(2):
        xbuf[half, pl.ds(2000, 48), :] = jnp.zeros((48, LANES), F32)
        gbuf[half, pl.ds(2000, 48), :] = jnp.zeros((48, LANES), F32)
    for g in range(GROUPS):
        pool[g][pl.ds(5 * RIM_ROWS, RIM_ROWS), :] = jnp.zeros((RIM_ROWS, LANES), F32)

        def clear(i, carry):
            padded[g, pl.ds(i * PAD * CAP, PAD * CAP), :] = jnp.zeros((PAD * CAP, LANES), F32)
            return carry

        lax.fori_loop(0, PAD, clear, 0)
    taps = wt_ref[...]
    taps = jnp.concatenate([taps, jnp.zeros((KSIZE * KSIZE, 6), F32)], axis=1)
    for g in range(GROUPS):
        for k in range(KSIZE * KSIZE):
            w[g, k] = jnp.broadcast_to(
                taps[k : k + 1, g * LANES : (g + 1) * LANES], (CAP, LANES)
            )
    ready()

    out_ahead, out_behind, out_partner = [], [], []
    for p, (g, half) in enumerate(PIECES):
        loads[p].wait()
        to_rows(xbuf, tiles, g, half)
        for first, rim, cells in rim_spans(half):
            pool[g][pl.ds(4 * RIM_ROWS + rim * CAP, cells * CAP), :] = tiles[
                g, pl.ds(first * CAP, cells * CAP), :
            ]
        own = piece(pool, 4, p)
        out_ahead.append(start(own, piece(pool, 1, p), ahead))
        out_behind.append(start(own, piece(pool, 0, p), behind))
        out_partner.append(start(own, piece(pool, 3, p), partner))

    for i, ref in enumerate((cb_ref, gain_ref, nbias_ref, bout_ref)):
        line = jnp.concatenate([ref[...], jnp.zeros((1, 6), F32)], axis=1)
        for g in range(GROUPS):
            lanes[g, i : i + 1, :] = line[:, g * LANES : (g + 1) * LANES]
    bias_in[...] = jnp.concatenate([bin_ref[...], jnp.zeros((1, 24), F32)], axis=1)
    row = lax.broadcasted_iota(jnp.int32, (CAP, LANES), 0)
    lane = lax.broadcasted_iota(jnp.int32, (CAP, LANES), 1)
    sample = jnp.zeros((CAP, LANES), jnp.int32)
    for t in range(CAP):
        sample = jnp.where(row == t, sample_ref[t], sample)
    member[...] = (sample == lane).astype(F32)
    for g in range(GROUPS):

        def centre(r, carry):
            padded[g, pl.ds(((r + RIM) * PAD + RIM) * CAP, SIDE * CAP), :] = tiles[
                g, pl.ds(r * SIDE * CAP, SIDE * CAP), :
            ]
            return carry

        lax.fori_loop(0, SIDE, centre, 0)
    for p, (g, half) in enumerate(PIECES):
        loads[4 + p].wait()
        to_rows(gbuf, grad, g, half)
    slot = lax.broadcasted_iota(jnp.int32, (CAP, CELLS), 0)
    ocean = jnp.where(slot < count_ref[0], ocean_ref[...].astype(F32), 0.0)
    for half in range(2):
        for t in range(CAP):
            mask[pl.ds(half * 1024 + t, LANES, stride=CAP), :] = jnp.broadcast_to(
                ocean[t : t + 1, half * LANES : (half + 1) * LANES], (LANES, LANES)
            ).T
    own_conv(0, padded, conv, w, lanes)
    passed = []

    def pass_on(p):
        out_ahead[p].wait_recv()
        passed.append(start(piece(pool, 1, p), piece(pool, 2, p), partner))

    pass_on(0)
    own_conv(1, padded, conv, w, lanes)
    pass_on(1)
    win_hi[...], win_lo[...] = split(edge_zero(win_ref[...], 1000, 250))
    wout_hi[...], wout_lo[...] = split(edge_zero(wout_ref[...], 1000, 250))
    onehots(near_ref, me, spread)
    for ref in (dw, vec, hvec):
        ref[...] = jnp.zeros_like(ref)
    sums = []
    for g in range(GROUPS):
        if g == 1:
            pass_on(2)
            pass_on(3)
        for copies in (out_behind, out_partner, passed):
            arrived(copies[2 * g : 2 * g + 2])
        gather(g, near_ref, me, pool, padded)
        halo_conv(g, padded, conv, w)
        sums.append(masked_sum(g, conv, mask))

    def reduce_vector(i, vector, merge, between):
        partial[i] = vector
        copies = exchange_start(
            partial.at[i], send, recv, inner.at[i], used[0], me % INNER, zc_peers
        )
        used[0] += INNER - 1
        between()
        for copy in copies:
            copy.wait()
        partial[2 + i] = merge(inner[i])
        copies = exchange_start(
            partial.at[2 + i], send, recv, outer.at[i], used[0], xy, xy_peers
        )
        used[0] += OUTER - 1
        for copy in copies:
            copy.wait()
        return merge(outer[i])

    stats = local_stats(sums[0][0] + sums[1][0], sums[0][1], conv, mask, member[...])
    stat_ref[...] = reduce_vector(0, stats, merge_stats, sent)

    def clear_pool():
        for g in range(GROUPS):

            def zero(i, carry):
                pool[g][pl.ds(i * HALF_RIM, HALF_RIM), :] = jnp.zeros((HALF_RIM, LANES), F32)
                return carry

            lax.fori_loop(0, 2 * BACK_ROLES, zero, 0)

    first, second = dense(
        stat_ref[...], member[...], conv, tiles, grad, mask, lanes, bias_in,
        (win_hi, win_lo, wout_hi, wout_lo), tiles, gbuf, dw, vec, hvec,
    )
    theirs = pl.multiple_of((1 - core) * HALF, HALF)
    mine = pl.multiple_of(core * HALF, HALF)
    halves = start(dw.at[pl.ds(theirs, HALF), :], other, partner)
    rows = [
        jnp.sum(member[...] * jnp.sum(x, axis=1, keepdims=True), axis=0, keepdims=True)
        for x in (first, second)
    ]
    scattered = []

    def scatter_weights():
        halves.wait_recv()
        dw[pl.ds(mine, HALF), :] = dw[pl.ds(mine, HALF), :] + other[...]
        for peer in xy_peers:
            at = pl.multiple_of(core * HALF + (peer // INNER) * SLAB, SLAB)
            scattered.append(start(dw.at[pl.ds(at, SLAB), :], slots.at[xy], peer))
        slots[xy] = dw[pl.ds(pl.multiple_of(core * HALF + xy * SLAB, SLAB), SLAB), :]
        clear_pool()

    sums = reduce_vector(1, stack_rows(*rows), merge_sums, scatter_weights)
    conv_gradient(stat_ref[...], sums, member[...], conv, gbuf, mask, lanes, db)

    payload, direct, near, merged = [], [], [], []

    def part_of(ref, p):
        g, part = PIECES[p]
        return ref.at[g, pl.ds(part * HALF_RIM, HALF_RIM), :]

    def on_chip(p):
        payload.append(start(piece(pool, 2, p), part_of(pay, p), partner))
        near.append(start(piece(pool, 3, p), part_of(got.at[2], p), partner))

    def off_chip(p):
        direct.append(start(piece(pool, 0, p), part_of(got.at[0], p), ahead))
        payload[p].wait_recv()
        g, part = PIECES[p]
        at = pl.ds(RIM_ROWS + part * HALF_RIM, HALF_RIM)
        pool[g][at, :] = pool[g][at, :] + pay[g, pl.ds(part * HALF_RIM, HALF_RIM), :]
        merged.append(start(piece(pool, 1, p), part_of(got.at[1], p), behind))

    input_gradient(0, gbuf, w, gpad)
    own_gradient(0, gpad, grad, mask)
    scatter(0, gpad, spread, pool)
    on_chip(0)
    on_chip(1)
    arrived(scattered)
    slab[...] = jnp.sum(slots[...], axis=0)
    z_gathered = [start(slab, zslots.at[z], peer) for peer in z_peers]
    zslots[z] = slab[...]
    off_chip(0)
    off_chip(1)
    input_gradient(1, gbuf, w, gpad)
    own_gradient(1, gpad, grad, mask)
    scatter(1, gpad, spread, pool)
    on_chip(2)
    on_chip(3)
    off_chip(2)
    arrived(z_gathered)
    big_rows = pl.ds(pl.multiple_of(core * HALF + xy * SLAB, SLAB), SLAB)
    big[big_rows, :] = jnp.sum(zslots[...], axis=0)
    own = big.at[big_rows, :]
    xy_gathered = [start(own, own, peer) for peer in xy_peers]

    for g in range(GROUPS):
        weight_gradient(g, padded, gbuf, small)
        lines = [jnp.sum(db[g], axis=0, keepdims=True)]
        lines += [jnp.sum(vec[g, i], axis=0, keepdims=True) for i in range(3)]
        lines += [hvec[0:1, pl.ds((g * 4 + i) * LANES, LANES)] for i in range(4)]
        for i, line in enumerate(lines):
            small[g, pl.ds(49 + i, 1), :] = line
        small[g, pl.ds(57, 7), :] = jnp.zeros((7, LANES), F32)
    small_tile = lambda q: small.at[q // 8, pl.ds(pl.multiple_of((q % 8) * CAP, CAP), CAP), :]
    small_scattered = [start(small_tile(peer // INNER), sslots.at[xy], peer) for peer in xy_peers]
    sslots[xy] = small[xy // 8, pl.ds(pl.multiple_of((xy % 8) * CAP, CAP), CAP), :]
    stores = store_native(xbuf, native_out, store_sem)
    for p in range(2):
        from_rows(tiles, xbuf, *PIECES[p])
        stores[p].start()
    arrived(small_scattered)
    tile[...] = jnp.sum(sslots[...], axis=0)
    zc_gathered = [start(tile, zcslots.at[me % INNER], peer) for peer in zc_peers]
    zcslots[me % INNER] = tile[...]
    off_chip(3)
    for p in range(2, 4):
        from_rows(tiles, xbuf, *PIECES[p])
        stores[p].start()
    arrived(xy_gathered)
    own = big.at[pl.ds(mine, HALF), :]
    crossed = start(own, own, partner)
    arrived(zc_gathered)
    small_ref[xy] = jnp.sum(zcslots[...], axis=0)
    small_gathered = [start(small_ref.at[xy], small_ref.at[xy], peer) for peer in xy_peers]
    crossed.wait_recv()
    stores.append(pltpu.make_async_copy(big, big_out, store_sem.at[4]))
    stores[4].start()
    for p, (g, half) in enumerate(PIECES):
        arrived([near[p], direct[p], merged[p]])
        for first, rim, cells in rim_spans(half):
            rows = pl.ds(first * CAP, cells * CAP)
            span = pl.ds(rim * CAP, cells * CAP)
            mine_at = pl.ds(4 * RIM_ROWS + rim * CAP, cells * CAP)
            grad[g, rows, :] = (grad[g, rows, :] + pool[g][mine_at, :]) + (
                got[2, g, span, :] + (got[0, g, span, :] + got[1, g, span, :])
            )
        rows = pl.ds(half * 1024, 1024)
        stores.append(
            pltpu.make_async_copy(grad.at[g, rows, :], total_out.at[g, rows, :], store_sem.at[5 + p])
        )
        stores[-1].start()
    arrived(small_gathered)
    sent()
    for copy in stores:
        copy.wait()


def block(near, count, sample, x, g, ocean, wt, cb, gain, nbias, bout, bin_, win, wout):
    rows = (GROUPS, ROWS, LANES)
    rim = (GROUPS, RIM_ROWS, LANES)
    vector = (CAP, LANES)
    weight = pltpu.VMEM((HIDDEN_PAD, 256), BF16)
    copies = 16 + 2 * (INNER + OUTER - 2) + 1 + 15 + 16 + 3 + 15 + 15 + 7 + 1 + 15
    weight_block = pl.BlockSpec((HIDDEN_PAD, 256), lambda i: (0, 0))
    return pl.pallas_call(
        block_kernel,
        grid=(1,),
        in_specs=[SMEM_SPEC] * 3 + [ANY_SPEC] * 2 + [VMEM_SPEC] * 7 + [weight_block] * 2,
        out_specs=(ANY_SPEC,) * 3 + (VMEM_SPEC,) * 2,
        out_shape=(
            shape(2000, 256), shape(*rows), shape(512, HIDDEN_PAD), shape(16, *vector),
            shape(*vector),
        ),
        scratch_shapes=[
            buffer(*rows), buffer(*rows), buffer(*rows), buffer(*rows),
            buffer(ROWS, LANES), buffer(ROLES * RIM_ROWS, LANES), buffer(ROLES * RIM_ROWS, LANES),
            buffer(GROUPS, PAD * PAD * CAP, LANES), buffer(*rows),
            buffer(GROUPS, KSIZE * KSIZE, CAP, LANES), buffer(GROUPS, *vector),
            buffer(*vector), buffer(1, HIDDEN_PAD), weight, weight, weight, weight,
            buffer(512, HIDDEN_PAD), buffer(GROUPS, 3, *vector), buffer(1, HIDDEN_PAD),
            buffer(GROUPS, *vector), buffer(PAD * PAD * CAP, LANES),
            pltpu.VMEM((8, BACK_ROLES * LANES, LANES), BF16), buffer(*rim), buffer(3, *rim),
            buffer(HALF, HIDDEN_PAD), buffer(OUTER, SLAB, HIDDEN_PAD),
            buffer(4, SLAB, HIDDEN_PAD), buffer(SLAB, HIDDEN_PAD), buffer(512, HIDDEN_PAD),
            buffer(GROUPS, 64, LANES), buffer(*vector), buffer(OUTER, *vector),
            buffer(INNER, *vector), buffer(2, INNER, *vector), buffer(2, OUTER, *vector),
            buffer(4, *vector), semaphores(8), semaphores(9), semaphores(copies),
            semaphores(copies),
        ],
        compiler_params=params(collective_id=1, has_side_effects=True),
        name="block",
    )(near, count, sample, x, g, ocean, wt, cb, gain, nbias, bout, bin_, win, wout)


def final_kernel(
    total_ref, native_ref, big_ref, small_ref, stat_ref,
    out_ref, tiles_ref, dwin_ref, dwout_ref, dconv_ref, lines_ref, hline_ref,
    total, buf, through, big, load_sem, store_sem,
):
    loads = [
        pltpu.make_async_copy(
            total_ref.at[g, pl.ds(half * 1024, 1024), :],
            total.at[g, pl.ds(half * 1024, 1024), :],
            load_sem.at[p],
        )
        for p, (g, half) in enumerate(PIECES)
    ]
    loads.append(pltpu.make_async_copy(big_ref, big, load_sem.at[4]))
    loads.append(pltpu.make_async_copy(native_ref, through, load_sem.at[5]))
    for copy in loads:
        copy.start()
    stores = store_native(buf, tiles_ref, store_sem)
    for p, (g, half) in enumerate(PIECES):
        loads[p].wait()
        from_rows(total, buf, g, half)
        stores[p].start()
    loads[5].wait()
    stores.append(pltpu.make_async_copy(through, out_ref, store_sem.at[4]))
    stores[4].start()
    sample = lax.broadcasted_iota(jnp.int32, (1, LANES), 1) < SAMPLES
    cells = jnp.sum(jnp.where(sample, stat_ref[0:1, :], 0.0), axis=1, keepdims=True)
    share = 250.0 / cells
    loads[4].wait()
    dwin_ref[...] = big[0:256, :].T[:1000, :250] * share
    dwout_ref[...] = big[256:512, :].T[:1000, :250] * share
    flat = [
        jnp.concatenate([small_ref[g * 8 + i] for i in range(8)], axis=0) * share
        for g in range(GROUPS)
    ]
    flat = jnp.concatenate(flat, axis=1)
    dconv_ref[...] = flat[0:49, :250]
    lines_ref[...] = flat[48:56, :250]
    for g in range(GROUPS):
        for i in range(4):
            j = 53 + i
            hline_ref[0:1, pl.ds((g * 4 + i) * LANES, LANES)] = (
                flat[j : j + 1, g * LANES : (g + 1) * LANES]
            )
    for copy in stores:
        copy.wait()


def final(total, out, big, small, stat):
    return pl.pallas_call(
        final_kernel,
        in_specs=[ANY_SPEC] * 3 + [VMEM_SPEC] * 2,
        out_specs=(ANY_SPEC,) * 2 + (VMEM_SPEC,) * 5,
        out_shape=(
            shape(2000, 256), shape(2000, 256), shape(1000, 250), shape(1000, 250),
            shape(49, 250), shape(8, 250), shape(1, HIDDEN_PAD),
        ),
        scratch_shapes=[
            buffer(GROUPS, ROWS, LANES), buffer(GROUPS, ROWS, LANES), buffer(2000, 256),
            buffer(512, HIDDEN_PAD), semaphores(6), semaphores(5),
        ],
        compiler_params=params(),
        name="final",
    )(total, out, big, small, stat)


def native(x):
    return jnp.transpose(x, (1, 0, 2)).reshape(2000, CELLS)


def from_native(x):
    return jnp.transpose(x.reshape(250, CAP, CELLS), (1, 0, 2))


def local(
    tiles_in, conv_weight, conv_bias, norm_gain, norm_bias, weight_in, bias_in,
    weight_out, bias_out, grad_out, tile_counts, ocean_mask, neighbours, sample_ids,
):
    out, total, big, small, stat = block(
        neighbours, tile_counts, sample_ids, native(tiles_in), native(grad_out), ocean_mask,
        conv_weight.T, conv_bias[None], norm_gain[None], norm_bias[None], bias_out[None],
        bias_in[None], weight_in.T, weight_out,
    )
    output, grad_tiles, dwin, dwout, dconv, lines, hline = final(total, out, big, small, stat)
    return (
        from_native(output),
        from_native(grad_tiles),
        dconv.T,
        lines[1],
        lines[3],
        lines[4],
        dwin.T,
        hline[0, :1000],
        dwout,
        lines[2],
    )


def solution(mesh):
    tiles = P("tiles")
    whole = P()
    return jax.shard_map(
        local,
        mesh=mesh,
        in_specs=(tiles,) + (whole,) * 8 + (tiles,) * 5,
        out_specs=(tiles, tiles) + (whole,) * 8,
        check_vma=False,
    )
```

time: 969 us -> 176 us (0.18); the launches traced: 958 us -> 175 us
  blocking collectives: 301 us -> 0 us
  other arithmetic: 241 us -> 0 us
  Pallas kernels: 0 us -> 173 us
  local copies, waits for them, and re-layouts: 142 us -> 1.42 us
  matrix products: 118 us -> 0 us
  waiting for transfers between devices: 114 us -> 0 us
  starting transfers between devices: 25.2 us -> 0 us
  between operations: 17 us -> 1.31 us
    psum x4 -> x0, blocking collectives: 301 us -> none  [the longest x1 107 us: local(): lax.psum((g_conv_weight, g_conv_bias, g_gain, g_nbias, g_weight_in, g_bia...]
    pallas_call x0 -> x2, Pallas kernels: none -> 173 us  [the longest x1 166 us: block(): pl.pallas_call(block_kernel, grid=(1,), in_specs=[SMEM_SPEC] * 3 + [ANY_S...]
    dot_general x16 -> x0, matrix products: 118 us -> none  [the longest x3 68.8 us: dense_branch(): jnp.einsum('hc,thp->tcp', weight_out, hidden, precision=HIGHEST_PRECISION)]
    add_any x5 -> x0, other arithmetic: 113 us -> none  [the longest x2 85.9 us: depthwise(): flat_tiles[:, :, anchor:anchor + out_span]]
    psum x1 -> x0, waiting for transfers between devices: 65.8 us -> none  [local(): lax.psum((g_conv_weight, g_conv_bias, g_gain, g_nbias, g_weight_in, g_bia...]
    mul x6 -> x0, other arithmetic: 51.3 us -> none  [the longest x3 44 us: depthwise(): conv_weight[:, row_step * KSIZE + col_step][None, :, None]]
    ppermute x8 -> x0, waiting for transfers between devices: 48.2 us -> none  [passed_along(): return lax.ppermute(block, axis, route)]
    reduce_sum x9 -> x0, other arithmetic: 33.2 us -> none  [the longest x3 22 us: depthwise(): conv_weight[:, row_step * KSIZE + col_step][None, :, None]]
  transfers between devices with their start and end apart: 9 -> 0, of which waited for: 4 -> 0; matrix products, arithmetic and copies ran while one was open for 6% -> 0% of each run, Pallas kernels for 0% -> 0%
where the time goes in v3:
time: 176 us; the launch traced here: 175 us
  Pallas kernels  173 us (98%)
    pallas_call x1, Pallas kernels, block(): pl.pallas_call(block_kernel, grid=(1,), in_specs=[SMEM_SPEC] * 3 + [ANY_S...  166 us
    pallas_call x1, Pallas kernels, final(): pl.pallas_call(final_kernel, in_specs=[ANY_SPEC] * 3 + [VMEM_SPEC] * 2, o...  7.14 us

profile of v3, /device:TPU:1, one launch (start us, length us, event | category | flops | bytes accessed | tf_op | source)
XLA Modules:
  0.0 175.4 jit_solution(2864778859797103139)
XLA Ops:
  1.3 165.5 %block.1 = (f32[2000,256]{1,0:T(8,128)}, f32[2,2048,128]{2,1,0:T(8,128)}, f32[512,1024]{1,0:T(8,128)}, f32[16,8,128]{2,1,0:T(8,128)}, f32[8,128]{1,0:T(8,128)}) custom-call(s32[8,8]{1,0:T(8,128)} %near_ref.1, s32[1]{0:T(128)S(6)} %copy.24.count_ref, s32[8]{0:T(128)} %sample_ref.1, f32[2000,256]{1,0:T(8,128)} %bitcast.27, f32[2000,256]{1,0:T(8,128)} %bitcast.28, ...), custom_call_target="tpu_custom_call" | custom-call | tf_op jit(solution)/shard_map/block/pallas_call | solution.py:896
  166.8 7.1 %final.1 = (f32[2000,256]{1,0:T(8,128)}, f32[2000,256]{1,0:T(8,128)}, f32[1000,250]{1,0:T(8,128)}, f32[1000,250]{1,0:T(8,128)}, f32[49,250]{1,0:T(8,128)}, /*index=5*/f32[8,250]{1,0:T(8,128)}, f32[1,1024]{1,0:T(1,128)}) custom-call(f32[2,2048,128]{2,1,0:T(8,128)} %get-tuple-element.22.total_ref, f32[2000,256]{1,0:T(8,128)} %get-tuple-element.23.native_ref, ...), custom_call_target="tpu_custom_call" | custom-call | tf_op jit(solution)/shard_map/final/pallas_call | solution.py:975
  174.0 1.4 fusion

commit v4 on v3

--- a/solution.py
+++ b/solution.py
@@ -31,7 +31,7 @@
 ANY_SPEC = pl.BlockSpec(memory_space=pl.ANY)
 
 
-def params(mib=60, **more):
+def params(mib=62, **more):
     return pltpu.CompilerParams(vmem_limit_bytes=mib * MIB, **more)
 
 
@@ -333,10 +333,13 @@
     return lax.fori_loop(0, SIDE, add, (zero, zero))
 
 
-def local_stats(sums, cells, conv, mask, member):
+def tile_average(sums, cells):
+    total = jnp.broadcast_to(jnp.sum(sums, axis=1, keepdims=True), (CAP, LANES))
+    return total / jnp.maximum(250.0 * cells, 1.0)
+
+
+def local_stats(mean, cells, conv, mask, member):
     entries = 250.0 * cells
-    total = jnp.broadcast_to(jnp.sum(sums, axis=1, keepdims=True), (CAP, LANES))
-    mean = total / jnp.maximum(entries, 1.0)
     zero = jnp.zeros((CAP, LANES), F32)
     squares = zero
     for g in range(GROUPS):
@@ -404,64 +407,145 @@
     return tile_values(stat[1:2], member), tile_values(inv, member)
 
 
-def edge_zero(x, rows, columns):
-    row = lax.broadcasted_iota(jnp.int32, x.shape, 0)
-    column = lax.broadcasted_iota(jnp.int32, x.shape, 1)
-    return jnp.where((row < rows) & (column < columns), x, 0.0)
-
-
-def dense(
-    stat, member, conv, tiles, grad, mask, lanes, bias_in, weights, out, gscaled, dw, vec, hvec
+HIDDEN_CHUNKS = HIDDEN_PAD // LANES
+
+
+def wide(x, parts):
+    return jnp.concatenate([x] * parts, axis=1)
+
+
+def flat(parts):
+    return jnp.concatenate([p.reshape(-1, LANES) for p in parts], axis=1)
+
+
+def block_rows(i):
+    return pl.ds(pl.multiple_of(i * BLOCK_ROWS, BLOCK_ROWS), BLOCK_ROWS)
+
+
+def hidden_gradient(grad, mask, wout, update_hi, update_lo, back, vec):
+    def block(i, carry):
+        rows = block_rows(i)
+        m = by_tile(mask[rows, :])
+        g_update = [by_tile(grad[g, rows, :]) * m for g in range(GROUPS)]
+        for g in range(GROUPS):
+            vec[g, 0] += jnp.sum(g_update[g], axis=0)
+        update_hi[rows, :], update_lo[rows, :] = split(flat(g_update))
+        operand = (update_hi[rows, :], update_lo[rows, :])
+        for h in range(0, HIDDEN_PAD, HIDDEN_PART):
+            part = slice(h, h + HIDDEN_PART)
+            back[rows, part] = dot3(operand, (wout[0][part, :], wout[1][part, :]), 1, 1)
+        return carry
+
+    lax.fori_loop(0, BLOCKS, block, 0)
+
+
+def centred_product(low, high, tile_mean, conv, lanes, win, ahead):
+    def block(i, carry):
+        rows = block_rows(i)
+        operand = split(
+            flat(
+                [
+                    (by_tile(conv[g, rows, :]) - tile_mean[None]) * lanes[g, 1:2, :][None]
+                    for g in range(GROUPS)
+                ]
+            )
+        )
+        for h in range(0, HIDDEN_PAD, HIDDEN_PART):
+            part = slice(h, h + HIDDEN_PART)
+            value = dot3(operand, (win[0][part, :], win[1][part, :]), 1, 1)
+            for c in range(HIDDEN_PART // LANES):
+                ahead[h // LANES + c, rows, :] = value[:, c * LANES : (c + 1) * LANES]
+        return carry
+
+    lax.fori_loop(low, high, block, 0)
+
+
+def scaled_operand(stat, member, conv, lanes, scaled_hi, scaled_lo):
+    mean, inv = norm_values(stat, member)
+
+    def block(i, carry):
+        rows = block_rows(i)
+        scaled_hi[rows, :], scaled_lo[rows, :] = split(
+            flat(
+                [
+                    (by_tile(conv[g, rows, :]) - mean[None]) * inv[None] * lanes[g, 1:2, :][None]
+                    + lanes[g, 2:3, :][None]
+                    for g in range(GROUPS)
+                ]
+            )
+        )
+        return carry
+
+    lax.fori_loop(0, BLOCKS, block, 0)
+
+
+def dense_part(
+    h, low, high, stat, member, tile_mean, lines, weights, scaled, update, ahead, back, tiles,
+    gscaled, dw, hvec,
 ):
     win_hi, win_lo, wout_hi, wout_lo = weights
     mean, inv = norm_values(stat, member)
-    line = lambda g, i: lanes[g, i : i + 1, :]
-    flat = lambda parts: jnp.concatenate([p.reshape(-1, LANES) for p in parts], axis=1)
-    zero = jnp.zeros((CAP, LANES), F32)
+    part = slice(h, h + HIDDEN_PART)
+    count = HIDDEN_PART // LANES
+    win = (win_hi[part, :], win_lo[part, :])
+    wout = (wout_hi[part, :], wout_lo[part, :])
+    offset = lines[1:2, part] + wide((tile_mean - mean) * inv, count) * lines[0:1, part]
+    inv = wide(inv, count)
 
     def block(i, carry):
-        first, second = carry
-        rows = pl.ds(pl.multiple_of(i * BLOCK_ROWS, BLOCK_ROWS), BLOCK_ROWS)
-        m = by_tile(mask[rows, :])
-        normed = [(by_tile(conv[g, rows, :]) - mean[None]) * inv[None] for g in range(GROUPS)]
-        scaled = split(
-            flat([normed[g] * line(g, 1)[None] + line(g, 2)[None] for g in range(GROUPS)])
-        )
-        g_update = [by_tile(grad[g, rows, :]) * m for g in range(GROUPS)]
-        g_split = split(flat(g_update))
-        update = 0.0
-        g_scaled = 0.0
-        for h in range(0, HIDDEN_PAD, HIDDEN_PART):
-            part = slice(h, h + HIDDEN_PART)
-            win = (win_hi[part, :], win_lo[part, :])
-            wout = (wout_hi[part, :], wout_lo[part, :])
-            pre = dot3(scaled, win, 1, 1) + bias_in[:, part]
-            g_hidden = dot3(g_split, wout, 1, 1)
-            hidden, slope = gelu_parts(pre)
-            hidden = split(hidden)
-            g_pre = g_hidden * slope
-            hvec[:, part] += jnp.sum(g_pre, axis=0, keepdims=True)
-            g_pre = split(g_pre)
-            update = update + dot3(hidden, wout, 1, 0)
-            g_scaled = g_scaled + dot3(g_pre, win, 1, 0)
-            dw[0:256, part] += dot3(scaled, g_pre, 0, 0)
-            dw[256:512, part] += dot3(g_split, hidden, 0, 0)
+        rows = block_rows(i)
+        pre = jnp.concatenate([ahead[h // LANES + c, rows, :] for c in range(count)], axis=1)
+        pre = pre.reshape(-1, CAP, HIDDEN_PART) * inv[None] + offset[None]
+        hidden, slope = gelu_parts(pre.reshape(-1, HIDDEN_PART))
+        hidden = split(hidden)
+        g_pre = back[rows, part] * slope
+        hvec[:, part] += jnp.sum(g_pre, axis=0, keepdims=True)
+        g_pre = split(g_pre)
+        dw[0:256, part] += dot3((scaled[0][rows, :], scaled[1][rows, :]), g_pre, 0, 0)
+        dw[256:512, part] += dot3((update[0][rows, :], update[1][rows, :]), hidden, 0, 0)
+        value = dot3(hidden, wout, 1, 0)
+        g_scaled = dot3(g_pre, win, 1, 0)
         for g in range(GROUPS):
             span = slice(g * LANES, (g + 1) * LANES)
-            value = m * (by_tile(tiles[g, rows, :]) + by_tile(update[:, span] + line(g, 3)))
-            out[g, rows, :] = value.reshape(-1, LANES)
-            gs = by_tile(g_scaled[:, span])
-            gscaled[g, rows, :] = gs.reshape(-1, LANES)
-            gain_sum = jnp.sum(gs * normed[g], axis=0)
-            bias_sum = jnp.sum(gs, axis=0)
-            first = first + bias_sum * line(g, 1)
-            second = second + gain_sum * line(g, 1)
-            vec[g, 0] += jnp.sum(g_update[g], axis=0)
-            vec[g, 1] += gain_sum
-            vec[g, 2] += bias_sum
-        return first, second
-
-    return lax.fori_loop(0, BLOCKS, block, (zero, zero))
+            tiles[g, rows, :] += value[:, span]
+            if h == 0:
+                gscaled[g, rows, :] = g_scaled[:, span]
+            else:
+                gscaled[g, rows, :] += g_scaled[:, span]
+        return carry
+
+    lax.fori_loop(low, high, block, 0)
+
+
+def scaled_sums(stat, member, conv, gscaled, lanes, vec):
+    mean, inv = norm_values(stat, member)
+    zero = jnp.zeros((CAP, LANES), F32)
+    first, second = zero, zero
+    for g in range(GROUPS):
+
+        def add(r, carry):
+            rows = pl.ds(r * SIDE * CAP, SIDE * CAP)
+            gs = by_tile(gscaled[g, rows, :])
+            normed = (by_tile(conv[g, rows, :]) - mean[None]) * inv[None]
+            return carry[0] + jnp.sum(gs, axis=0), carry[1] + jnp.sum(gs * normed, axis=0)
+
+        bias_sum, gain_sum = lax.fori_loop(0, SIDE, add, (zero, zero))
+        vec[g, 1] = gain_sum
+        vec[g, 2] = bias_sum
+        first = first + bias_sum * lanes[g, 1:2, :]
+        second = second + gain_sum * lanes[g, 1:2, :]
+    return first, second
+
+
+def finish_output(p, tiles, mask, lanes):
+    g, half = PIECES[p]
+
+    def finish(r, carry):
+        rows = pl.ds(r * SIDE * CAP, SIDE * CAP)
+        tiles[g, rows, :] = mask[rows, :] * (tiles[g, rows, :] + lanes[g, 3:4, :])
+        return carry
+
+    lax.fori_loop(half * 8, half * 8 + 8, finish, 0)
 
 
 def conv_gradient(stat, sums, member, conv, gscaled, mask, lanes, db):
@@ -605,23 +689,25 @@
 
 
 HALF = 256
-SLAB = 16
 
 
 def block_kernel(
-    near_ref, count_ref, sample_ref, x_ref, g_ref, ocean_ref, wt_ref, cb_ref, gain_ref, nbias_ref,
-    bout_ref, bin_ref, win_ref, wout_ref,
+    near_ref, count_ref, sample_ref, x_ref, g_ref, win_ref, wout_ref, ocean_ref, wt_ref, cb_ref,
+    gain_ref, nbias_ref, bout_ref, bin_ref,
     native_out, total_out, big_out, small_ref, stat_ref,
-    xbuf, gbuf, tiles, grad, mask, pool0, pool1, padded, conv, w, lanes, member, bias_in,
-    win_hi, win_lo, wout_hi, wout_lo, dw, vec, hvec, db, gpad, spread, pay, got,
-    other, slots, zslots, slab, big, small, tile, sslots, zcslots, inner, outer, partial,
-    load_sem, store_sem, send, recv,
+    xbuf, gbuf, tiles, grad, mask, pool0, pool1, padded, conv, w, lanes, member,
+    weight_buf, win_hi, win_lo, wout_hi, wout_lo, update_hi, update_lo, scaled_hi, scaled_lo,
+    back, arena, dw, vec, hvec, db, gpad, spread,
+    other, slots1, sum1, slots2, sum2, zslots, big, small, tile, sslots, zcslots,
+    inner, outer, partial, load_sem, store_sem, send, recv,
 ):
     pool = (pool0, pool1)
     me = lax.axis_index("tiles")
-    core, z, xy = me % 2, (me // 2) % 4, me // INNER
+    core, z, x, y, xy = me % 2, (me // 2) % 4, (me // INNER) % 4, me // 32, me // INNER
     ahead, behind, partner = halo_peers()
-    z_peers = [xy * INNER + ((z + j) % 4) * 2 + core for j in range(1, 4)]
+    z_peers = [me + (((z + j) % 4) - z) * 2 for j in range(1, 4)]
+    x_peers = [me + (((x + j) % 4) - x) * INNER for j in range(1, 4)]
+    y_peers = [me + (((y + j) % 4) - y) * 32 for j in range(1, 4)]
     xy_peers = outer_peers()
     zc_peers = inner_peers()
     ready = greet([ahead, behind, partner] + zc_peers + xy_peers)
@@ -647,19 +733,29 @@
         started.clear()
 
     loads = load_native(x_ref, xbuf, load_sem) + load_native(g_ref, gbuf, load_sem, 4)
+    loads.append(pltpu.make_async_copy(win_ref, weight_buf.at[0], load_sem.at[8]))
+    loads.append(pltpu.make_async_copy(wout_ref, weight_buf.at[1], load_sem.at[9]))
     for copy in loads:
         copy.start()
     for half in range(2):
         xbuf[half, pl.ds(2000, 48), :] = jnp.zeros((48, LANES), F32)
         gbuf[half, pl.ds(2000, 48), :] = jnp.zeros((48, LANES), F32)
-    for g in range(GROUPS):
-        pool[g][pl.ds(5 * RIM_ROWS, RIM_ROWS), :] = jnp.zeros((RIM_ROWS, LANES), F32)
-
-        def clear(i, carry):
-            padded[g, pl.ds(i * PAD * CAP, PAD * CAP), :] = jnp.zeros((PAD * CAP, LANES), F32)
-            return carry
-
-        lax.fori_loop(0, PAD, clear, 0)
+    for p, (g, half) in enumerate(PIECES):
+        loads[p].wait()
+        to_rows(xbuf, tiles, g, half)
+        for first, rim, cells in rim_spans(half):
+            pool[g][pl.ds(4 * RIM_ROWS + rim * CAP, cells * CAP), :] = tiles[
+                g, pl.ds(first * CAP, cells * CAP), :
+            ]
+    ready()
+
+    out_ahead, out_behind, out_partner = [], [], []
+    for p in range(4):
+        own = piece(pool, 4, p)
+        out_ahead.append(start(own, piece(pool, 1, p), ahead))
+        out_behind.append(start(own, piece(pool, 0, p), behind))
+        out_partner.append(start(own, piece(pool, 3, p), partner))
+
     taps = wt_ref[...]
     taps = jnp.concatenate([taps, jnp.zeros((KSIZE * KSIZE, 6), F32)], axis=1)
     for g in range(GROUPS):
@@ -667,41 +763,44 @@
             w[g, k] = jnp.broadcast_to(
                 taps[k : k + 1, g * LANES : (g + 1) * LANES], (CAP, LANES)
             )
-    ready()
-
-    out_ahead, out_behind, out_partner = [], [], []
-    for p, (g, half) in enumerate(PIECES):
-        loads[p].wait()
-        to_rows(xbuf, tiles, g, half)
-        for first, rim, cells in rim_spans(half):
-            pool[g][pl.ds(4 * RIM_ROWS + rim * CAP, cells * CAP), :] = tiles[
-                g, pl.ds(first * CAP, cells * CAP), :
+    for g in range(GROUPS):
+        pool[g][pl.ds(5 * RIM_ROWS, RIM_ROWS), :] = jnp.zeros((RIM_ROWS, LANES), F32)
+
+        def clear(i, carry):
+            padded[g, pl.ds(i * PAD * CAP, PAD * CAP), :] = jnp.zeros((PAD * CAP, LANES), F32)
+            return carry
+
+        lax.fori_loop(0, PAD, clear, 0)
+
+        def centre(r, carry):
+            padded[g, pl.ds(((r + RIM) * PAD + RIM) * CAP, SIDE * CAP), :] = tiles[
+                g, pl.ds(r * SIDE * CAP, SIDE * CAP), :
             ]
-        own = piece(pool, 4, p)
-        out_ahead.append(start(own, piece(pool, 1, p), ahead))
-        out_behind.append(start(own, piece(pool, 0, p), behind))
-        out_partner.append(start(own, piece(pool, 3, p), partner))
-
+            return carry
+
+        lax.fori_loop(0, SIDE, centre, 0)
     for i, ref in enumerate((cb_ref, gain_ref, nbias_ref, bout_ref)):
         line = jnp.concatenate([ref[...], jnp.zeros((1, 6), F32)], axis=1)
         for g in range(GROUPS):
             lanes[g, i : i + 1, :] = line[:, g * LANES : (g + 1) * LANES]
-    bias_in[...] = jnp.concatenate([bin_ref[...], jnp.zeros((1, 24), F32)], axis=1)
     row = lax.broadcasted_iota(jnp.int32, (CAP, LANES), 0)
     lane = lax.broadcasted_iota(jnp.int32, (CAP, LANES), 1)
     sample = jnp.zeros((CAP, LANES), jnp.int32)
     for t in range(CAP):
         sample = jnp.where(row == t, sample_ref[t], sample)
     member[...] = (sample == lane).astype(F32)
-    for g in range(GROUPS):
-
-        def centre(r, carry):
-            padded[g, pl.ds(((r + RIM) * PAD + RIM) * CAP, SIDE * CAP), :] = tiles[
-                g, pl.ds(r * SIDE * CAP, SIDE * CAP), :
-            ]
-            return carry
-
-        lax.fori_loop(0, SIDE, centre, 0)
+    for ref in (dw, vec, hvec):
+        ref[...] = jnp.zeros_like(ref)
+    passed = []
+
+    def pass_on(p):
+        out_ahead[p].wait_recv()
+        passed.append(start(piece(pool, 1, p), piece(pool, 2, p), partner))
+
+    own_conv(0, padded, conv, w, lanes)
+    pass_on(0)
+    own_conv(1, padded, conv, w, lanes)
+    pass_on(1)
     for p, (g, half) in enumerate(PIECES):
         loads[4 + p].wait()
         to_rows(gbuf, grad, g, half)
@@ -712,21 +811,21 @@
             mask[pl.ds(half * 1024 + t, LANES, stride=CAP), :] = jnp.broadcast_to(
                 ocean[t : t + 1, half * LANES : (half + 1) * LANES], (LANES, LANES)
             ).T
-    own_conv(0, padded, conv, w, lanes)
-    passed = []
-
-    def pass_on(p):
-        out_ahead[p].wait_recv()
-        passed.append(start(piece(pool, 1, p), piece(pool, 2, p), partner))
-
-    pass_on(0)
-    own_conv(1, padded, conv, w, lanes)
-    pass_on(1)
-    win_hi[...], win_lo[...] = split(edge_zero(win_ref[...], 1000, 250))
-    wout_hi[...], wout_lo[...] = split(edge_zero(wout_ref[...], 1000, 250))
+    for i, (high, low) in enumerate(((win_hi, win_lo), (wout_hi, wout_lo))):
+        loads[8 + i].wait()
+        value = jnp.concatenate([weight_buf[i], jnp.zeros((1000, 6), F32)], axis=1)
+        value = jnp.concatenate([value, jnp.zeros((24, 256), F32)], axis=0)
+        high[...], low[...] = split(value)
+    win, wout = (win_hi, win_lo), (wout_hi, wout_lo)
+    scaled, update = (scaled_hi, scaled_lo), (update_hi, update_lo)
+    hidden_gradient(grad, mask, wout, update_hi, update_lo, back, vec)
+    ends = jnp.concatenate(
+        [flat([lanes[g, 1:3, :] for g in range(GROUPS)]), jnp.zeros((14, 256), F32)], axis=0
+    )
+    lines = dot3(split(ends), (win_hi[...], win_lo[...]), 1, 1)
+    bias_in = jnp.concatenate([bin_ref[...], jnp.zeros((1, 24), F32)], axis=1)
+    lines = jnp.concatenate([lines[0:1], lines[1:2] + bias_in], axis=0)
     onehots(near_ref, me, spread)
-    for ref in (dw, vec, hvec):
-        ref[...] = jnp.zeros_like(ref)
     sums = []
     for g in range(GROUPS):
         if g == 1:
@@ -738,7 +837,7 @@
         halo_conv(g, padded, conv, w)
         sums.append(masked_sum(g, conv, mask))
 
-    def reduce_vector(i, vector, merge, between):
+    def reduce_vector(i, vector, merge, between, later):
         partial[i] = vector
         copies = exchange_start(
             partial.at[i], send, recv, inner.at[i], used[0], me % INNER, zc_peers
@@ -752,12 +851,105 @@
             partial.at[2 + i], send, recv, outer.at[i], used[0], xy, xy_peers
         )
         used[0] += OUTER - 1
+        later()
         for copy in copies:
             copy.wait()
         return merge(outer[i])
 
-    stats = local_stats(sums[0][0] + sums[1][0], sums[0][1], conv, mask, member[...])
-    stat_ref[...] = reduce_vector(0, stats, merge_stats, sent)
+    tile_mean = tile_average(sums[0][0] + sums[1][0], sums[0][1])
+    stats = local_stats(tile_mean, sums[0][1], conv, mask, member[...])
+    product = lambda low, high: centred_product(low, high, tile_mean, conv, lanes, win, arena)
+
+    def first_blocks():
+        product(0, BLOCKS // 2)
+        sent()
+
+    stat = reduce_vector(0, stats, merge_stats, first_blocks, lambda: product(BLOCKS // 2, BLOCKS))
+    stat_ref[...] = stat
+
+    mine = pl.multiple_of(core * HALF, HALF)
+    theirs = pl.multiple_of((1 - core) * HALF, HALF)
+    orders = [((y, y_peers, 32), (x, x_peers, INNER)), ((x, x_peers, INNER), (y, y_peers, 32))]
+
+    def at(q, i, j, rows):
+        (first, _, _), (second, _, _) = orders[q]
+        i = first if i is None else i
+        first_row = core * HALF + q * 128 + i * 32 + (0 if j is None else j * 8)
+        return pl.ds(pl.multiple_of(first_row, 8), rows)
+
+    def weight_sum(h):
+        k = h // HIDDEN_PART
+        part = pl.ds(h, HIDDEN_PART)
+        halves = start(dw.at[pl.ds(theirs, HALF), part], other.at[k], partner)
+        yield
+        halves.wait_recv()
+        dw[pl.ds(mine, HALF), part] = dw[pl.ds(mine, HALF), part] + other[k]
+        yield
+        copies = []
+        for q, ((i, peers, stride), _) in enumerate(orders):
+            for peer in peers:
+                rows = at(q, (peer // stride) % 4, None, 32)
+                copies.append(start(dw.at[rows, part], slots1.at[k, q, i], peer))
+            slots1[k, q, i] = dw[at(q, None, None, 32), part]
+        yield
+        arrived(copies)
+        copies = []
+        for q, (_, (j, peers, stride)) in enumerate(orders):
+            sum1[k, q] = jnp.sum(slots1[k, q], axis=0)
+            for peer in peers:
+                rows = pl.ds(pl.multiple_of(((peer // stride) % 4) * 8, 8), 8)
+                copies.append(start(sum1.at[k, q, rows, :], slots2.at[k, q, j], peer))
+            slots2[k, q, j] = sum1[k, q, pl.ds(pl.multiple_of(j * 8, 8), 8), :]
+        yield
+        arrived(copies)
+        for q in range(2):
+            sum2[k, q] = jnp.sum(slots2[k, q], axis=0)
+        copies = [start(sum2.at[k], zslots.at[k, z], peer) for peer in z_peers]
+        zslots[k, z] = sum2[k]
+        yield
+        arrived(copies)
+        copies = []
+        for q, (_, (j, peers, _)) in enumerate(orders):
+            rows = at(q, None, j, 8)
+            big[rows, part] = zslots[k, 0, q] + zslots[k, 1, q] + zslots[k, 2, q] + zslots[k, 3, q]
+            copies += [start(big.at[rows, part], big.at[rows, part], peer) for peer in peers]
+        yield
+        arrived(copies)
+        copies = []
+        for q, ((_, peers, _), _) in enumerate(orders):
+            rows = at(q, None, None, 32)
+            copies += [start(big.at[rows, part], big.at[rows, part], peer) for peer in peers]
+        yield
+        arrived(copies)
+        own = big.at[pl.ds(mine, HALF), part]
+        crossed = start(own, own, partner)
+        yield
+        crossed.wait_recv()
+        yield
+
+    scaled_operand(stat, member[...], conv, lanes, scaled_hi, scaled_lo)
+
+    def projections(h, low, high):
+        dense_part(
+            h, low, high, stat, member[...], tile_mean, lines, (win_hi, win_lo, wout_hi, wout_lo),
+            scaled, update, arena, back, tiles, gbuf, dw, hvec,
+        )
+
+    projections(0, 0, BLOCKS)
+    early = weight_sum(0)
+    next(early)
+    projections(HIDDEN_PART, 0, BLOCKS // 2)
+    next(early)
+    next(early)
+    projections(HIDDEN_PART, BLOCKS // 2, BLOCKS)
+    next(early)
+    late = weight_sum(HIDDEN_PART)
+    next(late)
+    first, second = scaled_sums(stat, member[...], conv, gbuf, lanes, vec)
+    rows = [
+        jnp.sum(member[...] * jnp.sum(value, axis=1, keepdims=True), axis=0, keepdims=True)
+        for value in (first, second)
+    ]
 
     def clear_pool():
         for g in range(GROUPS):
@@ -768,71 +960,60 @@
 
             lax.fori_loop(0, 2 * BACK_ROLES, zero, 0)
 
-    first, second = dense(
-        stat_ref[...], member[...], conv, tiles, grad, mask, lanes, bias_in,
-        (win_hi, win_lo, wout_hi, wout_lo), tiles, gbuf, dw, vec, hvec,
-    )
-    theirs = pl.multiple_of((1 - core) * HALF, HALF)
-    mine = pl.multiple_of(core * HALF, HALF)
-    halves = start(dw.at[pl.ds(theirs, HALF), :], other, partner)
-    rows = [
-        jnp.sum(member[...] * jnp.sum(x, axis=1, keepdims=True), axis=0, keepdims=True)
-        for x in (first, second)
-    ]
-    scattered = []
-
-    def scatter_weights():
-        halves.wait_recv()
-        dw[pl.ds(mine, HALF), :] = dw[pl.ds(mine, HALF), :] + other[...]
-        for peer in xy_peers:
-            at = pl.multiple_of(core * HALF + (peer // INNER) * SLAB, SLAB)
-            scattered.append(start(dw.at[pl.ds(at, SLAB), :], slots.at[xy], peer))
-        slots[xy] = dw[pl.ds(pl.multiple_of(core * HALF + xy * SLAB, SLAB), SLAB), :]
+    def before_outer():
+        next(late)
+        next(early)
+
+    def after_outer():
+        next(late)
         clear_pool()
-
-    sums = reduce_vector(1, stack_rows(*rows), merge_sums, scatter_weights)
-    conv_gradient(stat_ref[...], sums, member[...], conv, gbuf, mask, lanes, db)
+        next(early)
+
+    sums = reduce_vector(1, stack_rows(*rows), merge_sums, before_outer, after_outer)
+    conv_gradient(stat, sums, member[...], conv, gbuf, mask, lanes, db)
+    next(late)
+    next(early)
 
     payload, direct, near, merged = [], [], [], []
 
-    def part_of(ref, p):
+    def pay(p):
         g, part = PIECES[p]
-        return ref.at[g, pl.ds(part * HALF_RIM, HALF_RIM), :]
+        return arena.at[g, pl.ds(part * HALF_RIM, HALF_RIM), :]
+
+    def got(i, p):
+        g, part = PIECES[p]
+        return arena.at[2 + 2 * i + g, pl.ds(part * HALF_RIM, HALF_RIM), :]
 
     def on_chip(p):
-        payload.append(start(piece(pool, 2, p), part_of(pay, p), partner))
-        near.append(start(piece(pool, 3, p), part_of(got.at[2], p), partner))
+        payload.append(start(piece(pool, 2, p), pay(p), partner))
+        near.append(start(piece(pool, 3, p), got(2, p), partner))
 
     def off_chip(p):
-        direct.append(start(piece(pool, 0, p), part_of(got.at[0], p), ahead))
+        direct.append(start(piece(pool, 0, p), got(0, p), ahead))
         payload[p].wait_recv()
         g, part = PIECES[p]
-        at = pl.ds(RIM_ROWS + part * HALF_RIM, HALF_RIM)
-        pool[g][at, :] = pool[g][at, :] + pay[g, pl.ds(part * HALF_RIM, HALF_RIM), :]
-        merged.append(start(piece(pool, 1, p), part_of(got.at[1], p), behind))
+        rows = pl.ds(RIM_ROWS + part * HALF_RIM, HALF_RIM)
+        pool[g][rows, :] = pool[g][rows, :] + arena[g, pl.ds(part * HALF_RIM, HALF_RIM), :]
+        merged.append(start(piece(pool, 1, p), got(1, p), behind))
 
     input_gradient(0, gbuf, w, gpad)
+    next(late)
+    next(early)
     own_gradient(0, gpad, grad, mask)
     scatter(0, gpad, spread, pool)
     on_chip(0)
     on_chip(1)
-    arrived(scattered)
-    slab[...] = jnp.sum(slots[...], axis=0)
-    z_gathered = [start(slab, zslots.at[z], peer) for peer in z_peers]
-    zslots[z] = slab[...]
+    next(late)
     off_chip(0)
     off_chip(1)
     input_gradient(1, gbuf, w, gpad)
+    next(late)
+    next(early)
     own_gradient(1, gpad, grad, mask)
     scatter(1, gpad, spread, pool)
     on_chip(2)
     on_chip(3)
     off_chip(2)
-    arrived(z_gathered)
-    big_rows = pl.ds(pl.multiple_of(core * HALF + xy * SLAB, SLAB), SLAB)
-    big[big_rows, :] = jnp.sum(zslots[...], axis=0)
-    own = big.at[big_rows, :]
-    xy_gathered = [start(own, own, peer) for peer in xy_peers]
 
     for g in range(GROUPS):
         weight_gradient(g, padded, gbuf, small)
@@ -847,6 +1028,7 @@
     sslots[xy] = small[xy // 8, pl.ds(pl.multiple_of((xy % 8) * CAP, CAP), CAP), :]
     stores = store_native(xbuf, native_out, store_sem)
     for p in range(2):
+        finish_output(p, tiles, mask, lanes)
         from_rows(tiles, xbuf, *PIECES[p])
         stores[p].start()
     arrived(small_scattered)
@@ -854,16 +1036,15 @@
     zc_gathered = [start(tile, zcslots.at[me % INNER], peer) for peer in zc_peers]
     zcslots[me % INNER] = tile[...]
     off_chip(3)
+    next(late)
     for p in range(2, 4):
+        finish_output(p, tiles, mask, lanes)
         from_rows(tiles, xbuf, *PIECES[p])
         stores[p].start()
-    arrived(xy_gathered)
-    own = big.at[pl.ds(mine, HALF), :]
-    crossed = start(own, own, partner)
     arrived(zc_gathered)
     small_ref[xy] = jnp.sum(zcslots[...], axis=0)
     small_gathered = [start(small_ref.at[xy], small_ref.at[xy], peer) for peer in xy_peers]
-    crossed.wait_recv()
+    next(late)
     stores.append(pltpu.make_async_copy(big, big_out, store_sem.at[4]))
     stores[4].start()
     for p, (g, half) in enumerate(PIECES):
@@ -873,7 +1054,7 @@
             span = pl.ds(rim * CAP, cells * CAP)
             mine_at = pl.ds(4 * RIM_ROWS + rim * CAP, cells * CAP)
             grad[g, rows, :] = (grad[g, rows, :] + pool[g][mine_at, :]) + (
-                got[2, g, span, :] + (got[0, g, span, :] + got[1, g, span, :])
+                arena[6 + g, span, :] + (arena[2 + g, span, :] + arena[4 + g, span, :])
             )
         rows = pl.ds(half * 1024, 1024)
         stores.append(
@@ -886,17 +1067,15 @@
         copy.wait()
 
 
-def block(near, count, sample, x, g, ocean, wt, cb, gain, nbias, bout, bin_, win, wout):
+def block(near, count, sample, x, g, win, wout, ocean, wt, cb, gain, nbias, bout, bin_):
     rows = (GROUPS, ROWS, LANES)
-    rim = (GROUPS, RIM_ROWS, LANES)
     vector = (CAP, LANES)
     weight = pltpu.VMEM((HIDDEN_PAD, 256), BF16)
-    copies = 16 + 2 * (INNER + OUTER - 2) + 1 + 15 + 16 + 3 + 15 + 15 + 7 + 1 + 15
-    weight_block = pl.BlockSpec((HIDDEN_PAD, 256), lambda i: (0, 0))
+    operand = pltpu.VMEM((ROWS, 256), BF16)
+    copies = 16 + 2 * (INNER + OUTER - 2) + 2 * 29 + 16 + 15 + 7 + 15
     return pl.pallas_call(
         block_kernel,
-        grid=(1,),
-        in_specs=[SMEM_SPEC] * 3 + [ANY_SPEC] * 2 + [VMEM_SPEC] * 7 + [weight_block] * 2,
+        in_specs=[SMEM_SPEC] * 3 + [ANY_SPEC] * 4 + [VMEM_SPEC] * 7,
         out_specs=(ANY_SPEC,) * 3 + (VMEM_SPEC,) * 2,
         out_shape=(
             shape(2000, 256), shape(*rows), shape(512, HIDDEN_PAD), shape(16, *vector),
@@ -907,20 +1086,24 @@
             buffer(ROWS, LANES), buffer(ROLES * RIM_ROWS, LANES), buffer(ROLES * RIM_ROWS, LANES),
             buffer(GROUPS, PAD * PAD * CAP, LANES), buffer(*rows),
             buffer(GROUPS, KSIZE * KSIZE, CAP, LANES), buffer(GROUPS, *vector),
-            buffer(*vector), buffer(1, HIDDEN_PAD), weight, weight, weight, weight,
+            buffer(*vector), buffer(2, 1000, 250), weight, weight, weight, weight,
+            operand, operand, operand, operand,
+            buffer(ROWS, HIDDEN_PAD), buffer(HIDDEN_CHUNKS, ROWS, LANES),
             buffer(512, HIDDEN_PAD), buffer(GROUPS, 3, *vector), buffer(1, HIDDEN_PAD),
             buffer(GROUPS, *vector), buffer(PAD * PAD * CAP, LANES),
-            pltpu.VMEM((8, BACK_ROLES * LANES, LANES), BF16), buffer(*rim), buffer(3, *rim),
-            buffer(HALF, HIDDEN_PAD), buffer(OUTER, SLAB, HIDDEN_PAD),
-            buffer(4, SLAB, HIDDEN_PAD), buffer(SLAB, HIDDEN_PAD), buffer(512, HIDDEN_PAD),
+            pltpu.VMEM((8, BACK_ROLES * LANES, LANES), BF16),
+            buffer(2, HALF, HIDDEN_PART), buffer(2, 2, 4, 32, HIDDEN_PART),
+            buffer(2, 2, 32, HIDDEN_PART), buffer(2, 2, 4, 8, HIDDEN_PART),
+            buffer(2, 2, 8, HIDDEN_PART), buffer(2, 4, 2, 8, HIDDEN_PART),
+            buffer(512, HIDDEN_PAD),
             buffer(GROUPS, 64, LANES), buffer(*vector), buffer(OUTER, *vector),
             buffer(INNER, *vector), buffer(2, INNER, *vector), buffer(2, OUTER, *vector),
-            buffer(4, *vector), semaphores(8), semaphores(9), semaphores(copies),
+            buffer(4, *vector), semaphores(10), semaphores(9), semaphores(copies),
             semaphores(copies),
         ],
         compiler_params=params(collective_id=1, has_side_effects=True),
         name="block",
-    )(near, count, sample, x, g, ocean, wt, cb, gain, nbias, bout, bin_, win, wout)
+    )(near, count, sample, x, g, win, wout, ocean, wt, cb, gain, nbias, bout, bin_)
 
 
 def final_kernel(
@@ -1002,9 +1185,9 @@
     weight_out, bias_out, grad_out, tile_counts, ocean_mask, neighbours, sample_ids,
 ):
     out, total, big, small, stat = block(
-        neighbours, tile_counts, sample_ids, native(tiles_in), native(grad_out), ocean_mask,
-        conv_weight.T, conv_bias[None], norm_gain[None], norm_bias[None], bias_out[None],
-        bias_in[None], weight_in.T, weight_out,
+        neighbours, tile_counts, sample_ids, native(tiles_in), native(grad_out), weight_in.T,
+        weight_out, ocean_mask, conv_weight.T, conv_bias[None], norm_gain[None], norm_bias[None],
+        bias_out[None], bias_in[None],
     )
     output, grad_tiles, dwin, dwout, dconv, lines, hline = final(total, out, big, small, stat)
     return (

time: 176 us -> 149 us (0.85)
  Pallas kernels: 173 us -> 146 us
    pallas_call x1, Pallas kernels: 166 us -> 139 us  [block(): pl.pallas_call(block_kernel, in_specs=[SMEM_SPEC] * 3 + [ANY_SPEC] * 4 +...]
where the time goes in v4:
time: 149 us
  Pallas kernels  146 us (98%)
    pallas_call x1, Pallas kernels, block(): pl.pallas_call(block_kernel, in_specs=[SMEM_SPEC] * 3 + [ANY_SPEC] * 4 +...  139 us
    pallas_call x1, Pallas kernels, final(): pl.pallas_call(final_kernel, in_specs=[ANY_SPEC] * 3 + [VMEM_SPEC] * 2, o...  7.14 us

profile of v4, /device:TPU:1, one launch (start us, length us, event | category | flops | bytes accessed | tf_op | source)
XLA Modules:
  0.0 148.6 jit_solution(18151849694835587511)
XLA Ops:
  1.3 138.8 %block.1 = (f32[2000,256]{1,0:T(8,128)}, f32[2,2048,128]{2,1,0:T(8,128)}, f32[512,1024]{1,0:T(8,128)}, f32[16,8,128]{2,1,0:T(8,128)}, f32[8,128]{1,0:T(8,128)}) custom-call(s32[8,8]{1,0:T(8,128)} %near_ref.1, s32[1]{0:T(128)S(6)} %copy.24.count_ref, s32[8]{0:T(128)} %sample_ref.1, f32[2000,256]{1,0:T(8,128)} %bitcast.27, f32[2000,256]{1,0:T(8,128)} %bitcast.28, ...), custom_call_target="tpu_custom_call" | custom-call | tf_op jit(solution)/shard_map/block/pallas_call | solution.py:1076
  140.1 7.1 %final.1 = (f32[2000,256]{1,0:T(8,128)}, f32[2000,256]{1,0:T(8,128)}, f32[1000,250]{1,0:T(8,128)}, f32[1000,250]{1,0:T(8,128)}, f32[49,250]{1,0:T(8,128)}, /*index=5*/f32[8,250]{1,0:T(8,128)}, f32[1,1024]{1,0:T(1,128)}) custom-call(f32[2,2048,128]{2,1,0:T(8,128)} %get-tuple-element.22.total_ref, f32[2000,256]{1,0:T(8,128)} %get-tuple-element.23.native_ref, ...), custom_call_target="tpu_custom_call" | custom-call | tf_op jit(solution)/shard_map/final/pallas_call | solution.py:1158
  147.2 1.4 fusion

commit v5 on v4

--- a/solution.py
+++ b/solution.py
@@ -371,25 +371,17 @@
     return lax.dot_general(left, right, dimension_numbers=dims, preferred_element_type=F32)
 
 
-ERF_P = 0.3275911 * 0.7071067811865476
-ERF_A = [0.5 * c for c in (1.061405429, -1.453152027, 1.421413741, -0.284496736, 0.254829592)]
-
-
 def gelu_parts(x):
-    size = jnp.abs(x)
-    t = pl.reciprocal(1.0 + ERF_P * size)
-    e = jnp.exp(-0.5 * (x * x))
-    poly = ERF_A[0]
-    for c in ERF_A[1:]:
-        poly = poly * t + c
-    tail = poly * t * e
-    cdf = jnp.where(x < 0.0, tail, 1.0 - tail)
-    return x * cdf, cdf + x * (e * 0.3989422804014327)
+    cdf = 0.5 + 0.5 * lax.erf(x * 0.7071067811865476)
+    density = 0.3989422804014327 * jnp.exp2((-0.5 * 1.4426950408889634) * (x * x))
+    return x * cdf, cdf + x * density
 
 
 BLOCK_ROWS = 512
 BLOCKS = ROWS // BLOCK_ROWS
 HIDDEN_PART = 512
+WEIGHT_PART = 256
+PRODUCT_ROWS = 1024
 
 
 def tile_values(stat_row, member):
@@ -429,35 +421,33 @@
         g_update = [by_tile(grad[g, rows, :]) * m for g in range(GROUPS)]
         for g in range(GROUPS):
             vec[g, 0] += jnp.sum(g_update[g], axis=0)
-        update_hi[rows, :], update_lo[rows, :] = split(flat(g_update))
-        operand = (update_hi[rows, :], update_lo[rows, :])
+        operand = split(flat(g_update))
+        update_hi[rows, :], update_lo[rows, :] = operand
         for h in range(0, HIDDEN_PAD, HIDDEN_PART):
             part = slice(h, h + HIDDEN_PART)
-            back[rows, part] = dot3(operand, (wout[0][part, :], wout[1][part, :]), 1, 1)
+            value = dot3(operand, (wout[0][part, :], wout[1][part, :]), 1, 1)
+            for c in range(HIDDEN_PART // LANES):
+                back[h // LANES + c, rows, :] = value[:, c * LANES : (c + 1) * LANES]
         return carry
 
     lax.fori_loop(0, BLOCKS, block, 0)
 
 
-def centred_product(low, high, tile_mean, conv, lanes, win, ahead):
-    def block(i, carry):
-        rows = block_rows(i)
-        operand = split(
-            flat(
-                [
-                    (by_tile(conv[g, rows, :]) - tile_mean[None]) * lanes[g, 1:2, :][None]
-                    for g in range(GROUPS)
-                ]
-            )
+def centred_product(first, tile_mean, conv, lanes, win, ahead):
+    rows = pl.ds(first, PRODUCT_ROWS)
+    operand = split(
+        flat(
+            [
+                (by_tile(conv[g, rows, :]) - tile_mean[None]) * lanes[g, 1:2, :][None]
+                for g in range(GROUPS)
+            ]
         )
-        for h in range(0, HIDDEN_PAD, HIDDEN_PART):
-            part = slice(h, h + HIDDEN_PART)
-            value = dot3(operand, (win[0][part, :], win[1][part, :]), 1, 1)
-            for c in range(HIDDEN_PART // LANES):
-                ahead[h // LANES + c, rows, :] = value[:, c * LANES : (c + 1) * LANES]
-        return carry
-
-    lax.fori_loop(low, high, block, 0)
+    )
+    for h in range(0, HIDDEN_PAD, HIDDEN_PART):
+        part = slice(h, h + HIDDEN_PART)
+        value = dot3(operand, (win[0][part, :], win[1][part, :]), 1, 1)
+        for c in range(HIDDEN_PART // LANES):
+            ahead[h // LANES + c][rows, :] = value[:, c * LANES : (c + 1) * LANES]
 
 
 def scaled_operand(stat, member, conv, lanes, scaled_hi, scaled_lo):
@@ -479,73 +469,55 @@
     lax.fori_loop(0, BLOCKS, block, 0)
 
 
-def dense_part(
-    h, low, high, stat, member, tile_mean, lines, weights, scaled, update, ahead, back, tiles,
-    gscaled, dw, hvec,
-):
-    win_hi, win_lo, wout_hi, wout_lo = weights
+def weight_products(h, stat, member, tile_mean, lines, scaled, update, ahead, back, dw, hvec):
     mean, inv = norm_values(stat, member)
-    part = slice(h, h + HIDDEN_PART)
-    count = HIDDEN_PART // LANES
-    win = (win_hi[part, :], win_lo[part, :])
-    wout = (wout_hi[part, :], wout_lo[part, :])
-    offset = lines[1:2, part] + wide((tile_mean - mean) * inv, count) * lines[0:1, part]
-    inv = wide(inv, count)
+    part = slice(h, h + WEIGHT_PART)
+    chunks = range(h // LANES, (h + WEIGHT_PART) // LANES)
+    offset = lines[1:2, part] + wide((tile_mean - mean) * inv, len(chunks)) * lines[0:1, part]
+    pre = jnp.concatenate([ahead[c][...] for c in chunks], axis=1)
+    pre = pre.reshape(-1, CAP, WEIGHT_PART) * wide(inv, len(chunks))[None] + offset[None]
+    hidden, slope = gelu_parts(pre.reshape(-1, WEIGHT_PART))
+    g_pre = jnp.concatenate([back[c] for c in chunks], axis=1) * slope
+    for i, c in enumerate(chunks):
+        span = slice(i * LANES, (i + 1) * LANES)
+        ahead[c][...] = hidden[:, span]
+        back[c] = g_pre[:, span]
+    hvec[:, part] = jnp.sum(g_pre, axis=0, keepdims=True)
+    dw[0:256, part] = dot3((scaled[0][...], scaled[1][...]), split(g_pre), 0, 0)
+    dw[256:512, part] = dot3((update[0][...], update[1][...]), split(hidden), 0, 0)
+
+
+def scaled_gradient(low, high, sums, stat, member, win, back, conv, lanes, gscaled, vec):
+    mean, inv = norm_values(stat, member)
+    win = (win[0][...], win[1][...])
 
     def block(i, carry):
         rows = block_rows(i)
-        pre = jnp.concatenate([ahead[h // LANES + c, rows, :] for c in range(count)], axis=1)
-        pre = pre.reshape(-1, CAP, HIDDEN_PART) * inv[None] + offset[None]
-        hidden, slope = gelu_parts(pre.reshape(-1, HIDDEN_PART))
-        hidden = split(hidden)
-        g_pre = back[rows, part] * slope
-        hvec[:, part] += jnp.sum(g_pre, axis=0, keepdims=True)
-        g_pre = split(g_pre)
-        dw[0:256, part] += dot3((scaled[0][rows, :], scaled[1][rows, :]), g_pre, 0, 0)
-        dw[256:512, part] += dot3((update[0][rows, :], update[1][rows, :]), hidden, 0, 0)
-        value = dot3(hidden, wout, 1, 0)
-        g_scaled = dot3(g_pre, win, 1, 0)
+        g_pre = split(jnp.concatenate([back[c, rows, :] for c in range(HIDDEN_CHUNKS)], axis=1))
+        value = dot3(g_pre, win, 1, 0)
+        first, second = carry
         for g in range(GROUPS):
-            span = slice(g * LANES, (g + 1) * LANES)
-            tiles[g, rows, :] += value[:, span]
-            if h == 0:
-                gscaled[g, rows, :] = g_scaled[:, span]
-            else:
-                gscaled[g, rows, :] += g_scaled[:, span]
-        return carry
-
-    lax.fori_loop(low, high, block, 0)
-
-
-def scaled_sums(stat, member, conv, gscaled, lanes, vec):
-    mean, inv = norm_values(stat, member)
-    zero = jnp.zeros((CAP, LANES), F32)
-    first, second = zero, zero
+            gs = by_tile(value[:, g * LANES : (g + 1) * LANES])
+            normed = (by_tile(conv[g, rows, :]) - mean[None]) * inv[None]
+            gscaled[g, rows, :] = gs.reshape(-1, LANES)
+            gain_sum = jnp.sum(gs * normed, axis=0)
+            bias_sum = jnp.sum(gs, axis=0)
+            vec[g, 1] += gain_sum
+            vec[g, 2] += bias_sum
+            first = first + bias_sum * lanes[g, 1:2, :]
+            second = second + gain_sum * lanes[g, 1:2, :]
+        return first, second
+
+    return lax.fori_loop(low, high, block, sums)
+
+
+def output_block(i, ahead, wout, tiles, mask, lanes):
+    rows = pl.ds(i * BLOCK_ROWS, BLOCK_ROWS)
+    hidden = split(jnp.concatenate([chunk[rows, :] for chunk in ahead], axis=1))
+    value = dot3(hidden, (wout[0][...], wout[1][...]), 1, 0)
     for g in range(GROUPS):
-
-        def add(r, carry):
-            rows = pl.ds(r * SIDE * CAP, SIDE * CAP)
-            gs = by_tile(gscaled[g, rows, :])
-            normed = (by_tile(conv[g, rows, :]) - mean[None]) * inv[None]
-            return carry[0] + jnp.sum(gs, axis=0), carry[1] + jnp.sum(gs * normed, axis=0)
-
-        bias_sum, gain_sum = lax.fori_loop(0, SIDE, add, (zero, zero))
-        vec[g, 1] = gain_sum
-        vec[g, 2] = bias_sum
-        first = first + bias_sum * lanes[g, 1:2, :]
-        second = second + gain_sum * lanes[g, 1:2, :]
-    return first, second
-
-
-def finish_output(p, tiles, mask, lanes):
-    g, half = PIECES[p]
-
-    def finish(r, carry):
-        rows = pl.ds(r * SIDE * CAP, SIDE * CAP)
-        tiles[g, rows, :] = mask[rows, :] * (tiles[g, rows, :] + lanes[g, 3:4, :])
-        return carry
-
-    lax.fori_loop(half * 8, half * 8 + 8, finish, 0)
+        part = value[:, g * LANES : (g + 1) * LANES] + lanes[g, 3:4, :]
+        tiles[g, rows, :] = mask[rows, :] * (tiles[g, rows, :] + part)
 
 
 def conv_gradient(stat, sums, member, conv, gscaled, mask, lanes, db):
@@ -570,7 +542,7 @@
         db[g] = lax.fori_loop(0, SIDE, gradient, jnp.zeros((CAP, LANES), F32)) * lane_mask(g)
 
 
-def input_gradient(g, gconv, w, gpad):
+def input_gradient(g, ranges, gconv, w, gpad):
     def input_row(r, carry):
         low = jnp.maximum(r - (SIDE - 1), 0)
         high = jnp.minimum(r, KSIZE - 1)
@@ -589,7 +561,11 @@
             gpad[pl.ds((r * PAD + i) * CAP, CAP), :] = acc[i]
         return carry
 
-    lax.fori_loop(0, PAD, input_row, 0)
+    for low_row, high_row in ranges:
+        lax.fori_loop(low_row, high_row, input_row, 0)
+
+
+HALF_ROWS = [((RIM, RIM + 8), (RIM + SIDE, PAD)), ((0, RIM), (RIM + 8, RIM + SIDE))]
 
 
 def own_gradient(g, gpad, grad, mask):
@@ -605,26 +581,28 @@
 def scatter_chunks():
     spans = {-1: (0, SIDE - RIM), 0: (RIM, 0), 1: (RIM + SIDE, 0)}
     order = [(-1, -1), (-1, 0), (-1, 1), (0, -1), (0, 1), (1, -1), (1, 0), (1, 1)]
-    chunks = []
+    chunks = [[], []]
     for dr, dc in order:
         dst_r, src_r = spans[dr]
         dst_c, src_c = spans[dc]
         cols = RIM if dc else SIDE
+        groups = [[], []]
         if dr == 0:
-            groups = [range(0, 3), range(3, 8), range(8, 13), range(13, 16)]
+            groups = [[range(0, 3), range(3, 8)], [range(8, 13), range(13, 16)]]
         elif dc == 0:
-            groups = [[0], [1], [2]]
+            groups[dr < 0] = [[0], [1], [2]]
         else:
-            groups = [range(3)]
-        chunks.append(
-            [
+            groups[dr < 0] = [range(3)]
+        for half in range(2):
+            chunks[half].append(
                 [
-                    ((dst_r + i) * PAD + dst_c, rim_index(src_r + i, src_c), cols)
-                    for i in group
+                    [
+                        ((dst_r + i) * PAD + dst_c, rim_index(src_r + i, src_c), cols)
+                        for i in group
+                    ]
+                    for group in groups[half]
                 ]
-                for group in groups
-            ]
-        )
+            )
     return chunks
 
 
@@ -651,11 +629,13 @@
         spread[k] = jnp.where(code == wanted, 1.0, 0.0).astype(BF16)
 
 
-def scatter(g, gpad, spread, pool):
+def scatter(g, half, gpad, spread, pool):
     for k in range(8):
+        if not CHUNKS[half][k]:
+            continue
         hot = spread[k]
         hot = jnp.concatenate([hot, hot], axis=1)
-        for chunk in CHUNKS[k]:
+        for chunk in CHUNKS[half][k]:
             parts = [gpad[pl.ds(dst * CAP, cells * CAP), :] for dst, _, cells in chunk]
             used = sum(cells for _, _, cells in chunk)
             if used < CHUNK:
@@ -697,7 +677,7 @@
     native_out, total_out, big_out, small_ref, stat_ref,
     xbuf, gbuf, tiles, grad, mask, pool0, pool1, padded, conv, w, lanes, member,
     weight_buf, win_hi, win_lo, wout_hi, wout_lo, update_hi, update_lo, scaled_hi, scaled_lo,
-    back, arena, dw, vec, hvec, db, gpad, spread,
+    back, extra, dw, vec, hvec, db, gpad, spread,
     other, slots1, sum1, slots2, sum2, zslots, big, small, tile, sslots, zcslots,
     inner, outer, partial, load_sem, store_sem, send, recv,
 ):
@@ -735,11 +715,13 @@
     loads = load_native(x_ref, xbuf, load_sem) + load_native(g_ref, gbuf, load_sem, 4)
     loads.append(pltpu.make_async_copy(win_ref, weight_buf.at[0], load_sem.at[8]))
     loads.append(pltpu.make_async_copy(wout_ref, weight_buf.at[1], load_sem.at[9]))
-    for copy in loads:
+    for copy in loads[:4]:
         copy.start()
     for half in range(2):
         xbuf[half, pl.ds(2000, 48), :] = jnp.zeros((48, LANES), F32)
         gbuf[half, pl.ds(2000, 48), :] = jnp.zeros((48, LANES), F32)
+
+    out_ahead, out_behind, out_partner = [], [], []
     for p, (g, half) in enumerate(PIECES):
         loads[p].wait()
         to_rows(xbuf, tiles, g, half)
@@ -747,15 +729,15 @@
             pool[g][pl.ds(4 * RIM_ROWS + rim * CAP, cells * CAP), :] = tiles[
                 g, pl.ds(first * CAP, cells * CAP), :
             ]
-    ready()
-
-    out_ahead, out_behind, out_partner = [], [], []
-    for p in range(4):
+        if p == 0:
+            ready()
         own = piece(pool, 4, p)
         out_ahead.append(start(own, piece(pool, 1, p), ahead))
         out_behind.append(start(own, piece(pool, 0, p), behind))
         out_partner.append(start(own, piece(pool, 3, p), partner))
 
+    for copy in loads[4:]:
+        copy.start()
     taps = wt_ref[...]
     taps = jnp.concatenate([taps, jnp.zeros((KSIZE * KSIZE, 6), F32)], axis=1)
     for g in range(GROUPS):
@@ -789,8 +771,7 @@
     for t in range(CAP):
         sample = jnp.where(row == t, sample_ref[t], sample)
     member[...] = (sample == lane).astype(F32)
-    for ref in (dw, vec, hvec):
-        ref[...] = jnp.zeros_like(ref)
+    vec[...] = jnp.zeros_like(vec)
     passed = []
 
     def pass_on(p):
@@ -858,13 +839,11 @@
 
     tile_mean = tile_average(sums[0][0] + sums[1][0], sums[0][1])
     stats = local_stats(tile_mean, sums[0][1], conv, mask, member[...])
-    product = lambda low, high: centred_product(low, high, tile_mean, conv, lanes, win, arena)
-
-    def first_blocks():
-        product(0, BLOCKS // 2)
-        sent()
-
-    stat = reduce_vector(0, stats, merge_stats, first_blocks, lambda: product(BLOCKS // 2, BLOCKS))
+    sent()
+    products = [pool[c // 3].at[pl.ds(c % 3 * ROWS, ROWS), :] for c in range(6)]
+    products += [extra.at[c] for c in range(2)]
+    product = lambda first: centred_product(first, tile_mean, conv, lanes, win, products)
+    stat = reduce_vector(0, stats, merge_stats, lambda: product(0), lambda: product(PRODUCT_ROWS))
     stat_ref[...] = stat
 
     mine = pl.multiple_of(core * HALF, HALF)
@@ -929,91 +908,97 @@
 
     scaled_operand(stat, member[...], conv, lanes, scaled_hi, scaled_lo)
 
-    def projections(h, low, high):
-        dense_part(
-            h, low, high, stat, member[...], tile_mean, lines, (win_hi, win_lo, wout_hi, wout_lo),
-            scaled, update, arena, back, tiles, gbuf, dw, hvec,
+    def weights(h):
+        weight_products(
+            h, stat, member[...], tile_mean, lines, scaled, update, products, back, dw, hvec
         )
 
-    projections(0, 0, BLOCKS)
+    def gradient(low, high, sums):
+        return scaled_gradient(
+            low, high, sums, stat, member[...], win, back, conv, lanes, gbuf, vec
+        )
+
+    weights(0)
+    weights(WEIGHT_PART)
     early = weight_sum(0)
     next(early)
-    projections(HIDDEN_PART, 0, BLOCKS // 2)
+    weights(2 * WEIGHT_PART)
     next(early)
     next(early)
-    projections(HIDDEN_PART, BLOCKS // 2, BLOCKS)
-    next(early)
+    weights(3 * WEIGHT_PART)
     late = weight_sum(HIDDEN_PART)
     next(late)
-    first, second = scaled_sums(stat, member[...], conv, gbuf, lanes, vec)
+    zero = jnp.zeros((CAP, LANES), F32)
+    sums = gradient(0, BLOCKS - 1, (zero, zero))
+    next(late)
+    next(late)
+    next(early)
+    sums = gradient(BLOCKS - 1, BLOCKS, sums)
     rows = [
         jnp.sum(member[...] * jnp.sum(value, axis=1, keepdims=True), axis=0, keepdims=True)
-        for value in (first, second)
+        for value in sums
     ]
 
-    def clear_pool():
+    def before_outer():
+        output_block(0, products, wout, tiles, mask, lanes)
+        next(early)
+        output_block(1, products, wout, tiles, mask, lanes)
+        next(late)
+
+    def after_outer():
+        output_block(2, products, wout, tiles, mask, lanes)
+        next(early)
+        output_block(3, products, wout, tiles, mask, lanes)
+        next(late)
         for g in range(GROUPS):
 
-            def zero(i, carry):
+            def clear_rows(i, carry):
                 pool[g][pl.ds(i * HALF_RIM, HALF_RIM), :] = jnp.zeros((HALF_RIM, LANES), F32)
                 return carry
 
-            lax.fori_loop(0, 2 * BACK_ROLES, zero, 0)
-
-    def before_outer():
-        next(late)
-        next(early)
-
-    def after_outer():
-        next(late)
-        clear_pool()
+            lax.fori_loop(0, 2 * BACK_ROLES, clear_rows, 0)
         next(early)
 
     sums = reduce_vector(1, stack_rows(*rows), merge_sums, before_outer, after_outer)
     conv_gradient(stat, sums, member[...], conv, gbuf, mask, lanes, db)
-    next(late)
-    next(early)
 
     payload, direct, near, merged = [], [], [], []
 
     def pay(p):
         g, part = PIECES[p]
-        return arena.at[g, pl.ds(part * HALF_RIM, HALF_RIM), :]
+        return back.at[g, pl.ds(part * HALF_RIM, HALF_RIM), :]
 
     def got(i, p):
         g, part = PIECES[p]
-        return arena.at[2 + 2 * i + g, pl.ds(part * HALF_RIM, HALF_RIM), :]
-
-    def on_chip(p):
+        return back.at[2 + 2 * i + g, pl.ds(part * HALF_RIM, HALF_RIM), :]
+
+    def rims_of(p):
+        g, half = PIECES[p]
+        input_gradient(g, HALF_ROWS[half], gbuf, w, gpad)
+        scatter(g, half, gpad, spread, pool)
         payload.append(start(piece(pool, 2, p), pay(p), partner))
         near.append(start(piece(pool, 3, p), got(2, p), partner))
 
-    def off_chip(p):
-        direct.append(start(piece(pool, 0, p), got(0, p), ahead))
+    def merge(p):
         payload[p].wait_recv()
         g, part = PIECES[p]
         rows = pl.ds(RIM_ROWS + part * HALF_RIM, HALF_RIM)
-        pool[g][rows, :] = pool[g][rows, :] + arena[g, pl.ds(part * HALF_RIM, HALF_RIM), :]
+        pool[g][rows, :] = pool[g][rows, :] + back[g, pl.ds(part * HALF_RIM, HALF_RIM), :]
         merged.append(start(piece(pool, 1, p), got(1, p), behind))
 
-    input_gradient(0, gbuf, w, gpad)
-    next(late)
-    next(early)
-    own_gradient(0, gpad, grad, mask)
-    scatter(0, gpad, spread, pool)
-    on_chip(0)
-    on_chip(1)
+    def off_chip(p):
+        direct.append(start(piece(pool, 0, p), got(0, p), ahead))
+
+    rims_of(0)
     next(late)
     off_chip(0)
+    rims_of(1)
+    merge(0)
+    next(late)
     off_chip(1)
-    input_gradient(1, gbuf, w, gpad)
-    next(late)
+    own_gradient(0, gpad, grad, mask)
+    merge(1)
     next(early)
-    own_gradient(1, gpad, grad, mask)
-    scatter(1, gpad, spread, pool)
-    on_chip(2)
-    on_chip(3)
-    off_chip(2)
 
     for g in range(GROUPS):
         weight_gradient(g, padded, gbuf, small)
@@ -1026,27 +1011,29 @@
     small_tile = lambda q: small.at[q // 8, pl.ds(pl.multiple_of((q % 8) * CAP, CAP), CAP), :]
     small_scattered = [start(small_tile(peer // INNER), sslots.at[xy], peer) for peer in xy_peers]
     sslots[xy] = small[xy // 8, pl.ds(pl.multiple_of((xy % 8) * CAP, CAP), CAP), :]
-    stores = store_native(xbuf, native_out, store_sem)
-    for p in range(2):
-        finish_output(p, tiles, mask, lanes)
-        from_rows(tiles, xbuf, *PIECES[p])
-        stores[p].start()
+    rims_of(2)
+    off_chip(2)
+    next(late)
+    merge(2)
+    rims_of(3)
+    own_gradient(1, gpad, grad, mask)
     arrived(small_scattered)
     tile[...] = jnp.sum(sslots[...], axis=0)
     zc_gathered = [start(tile, zcslots.at[me % INNER], peer) for peer in zc_peers]
     zcslots[me % INNER] = tile[...]
     off_chip(3)
+    merge(3)
+    next(early)
     next(late)
-    for p in range(2, 4):
-        finish_output(p, tiles, mask, lanes)
+    stores = store_native(xbuf, native_out, store_sem)
+    for p in range(4):
         from_rows(tiles, xbuf, *PIECES[p])
         stores[p].start()
+    stores.append(pltpu.make_async_copy(big, big_out, store_sem.at[4]))
+    stores[4].start()
     arrived(zc_gathered)
     small_ref[xy] = jnp.sum(zcslots[...], axis=0)
     small_gathered = [start(small_ref.at[xy], small_ref.at[xy], peer) for peer in xy_peers]
-    next(late)
-    stores.append(pltpu.make_async_copy(big, big_out, store_sem.at[4]))
-    stores[4].start()
     for p, (g, half) in enumerate(PIECES):
         arrived([near[p], direct[p], merged[p]])
         for first, rim, cells in rim_spans(half):
@@ -1054,7 +1041,7 @@
             span = pl.ds(rim * CAP, cells * CAP)
             mine_at = pl.ds(4 * RIM_ROWS + rim * CAP, cells * CAP)
             grad[g, rows, :] = (grad[g, rows, :] + pool[g][mine_at, :]) + (
-                arena[6 + g, span, :] + (arena[2 + g, span, :] + arena[4 + g, span, :])
+                back[6 + g, span, :] + (back[2 + g, span, :] + back[4 + g, span, :])
             )
         rows = pl.ds(half * 1024, 1024)
         stores.append(
@@ -1088,7 +1075,7 @@
             buffer(GROUPS, KSIZE * KSIZE, CAP, LANES), buffer(GROUPS, *vector),
             buffer(*vector), buffer(2, 1000, 250), weight, weight, weight, weight,
             operand, operand, operand, operand,
-            buffer(ROWS, HIDDEN_PAD), buffer(HIDDEN_CHUNKS, ROWS, LANES),
+            buffer(HIDDEN_CHUNKS, ROWS, LANES), buffer(2, ROWS, LANES),
             buffer(512, HIDDEN_PAD), buffer(GROUPS, 3, *vector), buffer(1, HIDDEN_PAD),
             buffer(GROUPS, *vector), buffer(PAD * PAD * CAP, LANES),
             pltpu.VMEM((8, BACK_ROLES * LANES, LANES), BF16),
@@ -1108,8 +1095,8 @@
 
 def final_kernel(
     total_ref, native_ref, big_ref, small_ref, stat_ref,
-    out_ref, tiles_ref, dwin_ref, dwout_ref, dconv_ref, lines_ref, hline_ref,
-    total, buf, through, big, load_sem, store_sem,
+    out_ref, tiles_ref, dwin_ref, dwout_ref, dconv_ref, db_ref, dgain_ref, dnbias_ref, dbin_ref,
+    dbout_ref, total, buf, through, big, load_sem, store_sem,
 ):
     loads = [
         pltpu.make_async_copy(
@@ -1137,19 +1124,16 @@
     loads[4].wait()
     dwin_ref[...] = big[0:256, :].T[:1000, :250] * share
     dwout_ref[...] = big[256:512, :].T[:1000, :250] * share
-    flat = [
+    parts = [
         jnp.concatenate([small_ref[g * 8 + i] for i in range(8)], axis=0) * share
         for g in range(GROUPS)
     ]
-    flat = jnp.concatenate(flat, axis=1)
-    dconv_ref[...] = flat[0:49, :250]
-    lines_ref[...] = flat[48:56, :250]
-    for g in range(GROUPS):
-        for i in range(4):
-            j = 53 + i
-            hline_ref[0:1, pl.ds((g * 4 + i) * LANES, LANES)] = (
-                flat[j : j + 1, g * LANES : (g + 1) * LANES]
-            )
+    whole = jnp.concatenate(parts, axis=1)
+    dconv_ref[...] = whole[0:49, :250]
+    for i, ref in enumerate((db_ref, dbout_ref, dgain_ref, dnbias_ref)):
+        ref[...] = whole[49 + i : 50 + i, :250]
+    line = jnp.concatenate([part[53 + i : 54 + i] for part in parts for i in range(4)], axis=1)
+    dbin_ref[...] = line[:, :1000]
     for copy in stores:
         copy.wait()
 
@@ -1158,10 +1142,11 @@
     return pl.pallas_call(
         final_kernel,
         in_specs=[ANY_SPEC] * 3 + [VMEM_SPEC] * 2,
-        out_specs=(ANY_SPEC,) * 2 + (VMEM_SPEC,) * 5,
+        out_specs=(ANY_SPEC,) * 2 + (VMEM_SPEC,) * 8,
         out_shape=(
             shape(2000, 256), shape(2000, 256), shape(1000, 250), shape(1000, 250),
-            shape(49, 250), shape(8, 250), shape(1, HIDDEN_PAD),
+            shape(49, 250), shape(1, 250), shape(1, 250), shape(1, 250), shape(1, 1000),
+            shape(1, 250),
         ),
         scratch_shapes=[
             buffer(GROUPS, ROWS, LANES), buffer(GROUPS, ROWS, LANES), buffer(2000, 256),
@@ -1189,18 +1174,12 @@
         weight_out, ocean_mask, conv_weight.T, conv_bias[None], norm_gain[None], norm_bias[None],
         bias_out[None], bias_in[None],
     )
-    output, grad_tiles, dwin, dwout, dconv, lines, hline = final(total, out, big, small, stat)
+    output, grad_tiles, dwin, dwout, dconv, db, dgain, dnbias, dbin, dbout = final(
+        total, out, big, small, stat
+    )
     return (
-        from_native(output),
-        from_native(grad_tiles),
-        dconv.T,
-        lines[1],
-        lines[3],
-        lines[4],
-        dwin.T,
-        hline[0, :1000],
-        dwout,
-        lines[2],
+        from_native(output), from_native(grad_tiles), dconv.T, db[0], dgain[0], dnbias[0],
+        dwin.T, dbin[0], dwout, dbout[0],
     )
 
 

time: 149 us -> 139 us (0.933)
  Pallas kernels: 146 us -> 137 us
    pallas_call x1, Pallas kernels: 139 us -> 130 us  [block(): pl.pallas_call(block_kernel, in_specs=[SMEM_SPEC] * 3 + [ANY_SPEC] * 4 +...]
where the time goes in v5:
time: 139 us
  Pallas kernels  137 us (99%)
  between operations  1.5 us (1%)
    pallas_call x1, Pallas kernels, block(): pl.pallas_call(block_kernel, in_specs=[SMEM_SPEC] * 3 + [ANY_SPEC] * 4 +...  130 us
    pallas_call x1, Pallas kernels, final(): pl.pallas_call(final_kernel, in_specs=[ANY_SPEC] * 3 + [VMEM_SPEC] * 2, o...  7.15 us

profile of v5, /device:TPU:1, one launch (start us, length us, event | category | flops | bytes accessed | tf_op | source)
XLA Modules:
  0.0 138.9 jit_solution(8048303264875809621)
XLA Ops:
  1.3 130.3 %block.1 = (f32[2000,256]{1,0:T(8,128)}, f32[2,2048,128]{2,1,0:T(8,128)}, f32[512,1024]{1,0:T(8,128)}, f32[16,8,128]{2,1,0:T(8,128)}, f32[8,128]{1,0:T(8,128)}) custom-call(s32[8,8]{1,0:T(8,128)} %near_ref.1, s32[1]{0:T(128)S(6)} %copy.24.count_ref, s32[8]{0:T(128)} %sample_ref.1, f32[2000,256]{1,0:T(8,128)} %bitcast.26, f32[2000,256]{1,0:T(8,128)} %bitcast.27, ...), custom_call_target="tpu_custom_call" | custom-call | tf_op jit(solution)/shard_map/block/pallas_call | solution.py:1063
  131.6 7.2 %final.1 = (f32[2000,256]{1,0:T(8,128)}, f32[2000,256]{1,0:T(8,128)}, f32[1000,250]{1,0:T(8,128)}, f32[1000,250]{1,0:T(8,128)}, f32[49,250]{1,0:T(8,128)}, /*ind...) custom-call(f32[2,2048,128]{2,1,0:T(8,128)} %get-tuple-element.25.total_ref, ...), custom_call_target="tpu_custom_call" | custom-call | tf_op jit(solution)/shard_map/final/pallas_call | solution.py:1142
